TPU v7x, 256 devices: a whole 4x4x8 slice. The times are simulated.
256 devices in a mesh: lat: 16 (over y, x_hi, core), lon: 16 (over x_lo, z).
Axes of the slice: x: 4 (x_hi: 2, x_lo: 2; x = x_hi * 2 + x_lo), y: 4, z: 8, core: 2. Of those that a mesh axis runs over, the one named last changes fastest.
Arguments:
- cotangent: bfloat16 [256, 1440, 512], P('lat', 'lon'), may hold values from -6 to 6
- activations: bfloat16 [256, 1440, 512], P('lat', 'lon'), may hold values from -6 to 6
- weight: bfloat16 [4, 512, 512], replicated, may hold values from -0.125 to 0.125
- basis: bfloat16 [4, 3, 33, 256], replicated, may hold values from -1.1953125 to 1.1953125
- reach: int32 [256], replicated, may hold values from 1 to 16, as said below
Outputs:
- grad_input: bfloat16 [256, 1440, 512], P('lat', 'lon')
- grad_weight: bfloat16 [4, 512, 512], replicated
Inputs may be any that keep to these rules, and one draw needn't show every extreme that they name: reach of each latitude row, widest near the poles; rows 0 and 255 have reach 16.
All inputs are finite; a program needn't handle non-finite values.
Results may differ from a plain program's by a relative error of at most 0.0052.
Values may be sent and summed in bfloat16 or wider, within the bound.
No kernel may reach another device: no remote copies, remote signals or barrier semaphores. Data moves between devices by JAX's collectives and lax.ppermute only.
A program may use at most 128 MiB of HBM per device.

v0:
```python
import jax
import jax.numpy as jnp
from jax import lax
from jax.sharding import PartitionSpec as P


def with_halo(shard, sides, width, wrap):
    for axis, dim in sides:
        devices, length = (lax.axis_size(axis), shard.shape[dim])
        up = [(i, (i + 1) % devices) for i in range(devices if wrap else devices - 1)]
        down = [(j, i) for i, j in up]
        last = lax.slice_in_dim(shard, length - width, length, axis=dim)
        leading = lax.slice_in_dim(shard, 0, width, axis=dim)
        before = lax.ppermute(last, axis, up)
        after = lax.ppermute(leading, axis, down)
        shard = jnp.concatenate([before, shard, after], axis=dim)
    return shard


def passed_along(block, axis, distance):
    devices = range(lax.axis_size(axis))
    route = [((i - distance) % len(devices), i) for i in devices]
    return lax.ppermute(block, axis, route)


def make_tiles(row_taps, one_hot):
    return jnp.einsum(
        "ksn,sel->knel", row_taps, one_hot, preferred_element_type=jnp.float32
    ).astype(jnp.bfloat16)


def offset_term(block_taps, source, offset, spread, lon_cols):
    weights_col = lax.dynamic_index_in_dim(block_taps, spread + offset, 1, keepdims=False).astype(
        jnp.float32
    )
    shifted = lax.dynamic_slice_in_dim(source, spread - offset, lon_cols, 1).astype(jnp.float32)
    return weights_col.T[:, None, :, None] * shifted[:, :, None, :]


def on_device(cotangent, activations, weight, basis, reach):
    lat_rows, lon_cols, channels = cotangent.shape
    tap_count = basis.shape[2]
    spread = (tap_count - 1) // 2
    lat_reach = (basis.shape[1] - 1) // 2
    filters = basis.shape[0]
    lat_count = lax.axis_size("lat")
    lon_count = lax.axis_size("lon")
    band_index = lax.axis_index("lat")
    total_rows = lat_count * lat_rows
    extended = lon_cols + 2 * spread
    widened = with_halo(cotangent, (("lon", 1),), spread, True)
    gathered = with_halo(widened, (("lat", 0),), lat_reach, False)
    edge_wide = jnp.concatenate([widened[:lat_reach], widened[lat_rows - lat_reach :]], axis=0)
    mirror = passed_along(edge_wide, "lon", lon_count // 2)
    offsets = jnp.arange(tap_count, dtype=jnp.int32) - spread
    inside = (jnp.abs(offsets)[:, None] <= reach[None, :]).astype(basis.dtype)
    masked = basis * inside[None, None, :, :]
    padded = jnp.pad(masked, ((0, 0), (0, 0), (0, 0), (lat_reach, lat_reach)))
    row_start = band_index * lat_rows
    tap_index = lax.broadcasted_iota(jnp.int32, (tap_count, extended, lon_cols), 0)
    ext_index = lax.broadcasted_iota(jnp.int32, (tap_count, extended, lon_cols), 1)
    col_index = lax.broadcasted_iota(jnp.int32, (tap_count, extended, lon_cols), 2)
    one_hot = (ext_index == col_index + 2 * spread - tap_index).astype(jnp.bfloat16)
    row_taps_list = []
    sources_list = []
    for tap_row in range(2 * lat_reach + 1):
        shift_rows = tap_row - lat_reach
        row_taps_list.append(
            lax.dynamic_slice_in_dim(
                padded[:, tap_row], row_start - shift_rows + lat_reach, lat_rows, 2
            )
        )
        sources_list.append(gathered[lat_reach - shift_rows : lat_reach - shift_rows + lat_rows])
    accum = jnp.zeros((lat_rows, lon_cols, filters, channels), jnp.float32)
    reach_padded = jnp.pad(reach, (lat_reach, lat_reach))
    widest = jnp.max(lax.dynamic_slice_in_dim(reach_padded, row_start, lat_rows + 2 * lat_reach))

    def add_pair(offset, carried):
        later = jnp.where(offset > 0, 1.0, 0.0)
        for block_taps, source in zip(row_taps_list, sources_list):
            forward = offset_term(block_taps, source, offset, spread, lon_cols)
            backward = offset_term(block_taps, source, -offset, spread, lon_cols)
            carried = carried + forward + later * backward
        return carried

    accum = lax.fori_loop(0, widest + 1, add_pair, accum)
    pole_north = jnp.zeros((lat_reach, lon_cols, filters, channels), jnp.float32)
    pole_south = jnp.zeros((lat_reach, lon_cols, filters, channels), jnp.float32)
    for tap_row in range(2 * lat_reach + 1):
        shift_rows = tap_row - lat_reach
        north_row = -1 - 0 - shift_rows
        if 0 <= north_row < lat_reach:
            north_tile = make_tiles(masked[:, tap_row, :, north_row : north_row + 1], one_hot)[:, 0]
            pole_north = pole_north.at[0].add(
                jnp.einsum(
                    "ec,kel->lkc", mirror[north_row], north_tile, preferred_element_type=jnp.float32
                )
            )
        south_row = lat_reach - shift_rows
        if 0 <= south_row < lat_reach:
            global_row = total_rows - lat_reach + south_row
            south_tile = make_tiles(masked[:, tap_row, :, global_row : global_row + 1], one_hot)[
                :, 0
            ]
            pole_south = pole_south.at[lat_reach - 1].add(
                jnp.einsum(
                    "ec,kel->lkc",
                    mirror[lat_reach + south_row],
                    south_tile,
                    preferred_element_type=jnp.float32,
                )
            )
    north_on = (band_index == 0).astype(jnp.float32)
    south_on = (band_index == lat_count - 1).astype(jnp.float32)
    accum = accum.at[:lat_reach].add(north_on * pole_north)
    accum = accum.at[lat_rows - lat_reach :].add(south_on * pole_south)
    filter_input = accum.astype(jnp.bfloat16)
    cell_count = lat_rows * lon_cols
    filter_flat = filter_input.reshape(cell_count, filters * channels)
    input_flat = activations.reshape(cell_count, channels)
    norm_factor = float(total_rows * lon_count * lon_cols) ** (-0.5)
    local_sum = jnp.einsum("mr,md->rd", filter_flat, input_flat, preferred_element_type=jnp.float32)
    summed = lax.psum(local_sum, ("lat", "lon"))
    grad_weight = (summed * norm_factor).astype(jnp.bfloat16).reshape(filters, channels, channels)
    grad_input = jnp.einsum(
        "mkc,kcd->md",
        filter_flat.reshape(cell_count, filters, channels),
        weight,
        preferred_element_type=jnp.float32,
    )
    grad_input = grad_input.reshape(lat_rows, lon_cols, channels).astype(jnp.bfloat16)
    return (grad_input, grad_weight)


def solution(mesh):
    in_specs = (P("lat", "lon", None), P("lat", "lon", None), P(), P(), P())
    out_specs = (P("lat", "lon", None), P())
    return jax.shard_map(
        on_device, mesh=mesh, in_specs=in_specs, out_specs=out_specs, check_vma=False
    )
```

profile of v0, /device:TPU:1, one launch (start us, length us, event | category | flops | bytes accessed | tf_op | source)
XLA Modules:
  0.0 952.8 jit_solution(8399666800729936187)
XLA Ops:
  7.2 2.4 copy.43
  9.6 1.2 copy-done.3
  10.9 2.5 collective-permute-start
  13.4 5.0 collective-permute-start.1
  18.4 0.8 compare_convert_fusion
  19.1 0.1 broadcast_multiply_fusion
  19.3 0.3 pad_slice_fusion
  19.5 0.1 fusion.27
  19.6 0.1 copy.47
  19.8 1.2 fusion.15
  20.9 0.7 dynamic-slice_bitcast_fusion
  21.7 0.1 copy.51
  21.8 1.2 fusion.16
  22.9 1.4 collective-permute-done
  24.3 1.7 pad_maximum_fusion.6
  26.0 1.3 copy-done.1
  27.3 3.1 collective-permute-start.2
  30.5 4.3 collective-permute-start.3
  34.7 0.7 dynamic-slice_bitcast_fusion.2
  35.5 0.7 fusion.23
  36.8 3.3 copy.57
  40.2 2.4 reshape.240
  42.6 0.1 collective-permute-start.4
  42.8 4.0 pad_maximum_fusion
  46.7 6.8 broadcast_in_dim.2
  53.6 128.6 %while.17 = (s32[]{:T(128)}, f32[16,90,4,512]{3,2,1,0:T(4,128)}, s32[]{:T(128)}, bf16[4,33,16]{2,0,1:T(4,128)(2,1)}, bf16[16,122,512]{2,1,0:T(8,128)(2,1)}, /*in...) while((s32[]{:T(128)}, f32[16,90,4,512]{3,2,1,0:T(4,128)}, ...), condition=%wide.region_2.3_spmd, body=%wide.region_1.2_spmd.sunk | while | flops 48660884 | bytes 67837064 | solution.py:86
  54.0 8.6 dynamic-slice_convert_fusion.8
  62.7 0.8 convert_bitcast_fusion.8
  63.8 5.7 dynamic-slice_convert_fusion.9
  69.4 0.7 convert_bitcast_fusion.9
  70.3 15.8 %multiply_add_fusion.2 = f32[16,90,4,512]{3,2,1,0:T(4,128)} fusion(f32[16,90,4,512]{3,2,1,0:T(4,128)} %get-tuple-element.350, f32[16,90,512]{2,1,0:T(8,128)} %get-tuple-element.321, f32[16,4]{1,0:T(8,128)S(1)} %copy.84, f32[16,90,512]{2,1,0:T(8,128)} %get-tuple-element.323, f32[16,4]{1,0:T(8,128)S(1)} %copy.85, f32[16,90,512]{2,1,0:T(8,128)} %get-tuple-element.325, ...), kind=kLoop, calls=%fused_computation.clone.1 | loop fusion | flops 44236800 | bytes 41289220 | tf_op jit(solution)/shard_map/while/body/add | solution.py:83
  86.2 8.6 dynamic-slice_convert_fusion.8
  94.8 0.7 convert_bitcast_fusion.8
  95.9 5.7 dynamic-slice_convert_fusion.9
  101.5 0.7 convert_bitcast_fusion.9
  102.4 15.8 %multiply_add_fusion.2 = f32[16,90,4,512]{3,2,1,0:T(4,128)} fusion(f32[16,90,4,512]{3,2,1,0:T(4,128)} %get-tuple-element.350, f32[16,90,512]{2,1,0:T(8,128)} %get-tuple-element.321, f32[16,4]{1,0:T(8,128)S(1)} %copy.84, f32[16,90,512]{2,1,0:T(8,128)} %get-tuple-element.323, f32[16,4]{1,0:T(8,128)S(1)} %copy.85, f32[16,90,512]{2,1,0:T(8,128)} %get-tuple-element.325, ...), kind=kLoop, calls=%fused_computation.clone.1 | loop fusion | flops 44236800 | bytes 41289220 | tf_op jit(solution)/shard_map/while/body/add | solution.py:83
  118.2 8.6 dynamic-slice_convert_fusion.8
  126.9 0.7 convert_bitcast_fusion.8
  127.9 5.7 dynamic-slice_convert_fusion.9
  133.6 0.7 convert_bitcast_fusion.9
  134.4 15.8 %multiply_add_fusion.2 = f32[16,90,4,512]{3,2,1,0:T(4,128)} fusion(f32[16,90,4,512]{3,2,1,0:T(4,128)} %get-tuple-element.350, f32[16,90,512]{2,1,0:T(8,128)} %get-tuple-element.321, f32[16,4]{1,0:T(8,128)S(1)} %copy.84, f32[16,90,512]{2,1,0:T(8,128)} %get-tuple-element.323, f32[16,4]{1,0:T(8,128)S(1)} %copy.85, f32[16,90,512]{2,1,0:T(8,128)} %get-tuple-element.325, ...), kind=kLoop, calls=%fused_computation.clone.1 | loop fusion | flops 44236800 | bytes 41289220 | tf_op jit(solution)/shard_map/while/body/add | solution.py:83
  150.3 8.6 dynamic-slice_convert_fusion.8
  158.9 0.6 convert_bitcast_fusion.8
  159.9 5.7 dynamic-slice_convert_fusion.9
  165.5 0.6 convert_bitcast_fusion.9
  166.3 15.8 %multiply_add_fusion.2 = f32[16,90,4,512]{3,2,1,0:T(4,128)} fusion(f32[16,90,4,512]{3,2,1,0:T(4,128)} %get-tuple-element.350, f32[16,90,512]{2,1,0:T(8,128)} %get-tuple-element.321, f32[16,4]{1,0:T(8,128)S(1)} %copy.84, f32[16,90,512]{2,1,0:T(8,128)} %get-tuple-element.323, f32[16,4]{1,0:T(8,128)S(1)} %copy.85, f32[16,90,512]{2,1,0:T(8,128)} %get-tuple-element.325, ...), kind=kLoop, calls=%fused_computation.clone.1 | loop fusion | flops 44236800 | bytes 41289220 | tf_op jit(solution)/shard_map/while/body/add | solution.py:83
  182.2 15.5 %copy.50 = f32[16,90,4,512]{3,0,2,1:T(8,128)} copy(f32[16,90,4,512]{3,2,1,0:T(4,128)} %get-tuple-element.197) | data formatting | bytes 23592960 | tf_op jit(solution)/shard_map/while | solution.py:86
  197.7 0.2 convolution_multiply_fusion.1
  198.0 0.5 copy.76
  198.5 3.8 slice_add_fusion.1
  202.2 15.9 %scatter-add.6 = f32[16,90,4,512]{3,0,2,1:T(8,128)} dynamic-update-slice(f32[16,90,4,512]{3,0,2,1:T(8,128)} %copy.50, f32[1,90,4,512]{3,0,2,1:T(1,128)S(1)} %slice_add_fusion.1, s32[]{:T(128)} %constant.178.clone.1, s32[]{:T(128)} %constant.178.clone.1, s32[]{:T(128)} %constant.178.clone.1, s32[]{:T(128)} %constant.178.clone.1) | dynamic-update-slice | bytes 1474564 | tf_op jit(solution)/shard_map/scatter-add | solution.py:115
  218.2 0.2 convolution_multiply_fusion
  218.4 0.5 copy.75
  218.9 3.8 slice_add_fusion
  222.7 15.8 %scatter-add.9 = f32[16,90,4,512]{3,0,2,1:T(8,128)} dynamic-update-slice(f32[16,90,4,512]{3,0,2,1:T(8,128)} %scatter-add.6, f32[1,90,4,512]{3,0,2,1:T(1,128)S(1)} %slice_add_fusion, s32[]{:T(128)} %constant.192.clone.1, s32[]{:T(128)} %constant.178.clone.1, s32[]{:T(128)} %constant.178.clone.1, s32[]{:T(128)} %constant.178.clone.1) | dynamic-update-slice | bytes 1474564 | tf_op jit(solution)/shard_map/scatter-add | solution.py:116
  238.5 7.8 convert_element_type.128
  246.3 7.2 copy.77
  253.6 2.7 copy.60
  256.2 0.3 copy-done.2
  256.6 5.2 fusion.28
  261.8 6.2 bitcast_convert_fusion
  268.0 1.9 copy.58
  269.9 671.7 %all-reduce.4.cloned.1.call-done = f32[2048,512]{1,0:T(8,128)} async-done(((f32[2048,512]{1,0:T(8,128)}), f32[2048,512]{1,0:T(8,128)}) %all-reduce.4.cloned.1.call-update) | async-done | bytes 4194320 | tf_op jit(solution)/shard_map/psum | solution.py:123
  941.6 4.1 multiply_convert_fusion
  (50 shorter events, 2.2 us)
Async XLA Ops:
  7.2 254.6 %copy-start = (bf16[4,512,512]{2,1,0:T(8,128)(2,1)S(1)}, bf16[4,512,512]{2,1,0:T(8,128)(2,1)}, u32[]{:S(2)}) copy-start(bf16[4,512,512]{2,1,0:T(8,128)(2,1)} %param.17) | copy-start | bytes 6291460
  7.2 12.0 %copy-start.5 = (bf16[4,3,33,256]{3,0,2,1:T(4,128)(2,1)S(1)}, bf16[4,3,33,256]{3,0,2,1:T(4,128)(2,1)}, u32[]{:S(2)}) copy-start(bf16[4,3,33,256]{3,0,2,1:T(4,128)(2,1)} %param.18) | copy-start | bytes 608260
  7.2 934.4 %all-reduce.4.cloned.1.call-start = ((), (), s32[]{:S(2)}) async-start(), calls=%async_computation | async-start | bytes 8388608 | tf_op jit(solution)/shard_map/psum | solution.py:123
  9.6 1.2 copy-start.3
  10.9 24.6 %copy-start.8 = (s32[256]{0:T(256)S(1)}, s32[256]{0:T(256)}, u32[]{:S(2)}) copy-start(s32[256]{0:T(256)} %param.19) | copy-start | bytes 3076
  10.9 13.4 %collective-permute-start = (bf16[16,16,512]{2,1,0:T(8,128)(2,1)S(1)}, bf16[16,16,512]{2,1,0:T(8,128)(2,1)S(1)}, u32[]{:S(2)}, u32[]{:S(2)}) collective-permute-start(bf16[16,16,512]{2,1,0:T(8,128)(2,1)S(1)} %get-tuple-element.244), channel_id=1, source_target_pairs={{0,1},{1,2},{2,3},{3,4},{4,5},{5,6},{6,7},{7,8},{8,9},{9,10},{10,1... | collective-permute-start | bytes 786440 | tf_op jit(solution)/shard_map/ppermute | solution.py:14
  13.4 10.9 %collective-permute-start.1 = (bf16[16,16,512]{2,1,0:T(8,128)(2,1)S(1)}, bf16[16,16,512]{2,1,0:T(8,128)(2,1)S(1)}, u32[]{:S(2)}, u32[]{:S(2)}) collective-permute-start(bf16[16,16,512]{2,1,0:T(8,128)(2,1)S(1)} %get-tuple-element.245), channel_id=1, source_target_pairs={{1,0},{2,1},{3,2},{4,3},{5,4},{6,5},{7,6},{8,7},{9,8},{10,9},{11,1... | collective-permute-start | bytes 786440 | tf_op jit(solution)/shard_map/ppermute | solution.py:15
  26.0 1.3 copy-start.1
  27.3 15.4 %collective-permute-start.2 = (bf16[1,122,512]{2,1,0:T(8,128)(2,1)S(1)}, bf16[1,122,512]{2,1,0:T(8,128)(2,1)S(1)}, u32[]{:S(2)}, u32[]{:S(2)}) collective-permute-start(bf16[1,122,512]{2,1,0:T(8,128)(2,1)S(1)} %get-tuple-element.243), channel_id=1, source_target_pairs={{16,0},{32,16},{48,32},{64,48},{80,64},{96,80},{112,96},{128,112},... | collective-permute-start | bytes 374792 | tf_op jit(solution)/shard_map/ppermute | solution.py:15
  30.5 12.3 %collective-permute-start.3 = (bf16[1,122,512]{2,1,0:T(8,128)(2,1)S(1)}, bf16[1,122,512]{2,1,0:T(8,128)(2,1)}, u32[]{:S(2)}, u32[]{:S(2)}) collective-permute-start(bf16[1,122,512]{2,1,0:T(8,128)(2,1)S(1)} %get-tuple-element.242), channel_id=1, source_target_pairs={{0,16},{16,32},{32,48},{48,64},{64,80},{80,96},{96,112},{112,128},... | collective-permute-start | bytes 374792 | tf_op jit(solution)/shard_map/ppermute | solution.py:14
  42.6 155.1 %collective-permute-start.4 = (bf16[2,122,512]{2,1,0:T(8,128)(2,1)S(1)}, bf16[2,122,512]{2,1,0:T(8,128)(2,1)S(1)}, u32[]{:S(2)}, u32[]{:S(2)}) collective-permute-start(bf16[2,122,512]{2,1,0:T(8,128)(2,1)S(1)} %pad_maximum_fusion.7), channel_id=1, source_target_pairs={{8,0},{9,1},{10,2},{11,3},{12,4},{13,5},{14,6},{15,7},{0,8},{1,9},... | collective-permute-start | bytes 749576 | tf_op jit(solution)/shard_map/ppermute | solution.py:23
  182.2 15.5 %copy-start.6 = (bf16[4,122,90]{1,0,2:T(4,128)(2,1)S(1)}, bf16[4,122,90]{1,0,2:T(4,128)(2,1)}, u32[]{:S(2)}) copy-start(bf16[4,122,90]{1,0,2:T(4,128)(2,1)} %fusion.15) | copy-start | bytes 263524
  197.7 20.4 %copy-start.7 = (bf16[4,122,90]{1,0,2:T(4,128)(2,1)S(1)}, bf16[4,122,90]{1,0,2:T(4,128)(2,1)}, u32[]{:S(2)}) copy-start(bf16[4,122,90]{1,0,2:T(4,128)(2,1)} %fusion.16) | copy-start | bytes 263524
  253.5 3.0 copy-start.2
  253.6 3.0 copy-start.4
Sparse Core Ops, SparseCore 0:
  261.9 679.6 all-reduce.3
where the time goes:
time: 962 us; the launch traced here: 953 us
  waiting for transfers between devices  673 us (70%)
  other arithmetic  153 us (16%)
  local copies, waits for them, and re-layouts  82 us (9%)
  between operations  15.2 us (2%)
  starting transfers between devices  15 us (2%)
  matrix products  14.2 us (1%)
    psum x1, waiting for transfers between devices, on_device(): summed = lax.psum(local_sum, ('lat', 'lon'))  672 us
    add x4, other arithmetic, add_pair(): carried = carried + forward + later * backward  63.3 us
    convert_element_type x8, other arithmetic, offset_term(): lax.dynamic_slice_in_dim(source, spread - offset, lon_cols, 1)  57.2 us
  transfers between devices with their start and end apart: 6, of which 2 were waited for; matrix products, arithmetic and copies ran while one was open for 18% of the time, Pallas kernels for 0%

commit v1 on v0

v1 whole, which is shorter than its diff:
```python
import functools

import jax
import jax.numpy as jnp
from jax import lax
from jax.experimental import pallas as pl
from jax.experimental.pallas import tpu as pltpu
from jax.sharding import Mesh, PartitionSpec as P

ROWS, COLS, WIDE, PAD, REACH = 16, 90, 128, 96, 16
GAP = WIDE - COLS - 2 * REACH
RIGHT = WIDE - REACH
CHANNELS, FILTERS, TAPS = 512, 4, 3
AXES = ("y", "xh", "core", "xl", "z")
CHIPS = ("y", "xh", "xl", "z")
LAT, LON = 16, 16
VMEM = 60 * 1024 * 1024


def tiles_kernel(rev_ref, out_ref):
    lane = lax.broadcasted_iota(jnp.int32, (32, WIDE), 1)
    row = lax.broadcasted_iota(jnp.int32, (32, WIDE), 0) + 64
    for q in range(TAPS):
        for k in range(FILTERS):
            taps = rev_ref[0, pl.ds(q * FILTERS + k, 1), :]
            top = pltpu.roll(jnp.broadcast_to(taps, (64, WIDE)), 0, 1, stride=1, stride_axis=0)
            low = jnp.broadcast_to(taps, (32, WIDE))
            main = pltpu.roll(low, 64, 1, stride=1, stride_axis=0)
            right = pltpu.roll(low, 64 + GAP, 1, stride=1, stride_axis=0)
            low = jnp.where(lane < REACH + COLS, main, jnp.where(lane >= RIGHT, right, 0.0))
            low = jnp.where(row < COLS, low, 0.0)
            out_ref[0, k * PAD : k * PAD + 64, q * WIDE : (q + 1) * WIDE] = top.astype(jnp.bfloat16)
            out_ref[0, k * PAD + 64 : (k + 1) * PAD, q * WIDE : (q + 1) * WIDE] = low.astype(jnp.bfloat16)


def band_tiles(rev):
    return pl.pallas_call(
        tiles_kernel,
        grid=(ROWS,),
        in_specs=[pl.BlockSpec((1, 16, WIDE), lambda i: (i, 0, 0))],
        out_specs=pl.BlockSpec((1, FILTERS * PAD, TAPS * WIDE), lambda i: (i, 0, 0)),
        out_shape=jax.ShapeDtypeStruct((ROWS, FILTERS * PAD, TAPS * WIDE), jnp.bfloat16),
        name="band_tiles",
    )(rev)


def pad_rows(scratch, start, block):
    scratch[pl.ds(start + 80, 16), :] = jnp.zeros((16, CHANNELS), jnp.bfloat16)
    scratch[pl.ds(start, COLS), :] = block


def stencil_kernel(core, tiles, own, left, right, before, after, act, f_out, send, source, held, cells):
    step = pl.program_id(0)

    @pl.when(step == 0)
    def _():
        source[pl.ds(0, WIDE), :] = before[0]
        source[pl.ds((ROWS + 1) * WIDE, WIDE), :] = after[0]
        for r in range(ROWS):
            base = (r + 1) * WIDE
            source[pl.ds(base, REACH), :] = left[r]
            pad_rows(source, base + REACH, own[r])
            source[pl.ds(base + RIGHT, REACH), :] = right[r]
            pad_rows(cells, r * PAD, act[r])

    @pl.when(step < ROWS)
    def _():
        rows = source[pl.ds(pl.multiple_of(step * WIDE, WIDE), TAPS * WIDE), :]
        f = jnp.dot(tiles[0], rows, preferred_element_type=jnp.float32).astype(jnp.bfloat16)
        for k in range(FILTERS):
            part = f[k * PAD : (k + 1) * PAD]
            f_out[k] = part
            held[k, pl.ds(pl.multiple_of(step * PAD, 32), PAD), :] = part

    @pl.when(step >= ROWS)
    def _():
        k = 2 * (1 - core[0]) + step - ROWS
        d = lax.dot_general(held[k], cells[...], (((0,), (0,)), ((), ())), preferred_element_type=jnp.float32)
        send[0] = d.astype(jnp.bfloat16)


def stencil(core, tiles, own, left, right, before, after, act):
    whole = lambda a: pl.BlockSpec(a.shape, lambda i, c: (0,) * a.ndim)
    return pl.pallas_call(
        stencil_kernel,
        grid_spec=pltpu.PrefetchScalarGridSpec(
            num_scalar_prefetch=1,
            grid=(ROWS + 2,),
            in_specs=[
                pl.BlockSpec((1, FILTERS * PAD, TAPS * WIDE), lambda i, c: (jnp.minimum(i, ROWS - 1), 0, 0)),
                whole(own), whole(left), whole(right), whole(before), whole(after), whole(act),
            ],
            out_specs=[
                pl.BlockSpec((FILTERS, PAD, CHANNELS), lambda i, c: (0, jnp.minimum(i, ROWS - 1), 0)),
                pl.BlockSpec((1, CHANNELS, CHANNELS), lambda i, c: (jnp.maximum(i - ROWS, 0), 0, 0)),
            ],
            scratch_shapes=[
                pltpu.VMEM(((ROWS + 2) * WIDE, CHANNELS), jnp.bfloat16),
                pltpu.VMEM((FILTERS, ROWS * PAD, CHANNELS), jnp.bfloat16),
                pltpu.VMEM((ROWS * PAD, CHANNELS), jnp.bfloat16),
            ],
        ),
        out_shape=[
            jax.ShapeDtypeStruct((FILTERS, ROWS * PAD, CHANNELS), jnp.bfloat16),
            jax.ShapeDtypeStruct((2, CHANNELS, CHANNELS), jnp.bfloat16),
        ],
        compiler_params=pltpu.CompilerParams(vmem_limit_bytes=VMEM),
        name="stencil",
    )(core, tiles, own, left, right, before, after, act)


def input_kernel(f, weight, out):
    total = jnp.dot(f[0], weight[0], preferred_element_type=jnp.float32)
    for k in range(1, FILTERS):
        total += jnp.dot(f[k], weight[k], preferred_element_type=jnp.float32)
    for r in range(out.shape[0]):
        out[r] = total[r * PAD : r * PAD + COLS].astype(jnp.bfloat16)


def input_gradient(f, weight):
    group = 4
    flops = 2 * ROWS * PAD * FILTERS * CHANNELS * CHANNELS
    return pl.pallas_call(
        input_kernel,
        grid=(ROWS // group,),
        in_specs=[
            pl.BlockSpec((FILTERS, group * PAD, CHANNELS), lambda i: (0, i, 0)),
            pl.BlockSpec((FILTERS, CHANNELS, CHANNELS), lambda i: (0, 0, 0)),
        ],
        out_specs=pl.BlockSpec((group, COLS, CHANNELS), lambda i: (i, 0, 0)),
        out_shape=jax.ShapeDtypeStruct((ROWS, COLS, CHANNELS), jnp.bfloat16),
        compiler_params=pltpu.CompilerParams(vmem_limit_bytes=VMEM),
        cost_estimate=pl.CostEstimate(flops=flops, bytes_accessed=10_000_000, transcendentals=0),
        name="input_gradient",
    )(f, weight)


def own_half_kernel(core, f, act, got, out, cells):
    @pl.when(pl.program_id(0) == 0)
    def _():
        for r in range(ROWS):
            pad_rows(cells, r * PAD, act[r])

    d = lax.dot_general(f[0], cells[...], (((0,), (0,)), ((), ())), preferred_element_type=jnp.float32)
    out[0] = (d + got[0].astype(jnp.float32)).astype(jnp.bfloat16)


def own_half(core, f, act, got):
    block = (1, CHANNELS, CHANNELS)
    return pl.pallas_call(
        own_half_kernel,
        grid_spec=pltpu.PrefetchScalarGridSpec(
            num_scalar_prefetch=1,
            grid=(2,),
            in_specs=[
                pl.BlockSpec((1, ROWS * PAD, CHANNELS), lambda i, c: (2 * c[0] + i, 0, 0)),
                pl.BlockSpec(act.shape, lambda i, c: (0, 0, 0)),
                pl.BlockSpec(block, lambda i, c: (i, 0, 0)),
            ],
            out_specs=pl.BlockSpec(block, lambda i, c: (i, 0, 0)),
            scratch_shapes=[pltpu.VMEM((ROWS * PAD, CHANNELS), jnp.bfloat16)],
        ),
        out_shape=jax.ShapeDtypeStruct((2, CHANNELS, CHANNELS), jnp.bfloat16),
        compiler_params=pltpu.CompilerParams(vmem_limit_bytes=VMEM),
        name="own_half",
    )(core, f, act, got)


def device(lat, lon):
    return (lat % LAT) * LON + lon % LON


def route(pairs):
    return [(device(*a), device(*b)) for a, b in pairs]


GRID = [(a, b) for a in range(LAT) for b in range(LON)]
EAST = route(((a, b), (a, b + 1)) for a, b in GRID)
WEST = route(((a, b), (a, b - 1)) for a, b in GRID)
SOUTH = route(((a, b), (a + 1, b)) for a, b in GRID if a < LAT - 1)
NORTH = route(((a, b), (a - 1, b)) for a, b in GRID if a > 0)
ACROSS = route(((a, b), (a, b + LON // 2)) for a, b in GRID if a in (0, LAT - 1))
SIBLING = route(((a, b), (a ^ 1, b)) for a, b in GRID)


def reversed_taps(basis, reach, band):
    span = basis.shape[2]
    offsets = jnp.arange(span, dtype=jnp.int32) - REACH
    masked = jnp.where(jnp.abs(offsets)[:, None] <= reach[None, :], basis, 0)
    total = masked.shape[3]
    slabs = []
    for q in range(TAPS):
        t = TAPS - 1 - q
        edge = jnp.zeros_like(masked[:, t, :, :1])
        first = masked[:, 0, :, :1] if q == 0 else edge
        last = masked[:, 2, :, total - 1 :] if q == 2 else edge
        padded = jnp.concatenate([first, masked[:, t], last], axis=2)
        slabs.append(lax.dynamic_slice_in_dim(padded, band * ROWS + q, ROWS, 2))
    taps = jnp.stack(slabs)[:, :, ::-1, :].astype(jnp.float32)
    taps = jnp.transpose(taps, (3, 0, 1, 2)).reshape(ROWS, TAPS * FILTERS, span)
    return jnp.pad(taps, ((0, 0), (0, 16 - TAPS * FILTERS), (0, WIDE - span)))


def on_device(cotangent, activations, weight, basis, reach):
    band = lax.axis_index(("y", "xh", "core"))
    core = lax.axis_index("core").astype(jnp.int32)
    cores = core[None]
    left = lax.ppermute(cotangent[:, COLS - REACH :], AXES, EAST)
    right = lax.ppermute(cotangent[:, :REACH], AXES, WEST)
    tiles = band_tiles(reversed_taps(basis, reach, band))
    zeros = jnp.zeros((1, GAP, CHANNELS), jnp.bfloat16)
    first, last = (
        jnp.concatenate([left[r : r + 1], cotangent[r : r + 1], zeros, right[r : r + 1]], axis=1) for r in (0, ROWS - 1)
    )
    before = lax.ppermute(last, AXES, SOUTH)
    after = lax.ppermute(first, AXES, NORTH)
    mirror = lax.ppermute(jnp.where(band == 0, first, last), AXES, ACROSS)
    before = jnp.where(band == 0, mirror, before)
    after = jnp.where(band == LAT - 1, mirror, after)
    f, send = stencil(cores, tiles, cotangent, left, right, before, after, activations)
    got = lax.ppermute(send, AXES, SIBLING)
    grad_input = input_gradient(f, weight)
    half = own_half(cores, f, activations, got)
    chips = LAT * LON // 2
    parts = half.reshape(chips, 2 * CHANNELS // chips, CHANNELS)
    parts = lax.all_to_all(parts, CHIPS, 0, 0, tiled=True)
    norm_factor = float(ROWS * COLS * LAT * LON) ** (-0.5)
    part = (jnp.sum(parts.astype(jnp.float32), axis=0) * norm_factor).astype(jnp.bfloat16)
    parts = lax.all_to_all(jnp.broadcast_to(part, parts.shape), CHIPS, 0, 0, tiled=True)
    mine = parts.reshape(2, CHANNELS, CHANNELS)
    theirs = lax.ppermute(mine, AXES, SIBLING)
    grad_weight = jnp.where(core == 0, jnp.concatenate([mine, theirs]), jnp.concatenate([theirs, mine]))
    return grad_input, grad_weight


def solution(mesh):
    finer = Mesh(mesh.devices.reshape(4, 2, 2, 2, 8), AXES)
    cells = P(("y", "xh", "core"), ("xl", "z"), None)
    return jax.shard_map(
        on_device, mesh=finer, in_specs=(cells, cells, P(), P(), P()), out_specs=(cells, P()), check_vma=False
    )
```

time: 962 us -> 162 us (0.17)
  waiting for transfers between devices: 673 us -> 8.27 us
  other arithmetic: 153 us -> 3.66 us
  blocking collectives: 0 us -> 77.4 us
  local copies, waits for them, and re-layouts: 82 us -> 11.7 us
  Pallas kernels: 0 us -> 39.3 us
  between operations: 15.2 us -> 0.84 us
  matrix products: 14.2 us -> 0 us
    psum x1 -> x0, waiting for transfers between devices: 672 us -> none  [on_device(): summed = lax.psum(local_sum, ('lat', 'lon'))]
    all_to_all x0 -> x2, blocking collectives: none -> 77.4 us  [the longest x1 42.9 us: on_device(): parts = lax.all_to_all(parts, CHIPS, 0, 0, tiled=True)]
    add x7 -> x0, other arithmetic: 70.9 us -> none  [the longest x4 63.3 us: add_pair(): carried = carried + forward + later * backward]
    convert_element_type x11 -> x1, other arithmetic: 69.8 us -> 0.01 us  [on_device(): (jnp.sum(parts.astype(jnp.float32), axis=0) * norm_factor).astype(jnp.bfl...]
    pallas_call x0 -> x4, Pallas kernels: none -> 39.3 us  [the longest x1 17.2 us: stencil(): pl.pallas_call(stencil_kernel, grid_spec=pltpu.PrefetchScalarGridSpec(num...]
    scatter-add x2 -> x0, local copies, waits for them, and re-layouts: 31.7 us -> none  [the longest x1 15.9 us: on_device(): accum = accum.at[:lat_reach].add(north_on * pole_north)]
    while x1 -> x0, local copies, waits for them, and re-layouts: 15.5 us -> none  [on_device(): accum = lax.fori_loop(0, widest + 1, add_pair, accum)]
    dot_general x6 -> x0, matrix products: 14.2 us -> none  [the longest x1 6.18 us: on_device(): jnp.einsum('mkc,kcd->md', filter_flat.reshape(cell_count, filters, channe...]
  transfers between devices with their start and end apart: 6 -> 7, of which waited for: 2 -> 2; matrix products, arithmetic and copies ran while one was open for 18% -> 5% of each run, Pallas kernels for 0% -> 11%
where the time goes in v1:
time: 162 us; the launch traced here: 160 us
  blocking collectives  77.4 us (48%)
  Pallas kernels  39.3 us (24%)
  starting transfers between devices  19.2 us (12%)
  local copies, waits for them, and re-layouts  11.7 us (7%)
  waiting for transfers between devices  8.27 us (5%)
  other arithmetic  3.66 us (2%)
    all_to_all x1, blocking collectives, on_device(): parts = lax.all_to_all(parts, CHIPS, 0, 0, tiled=True)  42.9 us
    all_to_all x1, blocking collectives, on_device(): lax.all_to_all(jnp.broadcast_to(part, parts.shape), CHIPS, 0, 0, tiled=True)  34.6 us
    pallas_call x1, Pallas kernels, stencil(): pl.pallas_call(stencil_kernel, grid_spec=pltpu.PrefetchScalarGridSpec(num...  17.2 us
    pallas_call x1, Pallas kernels, band_tiles(): pl.pallas_call(tiles_kernel, grid=(ROWS,), in_specs=[pl.BlockSpec((1, 16,...  9.64 us
    unnamed x14, local copies, waits for them, and re-layouts  8.95 us
    pallas_call x1, Pallas kernels, input_gradient(): pl.pallas_call(input_kernel, grid=(ROWS // group,), in_specs=[pl.BlockSpe...  7.45 us
    ppermute x1, starting transfers between devices, on_device(): before = lax.ppermute(last, AXES, SOUTH)  5.47 us
    ppermute x1, waiting for transfers between devices, on_device(): left = lax.ppermute(cotangent[:, COLS - REACH:], AXES, EAST)  5.39 us
  transfers between devices with their start and end apart: 7, of which 2 were waited for; matrix products, arithmetic and copies ran while one was open for 5% of the time, Pallas kernels for 11%

profile of v1, /device:TPU:1, one launch (start us, length us, event | category | flops | bytes accessed | tf_op | source)
XLA Modules:
  0.0 160.5 jit_solution(8156644547783740772)
XLA Ops:
  0.6 0.0 copy-start.3
  0.6 0.0 copy-start.4
  0.6 2.2 %copy.69.own = bf16[16,90,512]{2,1,0:T(8,128)(2,1)S(1)} copy(bf16[16,90,512]{2,0,1:T(8,128)(2,1)} %param.5) | data formatting | bytes 2949120 | tf_op args[0]
  2.9 0.0 copy-start
  2.9 1.0 fusion.10
  3.9 2.5 %collective-permute-start = (bf16[16,16,512]{2,1,0:T(8,128)(2,1)}, bf16[16,16,512]{2,1,0:T(8,128)(2,1)}, u32[]{:S(2)}, u32[]{:S(2)}) collective-permute-start(bf16[16,16,512]{2,1,0:T(8,128)(2,1)} %get-tuple-element.22), channel_id=1, source_target_pairs={{0,1},{1,2},{2,3},{3,4},{4,5},{5,6},{6,7},{7,8},{8,9},{9,10},{10,1... | collective-permute-start | bytes 786440 | tf_op jit(solution)/shard_map/ppermute | solution.py:208
  6.3 4.9 %collective-permute-start.1 = (bf16[16,16,512]{2,1,0:T(8,128)(2,1)}, bf16[16,16,512]{2,1,0:T(8,128)(2,1)}, u32[]{:S(2)}, u32[]{:S(2)}) collective-permute-start(bf16[16,16,512]{2,1,0:T(8,128)(2,1)} %get-tuple-element.21), channel_id=1, source_target_pairs={{0,15},{1,0},{2,1},{3,2},{4,3},{5,4},{6,5},{7,6},{8,7},{9,8},{10,9... | collective-permute-start | bytes 786440 | tf_op jit(solution)/shard_map/ppermute | solution.py:209
  11.2 0.0 copy-done.3
  11.2 0.4 copy.61
  11.7 0.0 copy-done.4
  11.7 0.1 broadcast_compare_fusion
  11.8 0.1 broadcast_select_fusion
  11.8 0.1 slice_bitcast_fusion.2
  11.9 0.0 copy-done
  11.9 0.1 fusion.8
  12.1 0.1 pad.18.clone
  12.1 5.4 %collective-permute-done.left = bf16[16,16,512]{2,1,0:T(8,128)(2,1)} collective-permute-done((bf16[16,16,512]{2,1,0:T(8,128)(2,1)}, bf16[16,16,512]{2,1,0:T(8,128)(2,1)}, u32[]{:S(2)}, u32[]{:S(2)}) %collective-permute-start) | collective-permute-done | bytes 262176 | tf_op jit(solution)/shard_map/ppermute | solution.py:208
  17.5 0.7 fusion.11
  18.3 0.0 collective-permute-done.1.right
  18.3 0.7 fusion.12
  19.0 0.1 broadcast_select_fusion.3
  19.1 0.7 collective-permute-start.2
  19.8 5.5 %collective-permute-start.3 = (bf16[1,128,512]{2,1,0:T(8,128)(2,1)S(1)}, bf16[1,128,512]{2,1,0:T(8,128)(2,1)S(1)}, u32[]{:S(2)}, u32[]{:S(2)}) collective-permute-start(bf16[1,128,512]{2,1,0:T(8,128)(2,1)S(1)} %get-tuple-element.17), channel_id=1, source_target_pairs={{0,16},{1,17},{2,18},{3,19},{4,20},{5,21},{6,22},{7,23},{8,24},{9,... | collective-permute-start | bytes 393224 | tf_op jit(solution)/shard_map/ppermute | solution.py:215
  25.3 1.9 %collective-permute-start.4 = (bf16[1,128,512]{2,1,0:T(8,128)(2,1)S(1)}, bf16[1,128,512]{2,1,0:T(8,128)(2,1)S(1)}, u32[]{:S(2)}, u32[]{:S(2)}) collective-permute-start(bf16[1,128,512]{2,1,0:T(8,128)(2,1)S(1)} %get-tuple-element.18), channel_id=1, source_target_pairs={{16,0},{17,1},{18,2},{19,3},{20,4},{21,5},{22,6},{23,7},{24,8},{25... | collective-permute-start | bytes 393224 | tf_op jit(solution)/shard_map/ppermute | solution.py:216
  27.3 0.1 rev.3
  27.4 0.7 pad_convert_fusion.rev_ref
  28.1 0.0 copy-start.1
  28.1 9.6 %band_tiles.1.tiles = bf16[16,384,384]{2,1,0:T(8,128)(2,1)} custom-call(f32[16,16,128]{2,1,0:T(8,128)} %pad_convert_fusion.rev_ref), custom_call_target="tpu_custom_call" | custom-call | tf_op jit(solution)/shard_map/band_tiles/pallas_call | solution.py:37
  37.7 0.0 copy-done.1
  37.7 2.0 %copy.70.act = bf16[16,90,512]{2,1,0:T(8,128)(2,1)} copy(bf16[16,90,512]{2,0,1:T(8,128)(2,1)S(1)} %copy-done.1) | data formatting | bytes 2949120 | tf_op args[1]
  39.7 0.0 collective-permute-done.2
  39.7 0.0 collective-permute-done.3
  39.7 0.0 collective-permute-done.4
  39.7 0.7 broadcast_select_fusion.1
  40.4 17.2 %stencil.1 = (bf16[4,1536,512]{2,1,0:T(8,128)(2,1)}, bf16[2,512,512]{2,1,0:T(8,128)(2,1)}) custom-call(s32[1]{0:T(128)} %bitcast.core, bf16[16,384,384]{2,1,0:T(8,128)(2,1)} %band_tiles.1.tiles, bf16[16,90,512]{2,1,0:T(8,128)(2,1)} %copy-done, bf16[16,16,512]{2,1,0:T(8,128)(2,1)} %collective-permute-done.left, ...), custom_call_target="tpu_custom_call" | custom-call | tf_op jit(solution)/shard_map/stencil/pallas_call | solution.py:84
  57.7 0.0 collective-permute-start.5
  57.7 2.9 %collective-permute-done.5.got = bf16[2,512,512]{2,1,0:T(8,128)(2,1)S(1)} collective-permute-done((bf16[2,512,512]{2,1,0:T(8,128)(2,1)}, bf16[2,512,512]{2,1,0:T(8,128)(2,1)S(1)}, u32[]{:S(2)}, u32[]{:S(2)}) %collective-permute-start.5) | collective-permute-done | bytes 1048608 | tf_op jit(solution)/shard_map/ppermute | solution.py:221
  60.5 0.0 copy-start.2
  60.5 1.0 copy-done.2
  61.5 5.0 %own_half.1 = bf16[2,512,512]{2,1,0:T(8,128)(2,1)} custom-call(s32[1]{0:T(128)} %bitcast.core, bf16[4,1536,512]{2,1,0:T(8,128)(2,1)} %get-tuple-element.4.f, bf16[16,90,512]{2,1,0:T(8,128)(2,1)} %copy.70.act, bf16[2,512,512]{2,1,0:T(8,128)(2,1)} %copy-done.2), custom_call_target="tpu_custom_call" | custom-call | tf_op jit(solution)/shard_map/own_half/pallas_call | solution.py:150
  66.5 42.9 %all_to_all.10 = bf16[128,8,512]{2,1,0:T(8,128)(2,1)S(1)} all-to-all(bf16[128,8,512]{2,1,0:T(8,128)(2,1)} %bitcast.24), channel_id=1, replica_groups=mesh['y'=4,'xh'=2,'core'=2,'xl'=2,'z'=8] {'y','xh','xl','z'}, dimensions={0} | all-to-all | bytes 2097152 | tf_op jit(solution)/shard_map/all_to_all | solution.py:226
  109.4 0.2 convert_reduce_fusion
  109.6 0.1 broadcast_in_dim.23
  109.7 34.6 %all_to_all.11 = bf16[128,8,512]{2,1,0:T(8,128)(2,1)S(1)} all-to-all(bf16[128,8,512]{2,1,0:T(8,128)(2,1)S(1)} %broadcast_in_dim.23), channel_id=1, replica_groups=mesh['y'=4,'xh'=2,'core'=2,'xl'=2,'z'=8] {'y','xh','xl','z'}, dimensions={0} | all-to-all | bytes 2097152 | tf_op jit(solution)/shard_map/all_to_all | solution.py:229
  144.2 3.8 %collective-permute-start.6 = (bf16[2,512,512]{2,1,0:T(8,128)(2,1)S(1)}, bf16[2,512,512]{2,1,0:T(8,128)(2,1)S(1)}, u32[]{:S(2)}, u32[]{:S(2)}) collective-permute-start(bf16[2,512,512]{2,1,0:T(8,128)(2,1)S(1)} %bitcast.22), channel_id=1, source_target_pairs={{0,16},{1,17},{2,18},{3,19},{4,20},{5,21},{6,22},{7,23},{8,24},{9,... | collective-permute-start | bytes 3145736 | tf_op jit(solution)/shard_map/ppermute | solution.py:231
  148.1 7.5 %input_gradient.1 = bf16[16,90,512]{2,1,0:T(8,128)(2,1)} custom-call(bf16[4,1536,512]{2,1,0:T(8,128)(2,1)} %get-tuple-element.4.f, bf16[4,512,512]{2,1,0:T(8,128)(2,1)} %weight.1), custom_call_target="tpu_custom_call" | custom-call | flops 3221225472 | bytes 10000000 | tf_op jit(solution)/shard_map/input_gradient/pallas_call | solution.py:123
  155.5 3.3 %copy.72 = bf16[16,90,512]{2,0,1:T(8,128)(2,1)} copy(bf16[16,90,512]{2,1,0:T(8,128)(2,1)} %input_gradient.1) | data formatting | bytes 2949120
  158.9 0.0 collective-permute-done.6
  158.9 1.6 %maximum_select_fusion = bf16[4,512,512]{2,1,0:T(8,128)(2,1)} fusion(bf16[2,512,512]{2,1,0:T(8,128)(2,1)S(1)} %collective-permute-done.6, bf16[2,512,512]{2,1,0:T(8,128)(2,1)S(1)} %bitcast.23, pred[]{:T(512)S(6)} %eq.12), kind=kLoop, calls=%fused_computation | loop fusion | flops 3145728 | bytes 4194305 | tf_op jit(solution)/shard_map/jit(_where)/select_n | solution.py:232
  (8 shorter events, 0.1 us)
Async XLA Ops:
  0.6 10.6 %copy-start.3 = (bf16[4,3,33,256]{3,0,2,1:T(4,128)(2,1)S(1)}, bf16[4,3,33,256]{3,0,2,1:T(4,128)(2,1)}, u32[]{:S(2)}) copy-start(bf16[4,3,33,256]{3,0,2,1:T(4,128)(2,1)} %param.8) | copy-start | bytes 608260
  0.6 11.0 %copy-start.4 = (s32[256]{0:T(256)S(1)}, s32[256]{0:T(256)}, u32[]{:S(2)}) copy-start(s32[256]{0:T(256)} %param.9) | copy-start | bytes 3076
  2.9 9.0 %copy-start = (bf16[16,90,512]{2,1,0:T(8,128)(2,1)}, bf16[16,90,512]{2,1,0:T(8,128)(2,1)S(1)}, u32[]{:S(2)}) copy-start(bf16[16,90,512]{2,1,0:T(8,128)(2,1)S(1)} %copy.69.own) | copy-start | bytes 4423684
  3.9 13.7 %collective-permute-start = (bf16[16,16,512]{2,1,0:T(8,128)(2,1)}, bf16[16,16,512]{2,1,0:T(8,128)(2,1)}, u32[]{:S(2)}, u32[]{:S(2)}) collective-permute-start(bf16[16,16,512]{2,1,0:T(8,128)(2,1)} %get-tuple-element.22), channel_id=1, source_target_pairs={{0,1},{1,2},{2,3},{3,4},{4,5},{5,6},{6,7},{7,8},{8,9},{9,10},{10,1... | collective-permute-start | bytes 786440 | tf_op jit(solution)/shard_map/ppermute | solution.py:208
  6.3 12.0 %collective-permute-start.1 = (bf16[16,16,512]{2,1,0:T(8,128)(2,1)}, bf16[16,16,512]{2,1,0:T(8,128)(2,1)}, u32[]{:S(2)}, u32[]{:S(2)}) collective-permute-start(bf16[16,16,512]{2,1,0:T(8,128)(2,1)} %get-tuple-element.21), channel_id=1, source_target_pairs={{0,15},{1,0},{2,1},{3,2},{4,3},{5,4},{6,5},{7,6},{8,7},{9,8},{10,9... | collective-permute-start | bytes 786440 | tf_op jit(solution)/shard_map/ppermute | solution.py:209
  19.1 20.6 %collective-permute-start.2 = (bf16[1,128,512]{2,1,0:T(8,128)(2,1)S(1)}, bf16[1,128,512]{2,1,0:T(8,128)(2,1)S(1)}, u32[]{:S(2)}, u32[]{:S(2)}) collective-permute-start(bf16[1,128,512]{2,1,0:T(8,128)(2,1)S(1)} %get-tuple-element.16), channel_id=1, source_target_pairs={{0,8},{1,9},{2,10},{3,11},{4,12},{5,13},{6,14},{7,15},{8,0},{9,1},... | collective-permute-start | bytes 393224 | tf_op jit(solution)/shard_map/ppermute | solution.py:217
  19.8 19.9 %collective-permute-start.3 = (bf16[1,128,512]{2,1,0:T(8,128)(2,1)S(1)}, bf16[1,128,512]{2,1,0:T(8,128)(2,1)S(1)}, u32[]{:S(2)}, u32[]{:S(2)}) collective-permute-start(bf16[1,128,512]{2,1,0:T(8,128)(2,1)S(1)} %get-tuple-element.17), channel_id=1, source_target_pairs={{0,16},{1,17},{2,18},{3,19},{4,20},{5,21},{6,22},{7,23},{8,24},{9,... | collective-permute-start | bytes 393224 | tf_op jit(solution)/shard_map/ppermute | solution.py:215
  25.3 14.4 %collective-permute-start.4 = (bf16[1,128,512]{2,1,0:T(8,128)(2,1)S(1)}, bf16[1,128,512]{2,1,0:T(8,128)(2,1)S(1)}, u32[]{:S(2)}, u32[]{:S(2)}) collective-permute-start(bf16[1,128,512]{2,1,0:T(8,128)(2,1)S(1)} %get-tuple-element.18), channel_id=1, source_target_pairs={{16,0},{17,1},{18,2},{19,3},{20,4},{21,5},{22,6},{23,7},{24,8},{25... | collective-permute-start | bytes 393224 | tf_op jit(solution)/shard_map/ppermute | solution.py:216
  28.1 9.6 %copy-start.1 = (bf16[16,90,512]{2,0,1:T(8,128)(2,1)S(1)}, bf16[16,90,512]{2,0,1:T(8,128)(2,1)}, u32[]{:S(2)}) copy-start(bf16[16,90,512]{2,0,1:T(8,128)(2,1)} %param.6) | copy-start | bytes 4423684
  57.7 2.9 %collective-permute-start.5 = (bf16[2,512,512]{2,1,0:T(8,128)(2,1)}, bf16[2,512,512]{2,1,0:T(8,128)(2,1)S(1)}, u32[]{:S(2)}, u32[]{:S(2)}) collective-permute-start(bf16[2,512,512]{2,1,0:T(8,128)(2,1)} %get-tuple-element.5), channel_id=1, source_target_pairs={{0,16},{1,17},{2,18},{3,19},{4,20},{5,21},{6,22},{7,23},{8,24},{9,... | collective-permute-start | bytes 3145736 | tf_op jit(solution)/shard_map/ppermute | solution.py:221
  60.5 1.0 copy-start.2
  144.2 14.6 %collective-permute-start.6 = (bf16[2,512,512]{2,1,0:T(8,128)(2,1)S(1)}, bf16[2,512,512]{2,1,0:T(8,128)(2,1)S(1)}, u32[]{:S(2)}, u32[]{:S(2)}) collective-permute-start(bf16[2,512,512]{2,1,0:T(8,128)(2,1)S(1)} %bitcast.22), channel_id=1, source_target_pairs={{0,16},{1,17},{2,18},{3,19},{4,20},{5,21},{6,22},{7,23},{8,24},{9,... | collective-permute-start | bytes 3145736 | tf_op jit(solution)/shard_map/ppermute | solution.py:231

commit v2 on v1

v2 whole, which is shorter than its diff:
```python
import jax
import jax.numpy as jnp
from jax import lax
from jax.experimental import pallas as pl
from jax.experimental.pallas import tpu as pltpu
from jax.sharding import Mesh, PartitionSpec as P

ROWS, COLS, REACH = 16, 90, 16
PAD, HALF, SPAN, WIDE = 96, 48, 80, 128
DEPTH = 256
CHANNELS, FILTERS, TAPS = 512, 4, 3
AXES = ("y", "xh", "core", "xl", "zh", "zl")
BLOCK = ("y", "xh", "xl", "zl")
LAT, LON = 16, 16
VMEM = 56 * 1024 * 1024
BF16, F32 = jnp.bfloat16, jnp.float32


def turned(block):
    return jnp.swapaxes(block, 0, 1)


def prepare_kernel(taps, act, tiles, cells):
    step = pl.program_id(0)
    for r in range(ROWS // 2):
        for k in range(FILTERS):
            row = jnp.broadcast_to(taps[r, pl.ds(k, 1), :], (HALF, DEPTH))
            band = pltpu.roll(row, 0, 1, stride=1, stride_axis=0)
            tiles[r, k * HALF : (k + 1) * HALF, :] = band.astype(BF16)
    col = lax.broadcasted_iota(jnp.int32, (16, 16, CHANNELS), 0)
    for b in range(HALF // 16):
        block = act[b * 16 : (b + 1) * 16]
        if (b + 1) * 16 > COLS - HALF:
            block = jnp.where(col + (step * HALF + b * 16) < COLS, block, jnp.zeros_like(block))
        cells[:, b * 16 : (b + 1) * 16, :] = turned(block)


def prepare(taps, act):
    return pl.pallas_call(
        prepare_kernel,
        grid=(2,),
        in_specs=[
            pl.BlockSpec((ROWS // 2, 8, DEPTH), lambda i: (i, 0, 0)),
            pl.BlockSpec((HALF, ROWS, CHANNELS), lambda i: (i, 0, 0)),
        ],
        out_specs=[
            pl.BlockSpec((ROWS // 2, FILTERS * HALF, DEPTH), lambda i: (i, 0, 0)),
            pl.BlockSpec((ROWS, HALF, CHANNELS), lambda i: (0, i, 0)),
        ],
        out_shape=[
            jax.ShapeDtypeStruct((ROWS, FILTERS * HALF, DEPTH), BF16),
            jax.ShapeDtypeStruct((ROWS, PAD, CHANNELS), BF16),
        ],
        cost_estimate=pl.CostEstimate(flops=10_000_000, bytes_accessed=5_000_000, transcendentals=0),
        compiler_params=pltpu.CompilerParams(vmem_limit_bytes=VMEM),
        name="prepare",
    )(taps, act)


GROUP = 4
STEPS = ROWS // GROUP


def outer(f, cells):
    f = f.reshape(ROWS * PAD, CHANNELS)
    cells = cells.reshape(ROWS * PAD, CHANNELS)
    return lax.dot_general(f, cells, (((0,), (0,)), ((), ())), preferred_element_type=F32)


def stencil_kernel(place, tiles, own, lon_a, lon_b, lat_a, lat_b, cells, f_out, send, low, high, held):
    step = pl.program_id(0)

    @pl.when(step == 0)
    def _():
        even = place[1] == 0
        left = jnp.where(even, lon_b[...], lon_a[...])
        right = jnp.where(even, lon_a[...], lon_b[...])
        blocks = [left] + [own[16 * b : 16 * (b + 1)] for b in range(5)]
        blocks.append(jnp.concatenate([own[80:COLS], right[:6]]))
        blocks.append(jnp.concatenate([right[6:], jnp.zeros((6, ROWS, CHANNELS), BF16)]))
        for b, block in enumerate(blocks):
            block = turned(block)
            if b < 5:
                low[1 : ROWS + 1, 16 * b : 16 * (b + 1), :] = block
            if b > 2:
                high[1 : ROWS + 1, 16 * (b - 3) : 16 * (b - 2), :] = block
        first = place[0] == 0
        before = jnp.where(first, lat_b[...], lat_a[...])
        after = jnp.where(first, lat_a[...], lat_b[...])
        low[0], low[ROWS + 1] = before[:SPAN], after[:SPAN]
        high[0], high[ROWS + 1] = before[HALF:], after[HALF:]

    @pl.when(step < STEPS)
    def _():
        rest = jnp.zeros((DEPTH - TAPS * SPAN, CHANNELS), BF16)
        for j in range(GROUP):
            r = step * GROUP + j
            for h, source in enumerate((low, high)):
                rows = source[pl.ds(r, TAPS)].reshape(TAPS * SPAN, CHANNELS)
                rows = jnp.concatenate([rows, rest])
                f = jnp.dot(tiles[j], rows, preferred_element_type=F32).astype(BF16)
                f = f.reshape(FILTERS, HALF, CHANNELS)
                f_out[:, j, h * HALF : (h + 1) * HALF, :] = f
                held[:, r, h * HALF : (h + 1) * HALF, :] = f

    @pl.when(step >= STEPS)
    def _():
        k = 2 * (1 - place[0]) + step - STEPS
        send[0] = outer(held[k], cells[...]).astype(BF16)


def stencil(place, tiles, own, lon_a, lon_b, lat_a, lat_b, cells):
    whole = lambda a: pl.BlockSpec(a.shape, lambda i, c: (0,) * a.ndim)
    return pl.pallas_call(
        stencil_kernel,
        grid_spec=pltpu.PrefetchScalarGridSpec(
            num_scalar_prefetch=1,
            grid=(STEPS + 2,),
            in_specs=[
                pl.BlockSpec((GROUP, FILTERS * HALF, DEPTH), lambda i, c: (jnp.minimum(i, STEPS - 1), 0, 0)),
                *[whole(a) for a in (own, lon_a, lon_b, lat_a, lat_b, cells)],
            ],
            out_specs=[
                pl.BlockSpec((FILTERS, GROUP, PAD, CHANNELS), lambda i, c: (0, jnp.minimum(i, STEPS - 1), 0, 0)),
                pl.BlockSpec((1, CHANNELS, CHANNELS), lambda i, c: (jnp.maximum(i - STEPS, 0), 0, 0)),
            ],
            scratch_shapes=[
                pltpu.VMEM((ROWS + 2, SPAN, CHANNELS), BF16),
                pltpu.VMEM((ROWS + 2, SPAN, CHANNELS), BF16),
                pltpu.VMEM((FILTERS, ROWS, PAD, CHANNELS), BF16),
            ],
        ),
        out_shape=[
            jax.ShapeDtypeStruct((FILTERS, ROWS, PAD, CHANNELS), BF16),
            jax.ShapeDtypeStruct((2, CHANNELS, CHANNELS), BF16),
        ],
        compiler_params=pltpu.CompilerParams(vmem_limit_bytes=VMEM),
        name="stencil",
    )(place, tiles, own, lon_a, lon_b, lat_a, lat_b, cells)


def input_kernel(f, weight, out):
    cols = out.shape[0]
    total = 0.0
    for k in range(FILTERS):
        total += jnp.dot(f[k].reshape(ROWS * cols, CHANNELS), weight[k], preferred_element_type=F32)
    total = total.astype(BF16).reshape(ROWS, cols, CHANNELS)
    for b in range(cols // 16):
        out[b * 16 : (b + 1) * 16] = turned(total[:, b * 16 : (b + 1) * 16])


def input_gradient(f, weight):
    cols = 32
    flops = 2 * ROWS * PAD * FILTERS * CHANNELS * CHANNELS
    return pl.pallas_call(
        input_kernel,
        grid=(PAD // cols,),
        in_specs=[
            pl.BlockSpec((FILTERS, ROWS, cols, CHANNELS), lambda i: (0, 0, i, 0)),
            pl.BlockSpec((FILTERS, CHANNELS, CHANNELS), lambda i: (0, 0, 0)),
        ],
        out_specs=pl.BlockSpec((cols, ROWS, CHANNELS), lambda i: (i, 0, 0)),
        out_shape=jax.ShapeDtypeStruct((COLS, ROWS, CHANNELS), BF16),
        compiler_params=pltpu.CompilerParams(vmem_limit_bytes=VMEM),
        cost_estimate=pl.CostEstimate(flops=flops, bytes_accessed=10_000_000, transcendentals=0),
        name="input_gradient",
    )(f, weight)


def own_half_kernel(place, f, cells, got, out):
    out[0] = (outer(f[0], cells[...]) + got[0].astype(F32)).astype(BF16)


def own_half(place, f, cells, got):
    block = (1, CHANNELS, CHANNELS)
    return pl.pallas_call(
        own_half_kernel,
        grid_spec=pltpu.PrefetchScalarGridSpec(
            num_scalar_prefetch=1,
            grid=(2,),
            in_specs=[
                pl.BlockSpec((1, ROWS, PAD, CHANNELS), lambda i, c: (2 * c[0] + i, 0, 0, 0)),
                pl.BlockSpec(cells.shape, lambda i, c: (0, 0, 0)),
                pl.BlockSpec(block, lambda i, c: (i, 0, 0)),
            ],
            out_specs=pl.BlockSpec(block, lambda i, c: (i, 0, 0)),
        ),
        out_shape=jax.ShapeDtypeStruct((2, CHANNELS, CHANNELS), BF16),
        compiler_params=pltpu.CompilerParams(vmem_limit_bytes=VMEM),
        name="own_half",
    )(place, f, cells, got)


def device(lat, lon):
    return lat * LON + lon % LON


def route(target):
    return [(device(a, b), device(*target(a, b))) for a in range(LAT) for b in range(LON)]


def lat_b_partner(a, b):
    if a in (0, LAT - 1):
        return a, b + LON // 2
    return (a + 1 if a % 2 else a - 1), b


LON_A = route(lambda a, b: (a, b ^ 1))
LON_B = route(lambda a, b: (a, b + 1 if b % 2 else b - 1))
LAT_A = route(lambda a, b: (a ^ 1, b))
LAT_B = route(lat_b_partner)
SIBLING = LAT_A


def along_z(mask):
    return route(lambda a, b: (a, b ^ mask))


def reversed_taps(basis, reach, band):
    span = basis.shape[2]
    offsets = jnp.arange(span, dtype=jnp.int32) - REACH
    masked = jnp.where(jnp.abs(offsets)[:, None] <= reach[None, :], basis, 0)
    total = masked.shape[3]
    slabs = []
    for q in range(TAPS):
        t = TAPS - 1 - q
        edge = jnp.zeros_like(masked[:, t, :, :1])
        first = masked[:, 0, :, :1] if q == 0 else edge
        last = masked[:, 2, :, total - 1 :] if q == 2 else edge
        padded = jnp.concatenate([first, masked[:, t], last], axis=2)
        slabs.append(lax.dynamic_slice_in_dim(padded, band * ROWS + q, ROWS, 2))
    taps = jnp.stack(slabs)[:, :, ::-1, :].astype(F32)
    taps = jnp.pad(jnp.transpose(taps, (3, 1, 0, 2)), ((0, 0), (0, 0), (0, 0), (0, SPAN - span)))
    taps = taps.reshape(ROWS, FILTERS, TAPS * SPAN)
    return jnp.pad(taps, ((0, 0), (0, 8 - FILTERS), (0, DEPTH - TAPS * SPAN)))


def haloes(own, core, odd):
    start_a = jnp.where(odd == 0, COLS - REACH, 0)
    start_b = jnp.where(odd == 0, 0, COLS - REACH)
    lon_a, lon_b = (lax.dynamic_slice_in_dim(own, s, REACH, 0) for s in (start_a, start_b))
    row_a = jnp.where(core == 0, ROWS - 1, 0)
    row_b = ROWS - 1 - row_a
    edges = lambda x: jnp.concatenate([x[:, :1], x[:, ROWS - 1 :]], axis=1)
    edge_a = lax.ppermute(edges(lon_a), AXES, LON_A)
    edge_b = lax.ppermute(edges(lon_b), AXES, LON_B)
    lon_a = lax.ppermute(lon_a, AXES, LON_A)
    lon_b = lax.ppermute(lon_b, AXES, LON_B)
    left = jnp.where(odd == 0, edge_b, edge_a)
    right = jnp.where(odd == 0, edge_a, edge_b)
    middle = edges(own)
    rest = jnp.zeros((WIDE - COLS - 2 * REACH, 2, CHANNELS), BF16)
    wide = jnp.concatenate([left, middle, right, rest])
    first, last = wide[:, 0], wide[:, 1]
    lat_a = lax.ppermute(jnp.where(core == 0, last, first), AXES, LAT_A)
    lat_b = lax.ppermute(jnp.where(core == 0, first, last), AXES, LAT_B)
    return lon_a, lon_b, lat_a, lat_b


def summed(parts, groups, axes):
    parts = lax.all_to_all(parts.reshape(groups, -1, CHANNELS), axes, 0, 0, tiled=True)
    return jnp.sum(parts.astype(F32), axis=0)


def on_device(cotangent, activations, weight, basis, reach):
    band = lax.axis_index(("y", "xh", "core"))
    core = lax.axis_index("core").astype(jnp.int32)
    odd = lax.axis_index("zl").astype(jnp.int32)
    place = jnp.stack([core, odd])
    own, act = jnp.swapaxes(cotangent, 0, 1), jnp.swapaxes(activations, 0, 1)
    around = haloes(own, core, odd)
    tiles, cells = prepare(reversed_taps(basis, reach, band), act)
    f, send = stencil(place, tiles, own, *around, cells)
    got = lax.ppermute(send, AXES, SIBLING)
    grad_input = jnp.swapaxes(input_gradient(f, weight), 0, 1)
    half = own_half(place, f, cells, got)
    part = lax.optimization_barrier(summed(half.reshape(-1, CHANNELS), 32, BLOCK).astype(BF16))
    others = [lax.ppermute(part, AXES, along_z(m)).astype(F32) for m in (2, 6, 4)]
    norm_factor = float(ROWS * COLS * LAT * LON) ** (-0.5)
    part = (part.astype(F32) + others[0]) + (others[1] + others[2])
    part = (part * norm_factor).astype(BF16)
    parts = lax.all_to_all(jnp.broadcast_to(part, (32, *part.shape)), BLOCK, 0, 0, tiled=True)
    mine = parts.reshape(2, CHANNELS, CHANNELS)
    theirs = lax.ppermute(mine, AXES, SIBLING)
    grad_weight = jnp.where(core == 0, jnp.concatenate([mine, theirs]), jnp.concatenate([theirs, mine]))
    return grad_input, grad_weight


def solution(mesh):
    finer = Mesh(mesh.devices.reshape(4, 2, 2, 2, 4, 2), AXES)
    cells = P(("y", "xh", "core"), ("xl", "zh", "zl"), None)
    return jax.shard_map(
        on_device, mesh=finer, in_specs=(cells, cells, P(), P(), P()), out_specs=(cells, P()), check_vma=False
    )
```

time: 162 us -> 115 us (0.71)
  blocking collectives: 77.4 us -> 40.3 us
  Pallas kernels: 39.3 us -> 26.7 us
  starting transfers between devices: 19.2 us -> 24.5 us
  local copies, waits for them, and re-layouts: 11.7 us -> 7.8 us
  other arithmetic: 3.66 us -> 5.6 us
    all_to_all x2, blocking collectives: 77.4 us -> 40.3 us  [the longest x1 22.5 us: summed(): lax.all_to_all(parts.reshape(groups, -1, CHANNELS), axes, 0, 0, tiled=True)]
    pallas_call x1, Pallas kernels: 17.2 us -> 10.5 us  [stencil(): pl.pallas_call(stencil_kernel, grid_spec=pltpu.PrefetchScalarGridSpec(num...]
    pallas_call x2, Pallas kernels: 17.1 us -> 10.6 us  [the longest x1 7.5 us: input_gradient(): pl.pallas_call(input_kernel, grid=(PAD // cols,), in_specs=[pl.BlockSpec(...]
    unnamed x14 -> x13, local copies, waits for them, and re-layouts: 8.95 us -> 4.36 us
    ppermute x5 -> x9, starting transfers between devices: 15.4 us -> 19.8 us  [the longest x1 7.42 us: haloes(): lon_b = lax.ppermute(lon_b, AXES, LON_B)]
    ppermute x0 -> x2, local copies, waits for them, and re-layouts: none -> 2.72 us  [the longest x1 1.84 us: haloes(): lon_b = lax.ppermute(lon_b, AXES, LON_B)]
    slice x4 -> x2, local copies, waits for them, and re-layouts: 2.45 us -> 0.02 us  [haloes(): edges = lambda x: jnp.concatenate([x[:, :1], x[:, ROWS - 1:]], axis=1)]
    ppermute x5 -> x9, waiting for transfers between devices: 5.4 us -> 6.6 us  [the longest x1 3.49 us: haloes(): edge_a = lax.ppermute(edges(lon_a), AXES, LON_A)]
  transfers between devices with their start and end apart: 7 -> 11, of which waited for: 2 -> 5; matrix products, arithmetic and copies ran while one was open for 5% -> 6% of each run, Pallas kernels for 11% -> 9%
where the time goes in v2:
time: 115 us
  blocking collectives  40.3 us (35%)
  Pallas kernels  26.7 us (23%)
  starting transfers between devices  24.5 us (21%)
  waiting for transfers between devices  9.1 us (8%)
  local copies, waits for them, and re-layouts  7.8 us (7%)
  other arithmetic  5.6 us (5%)
    all_to_all x1, blocking collectives, summed(): lax.all_to_all(parts.reshape(groups, -1, CHANNELS), axes, 0, 0, tiled=True)  22.5 us
    all_to_all x1, blocking collectives, on_device(): lax.all_to_all(jnp.broadcast_to(part, (32, *part.shape)), BLOCK, 0, 0, ti...  17.8 us
    pallas_call x1, Pallas kernels, stencil(): pl.pallas_call(stencil_kernel, grid_spec=pltpu.PrefetchScalarGridSpec(num...  10.5 us
    pallas_call x1, Pallas kernels, input_gradient(): pl.pallas_call(input_kernel, grid=(PAD // cols,), in_specs=[pl.BlockSpec(...  7.5 us
    ppermute x1, starting transfers between devices, haloes(): lon_b = lax.ppermute(lon_b, AXES, LON_B)  7.42 us
    ppermute x3, starting transfers between devices, on_device(): lax.ppermute(part, AXES, along_z(m)).astype(F32)  5.74 us
    pallas_call x1, Pallas kernels, own_half(): pl.pallas_call(own_half_kernel, grid_spec=pltpu.PrefetchScalarGridSpec(nu...  5.55 us
    ppermute x1, starting transfers between devices, haloes(): lat_b = lax.ppermute(jnp.where(core == 0, first, last), AXES, LAT_B)  5.09 us
  transfers between devices with their start and end apart: 11, of which 5 were waited for; matrix products, arithmetic and copies ran while one was open for 6% of the time, Pallas kernels for 9%

profile of v2, /device:TPU:1, one launch (start us, length us, event | category | flops | bytes accessed | tf_op | source)
XLA Modules:
  0.0 114.8 jit_solution(17727446007536216853)
XLA Ops:
  0.6 0.0 copy-start.1
  0.7 0.0 copy-start.4
  0.7 2.2 %copy.73 = bf16[16,90,512]{2,1,0:T(8,128)(2,1)S(1)} copy(bf16[16,90,512]{2,0,1:T(8,128)(2,1)} %param.5) | data formatting | bytes 2949120 | tf_op args[0]
  2.9 0.2 dynamic-slice_bitcast_fusion
  3.1 7.4 %collective-permute-start.1 = (bf16[16,16,512]{2,0,1:T(8,128)(2,1)S(1)}, bf16[16,16,512]{2,0,1:T(8,128)(2,1)}, u32[]{:S(2)}, u32[]{:S(2)}) collective-permute-start(bf16[16,16,512]{2,0,1:T(8,128)(2,1)S(1)} %get-tuple-element.12), channel_id=1, source_target_pairs={{0,15},{1,2},{2,1},{3,4},{4,3},{5,6},{6,5},{7,8},{8,7},{9,10},{10,... | collective-permute-start | bytes 786440 | tf_op jit(solution)/shard_map/ppermute | solution.py:248
  10.5 0.0 collective-permute-start
  10.5 0.6 pad_maximum_fusion.2
  11.2 1.5 %collective-permute-start.3 = (bf16[16,2,512]{2,0,1:T(8,128)(2,1)}, bf16[16,2,512]{2,0,1:T(8,128)(2,1)}, u32[]{:S(2)}, u32[]{:S(2)}) collective-permute-start(bf16[16,2,512]{2,0,1:T(8,128)(2,1)} %pad_maximum_fusion.2), channel_id=1, source_target_pairs={{0,1},{1,0},{2,3},{3,2},{4,5},{5,4},{6,7},{7,6},{8,9},{9,8},{10,11... | collective-permute-start | bytes 98312 | tf_op jit(solution)/shard_map/ppermute | solution.py:245
  12.6 0.6 pad_maximum_fusion.1
  13.2 0.1 collective-permute-start.2
  13.3 0.0 copy-done.1
  13.3 0.4 copy.56
  13.8 0.0 copy-done.4
  13.8 0.1 broadcast_compare_fusion
  13.9 0.1 broadcast_select_fusion
  14.0 0.1 slice_bitcast_fusion.2
  14.1 0.1 fusion.8
  14.2 0.1 rev.3
  14.4 0.1 reshape.23
  14.5 0.1 pad.22.clone
  14.6 3.5 %collective-permute-done.3 = bf16[16,2,512]{2,0,1:T(8,128)(2,1)} collective-permute-done((bf16[16,2,512]{2,0,1:T(8,128)(2,1)}, bf16[16,2,512]{2,0,1:T(8,128)(2,1)}, u32[]{:S(2)}, u32[]{:S(2)}) %collective-permute-start.3) | collective-permute-done | bytes 32800 | tf_op jit(solution)/shard_map/ppermute | solution.py:245
  18.1 0.3 collective-permute-done.2
  18.4 0.8 broadcast_select_fusion.2
  19.2 0.1 maximum_maximum_fusion
  19.4 5.1 %collective-permute-start.5 = (bf16[128,512]{1,0:T(8,128)(2,1)S(1)}, bf16[128,512]{1,0:T(8,128)(2,1)S(1)}, u32[]{:S(2)}, u32[]{:S(2)}) collective-permute-start(bf16[128,512]{1,0:T(8,128)(2,1)S(1)} %get-tuple-element.21), channel_id=1, source_target_pairs={{0,8},{1,9},{2,10},{3,11},{4,12},{5,13},{6,14},{7,15},{8,0},{9,1},... | collective-permute-start | bytes 393224 | tf_op jit(solution)/shard_map/ppermute | solution.py:256
  24.4 0.0 collective-permute-start.4
  24.4 0.7 pad_convert_fusion.taps
  25.1 3.1 %prepare.1 = (bf16[16,192,256]{2,1,0:T(8,128)(2,1)}, bf16[16,96,512]{2,1,0:T(8,128)(2,1)}) custom-call(f32[16,8,256]{2,1,0:T(8,128)} %pad_convert_fusion.taps, bf16[90,16,512]{2,1,0:T(8,128)(2,1)} %bitcast.40), custom_call_target="tpu_custom_call" | custom-call | flops 10000000 | bytes 5000000 | tf_op jit(solution)/shard_map/prepare/pallas_call | solution.py:39
  28.3 0.7 pad_add_fusion.place
  28.9 0.0 collective-permute-done.1
  28.9 1.8 %copy.66.lon_b = bf16[16,16,512]{2,1,0:T(8,128)(2,1)} copy(bf16[16,16,512]{2,0,1:T(8,128)(2,1)} %collective-permute-done.1) | data formatting | bytes 524288 | tf_op jit(solution)/shard_map/ppermute | solution.py:248
  30.8 0.0 collective-permute-done
  30.8 0.9 copy.65.lon_a
  31.7 0.0 collective-permute-done.5.lat_b
  31.7 0.0 copy-start.2
  31.7 0.0 collective-permute-done.4.lat_a
  31.7 0.0 copy-start.3
  31.7 0.6 copy-done.2
  32.3 0.1 copy-done.3
  32.4 10.5 %stencil.1 = (bf16[4,16,96,512]{3,2,1,0:T(8,128)(2,1)}, bf16[2,512,512]{2,1,0:T(8,128)(2,1)}) custom-call(s32[2]{0:T(128)} %pad_add_fusion.place, bf16[16,192,256]{2,1,0:T(8,128)(2,1)} %get-tuple-element.6.tiles, bf16[90,16,512]{2,1,0:T(8,128)(2,1)} %bitcast.35, bf16[16,16,512]{2,1,0:T(8,128)(2,1)} %copy.65.lon_a, bf16[16,16,512]{2,1,0:T(8,128)(2,1)} %copy.66.lon_b, ...), custom_call_target="tpu_custom_call" | custom-call | tf_op jit(solution)/shard_map/stencil/pallas_call | solution.py:114
  42.9 0.5 collective-permute-start.6
  43.4 2.5 %collective-permute-done.6.got = bf16[2,512,512]{2,1,0:T(8,128)(2,1)S(1)} collective-permute-done((bf16[2,512,512]{2,1,0:T(8,128)(2,1)}, bf16[2,512,512]{2,1,0:T(8,128)(2,1)S(1)}, u32[]{:S(2)}, u32[]{:S(2)}) %collective-permute-start.6) | collective-permute-done | bytes 1048608 | tf_op jit(solution)/shard_map/ppermute | solution.py:274
  45.9 0.0 copy-start
  45.9 1.0 copy-done
  46.9 5.6 %own_half.1 = bf16[2,512,512]{2,1,0:T(8,128)(2,1)} custom-call(s32[2]{0:T(128)} %pad_add_fusion.place, bf16[4,16,96,512]{3,2,1,0:T(8,128)(2,1)} %get-tuple-element.8.f, bf16[16,96,512]{2,1,0:T(8,128)(2,1)} %get-tuple-element.7.cells, bf16[2,512,512]{2,1,0:T(8,128)(2,1)} %copy-done), custom_call_target="tpu_custom_call" | custom-call | tf_op jit(solution)/shard_map/own_half/pallas_call | solution.py:176
  52.4 22.5 %all_to_all.10 = bf16[32,32,512]{2,1,0:T(8,128)(2,1)S(1)} all-to-all(bf16[32,32,512]{2,1,0:T(8,128)(2,1)} %bitcast.38), channel_id=1, replica_groups=mesh['y'=4,'xh'=2,'core'=2,'xl'=2,'zh'=4,'zl'=2] {'y','xh','xl','zl'}, dimensions={0} | all-to-all | bytes 2097152 | tf_op jit(solution)/shard_map/all_to_all | solution.py:261
  74.9 0.2 reduce_sum.12
  75.1 1.3 %collective-permute-start.9 = (bf16[32,512]{1,0:T(8,128)(2,1)S(1)}, bf16[32,512]{1,0:T(8,128)(2,1)S(1)}, u32[]{:S(2)}, u32[]{:S(2)}) collective-permute-start(bf16[32,512]{1,0:T(8,128)(2,1)S(1)} %reduce_sum.12), channel_id=1, source_target_pairs={{0,4},{1,5},{2,6},{3,7},{4,0},{5,1},{6,2},{7,3},{8,12},{9,13},{10,... | collective-permute-start | bytes 98312 | tf_op jit(solution)/shard_map/ppermute | solution.py:278
  76.4 2.5 %collective-permute-start.8 = (bf16[32,512]{1,0:T(8,128)(2,1)S(1)}, bf16[32,512]{1,0:T(8,128)(2,1)S(1)}, u32[]{:S(2)}, u32[]{:S(2)}) collective-permute-start(bf16[32,512]{1,0:T(8,128)(2,1)S(1)} %reduce_sum.12), channel_id=1, source_target_pairs={{0,6},{1,7},{2,4},{3,5},{4,2},{5,3},{6,0},{7,1},{8,14},{9,15},{10,... | collective-permute-start | bytes 98312 | tf_op jit(solution)/shard_map/ppermute | solution.py:278
  78.9 1.9 %collective-permute-start.7 = (bf16[32,512]{1,0:T(8,128)(2,1)S(1)}, bf16[32,512]{1,0:T(8,128)(2,1)S(1)}, u32[]{:S(2)}, u32[]{:S(2)}) collective-permute-start(bf16[32,512]{1,0:T(8,128)(2,1)S(1)} %reduce_sum.12), channel_id=1, source_target_pairs={{0,2},{1,3},{2,0},{3,1},{4,6},{5,7},{6,4},{7,5},{8,10},{9,11},{10,... | collective-permute-start | bytes 98312 | tf_op jit(solution)/shard_map/ppermute | solution.py:278
  80.8 1.0 collective-permute-done.9
  81.9 0.0 collective-permute-done.8
  81.9 1.7 %collective-permute-done.7 = bf16[32,512]{1,0:T(8,128)(2,1)S(1)} collective-permute-done((bf16[32,512]{1,0:T(8,128)(2,1)S(1)}, bf16[32,512]{1,0:T(8,128)(2,1)S(1)}, u32[]{:S(2)}, u32[]{:S(2)}) %collective-permute-start.7) | collective-permute-done | bytes 32800 | tf_op jit(solution)/shard_map/ppermute | solution.py:278
  83.6 0.1 broadcast_in_dim.19
  83.7 17.8 %all_to_all.11 = bf16[32,32,512]{2,1,0:T(8,128)(2,1)S(1)} all-to-all(bf16[32,32,512]{2,1,0:T(8,128)(2,1)S(1)} %broadcast_in_dim.19), channel_id=1, replica_groups=mesh['y'=4,'xh'=2,'core'=2,'xl'=2,'zh'=4,'zl'=2] {'y','xh','xl','zl'}, dimensions={0} | all-to-all | bytes 2097152 | tf_op jit(solution)/shard_map/all_to_all | solution.py:282
  101.5 4.1 %collective-permute-start.10 = (bf16[2,512,512]{2,1,0:T(8,128)(2,1)S(1)}, bf16[2,512,512]{2,1,0:T(8,128)(2,1)S(1)}, u32[]{:S(2)}, u32[]{:S(2)}) collective-permute-start(bf16[2,512,512]{2,1,0:T(8,128)(2,1)S(1)} %bitcast.36), channel_id=1, source_target_pairs={{0,16},{1,17},{2,18},{3,19},{4,20},{5,21},{6,22},{7,23},{8,24},{9,... | collective-permute-start | bytes 3145736 | tf_op jit(solution)/shard_map/ppermute | solution.py:284
  105.6 7.5 %input_gradient.1 = bf16[90,16,512]{2,1,0:T(8,128)(2,1)} custom-call(bf16[4,16,96,512]{3,2,1,0:T(8,128)(2,1)} %get-tuple-element.8.f, bf16[4,512,512]{2,1,0:T(8,128)(2,1)} %weight.1), custom_call_target="tpu_custom_call" | custom-call | flops 3221225472 | bytes 10000000 | tf_op jit(solution)/shard_map/input_gradient/pallas_call | solution.py:155
  113.1 0.0 collective-permute-done.10
  113.1 1.6 %maximum_select_fusion = bf16[4,512,512]{2,1,0:T(8,128)(2,1)} fusion(bf16[2,512,512]{2,1,0:T(8,128)(2,1)S(1)} %collective-permute-done.10, bf16[2,512,512]{2,1,0:T(8,128)(2,1)S(1)} %bitcast.37, pred[]{:T(512)S(6)} %eq.5), kind=kLoop, calls=%fused_computation | loop fusion | flops 3145728 | bytes 4194305 | tf_op jit(solution)/shard_map/jit(_where)/select_n | solution.py:285
  (11 shorter events, 0.2 us)
Async XLA Ops:
  0.6 12.7 %copy-start.1 = (bf16[4,3,33,256]{3,0,2,1:T(4,128)(2,1)S(1)}, bf16[4,3,33,256]{3,0,2,1:T(4,128)(2,1)}, u32[]{:S(2)}) copy-start(bf16[4,3,33,256]{3,0,2,1:T(4,128)(2,1)} %param.8) | copy-start | bytes 608260
  0.7 13.1 %copy-start.4 = (s32[256]{0:T(256)S(1)}, s32[256]{0:T(256)}, u32[]{:S(2)}) copy-start(s32[256]{0:T(256)} %param.9) | copy-start | bytes 3076
  3.1 25.8 %collective-permute-start.1 = (bf16[16,16,512]{2,0,1:T(8,128)(2,1)S(1)}, bf16[16,16,512]{2,0,1:T(8,128)(2,1)}, u32[]{:S(2)}, u32[]{:S(2)}) collective-permute-start(bf16[16,16,512]{2,0,1:T(8,128)(2,1)S(1)} %get-tuple-element.12), channel_id=1, source_target_pairs={{0,15},{1,2},{2,1},{3,4},{4,3},{5,6},{6,5},{7,8},{8,7},{9,10},{10,... | collective-permute-start | bytes 786440 | tf_op jit(solution)/shard_map/ppermute | solution.py:248
  10.5 20.3 %collective-permute-start = (bf16[16,16,512]{2,0,1:T(8,128)(2,1)S(1)}, bf16[16,16,512]{2,0,1:T(8,128)(2,1)S(1)}, u32[]{:S(2)}, u32[]{:S(2)}) collective-permute-start(bf16[16,16,512]{2,0,1:T(8,128)(2,1)S(1)} %get-tuple-element.13), channel_id=1, source_target_pairs={{0,1},{1,0},{2,3},{3,2},{4,5},{5,4},{6,7},{7,6},{8,9},{9,8},{10,11... | collective-permute-start | bytes 786440 | tf_op jit(solution)/shard_map/ppermute | solution.py:247
  11.2 6.9 %collective-permute-start.3 = (bf16[16,2,512]{2,0,1:T(8,128)(2,1)}, bf16[16,2,512]{2,0,1:T(8,128)(2,1)}, u32[]{:S(2)}, u32[]{:S(2)}) collective-permute-start(bf16[16,2,512]{2,0,1:T(8,128)(2,1)} %pad_maximum_fusion.2), channel_id=1, source_target_pairs={{0,1},{1,0},{2,3},{3,2},{4,5},{5,4},{6,7},{7,6},{8,9},{9,8},{10,11... | collective-permute-start | bytes 98312 | tf_op jit(solution)/shard_map/ppermute | solution.py:245
  13.2 5.2 %collective-permute-start.2 = (bf16[16,2,512]{2,0,1:T(8,128)(2,1)}, bf16[16,2,512]{2,0,1:T(8,128)(2,1)}, u32[]{:S(2)}, u32[]{:S(2)}) collective-permute-start(bf16[16,2,512]{2,0,1:T(8,128)(2,1)} %pad_maximum_fusion.1), channel_id=1, source_target_pairs={{0,15},{1,2},{2,1},{3,4},{4,3},{5,6},{6,5},{7,8},{8,7},{9,10},{10,... | collective-permute-start | bytes 98312 | tf_op jit(solution)/shard_map/ppermute | solution.py:246
  19.4 12.3 %collective-permute-start.5 = (bf16[128,512]{1,0:T(8,128)(2,1)S(1)}, bf16[128,512]{1,0:T(8,128)(2,1)S(1)}, u32[]{:S(2)}, u32[]{:S(2)}) collective-permute-start(bf16[128,512]{1,0:T(8,128)(2,1)S(1)} %get-tuple-element.21), channel_id=1, source_target_pairs={{0,8},{1,9},{2,10},{3,11},{4,12},{5,13},{6,14},{7,15},{8,0},{9,1},... | collective-permute-start | bytes 393224 | tf_op jit(solution)/shard_map/ppermute | solution.py:256
  24.4 7.2 %collective-permute-start.4 = (bf16[128,512]{1,0:T(8,128)(2,1)S(1)}, bf16[128,512]{1,0:T(8,128)(2,1)S(1)}, u32[]{:S(2)}, u32[]{:S(2)}) collective-permute-start(bf16[128,512]{1,0:T(8,128)(2,1)S(1)} %get-tuple-element.22), channel_id=1, source_target_pairs={{0,16},{1,17},{2,18},{3,19},{4,20},{5,21},{6,22},{7,23},{8,24},{9,... | collective-permute-start | bytes 393224 | tf_op jit(solution)/shard_map/ppermute | solution.py:255
  31.7 0.7 copy-start.2
  31.7 0.7 copy-start.3
  42.9 3.0 %collective-permute-start.6 = (bf16[2,512,512]{2,1,0:T(8,128)(2,1)}, bf16[2,512,512]{2,1,0:T(8,128)(2,1)S(1)}, u32[]{:S(2)}, u32[]{:S(2)}) collective-permute-start(bf16[2,512,512]{2,1,0:T(8,128)(2,1)} %get-tuple-element.9), channel_id=1, source_target_pairs={{0,16},{1,17},{2,18},{3,19},{4,20},{5,21},{6,22},{7,23},{8,24},{9,... | collective-permute-start | bytes 3145736 | tf_op jit(solution)/shard_map/ppermute | solution.py:274
  45.9 1.0 copy-start
  75.1 6.8 %collective-permute-start.9 = (bf16[32,512]{1,0:T(8,128)(2,1)S(1)}, bf16[32,512]{1,0:T(8,128)(2,1)S(1)}, u32[]{:S(2)}, u32[]{:S(2)}) collective-permute-start(bf16[32,512]{1,0:T(8,128)(2,1)S(1)} %reduce_sum.12), channel_id=1, source_target_pairs={{0,4},{1,5},{2,6},{3,7},{4,0},{5,1},{6,2},{7,3},{8,12},{9,13},{10,... | collective-permute-start | bytes 98312 | tf_op jit(solution)/shard_map/ppermute | solution.py:278
  76.4 5.5 %collective-permute-start.8 = (bf16[32,512]{1,0:T(8,128)(2,1)S(1)}, bf16[32,512]{1,0:T(8,128)(2,1)S(1)}, u32[]{:S(2)}, u32[]{:S(2)}) collective-permute-start(bf16[32,512]{1,0:T(8,128)(2,1)S(1)} %reduce_sum.12), channel_id=1, source_target_pairs={{0,6},{1,7},{2,4},{3,5},{4,2},{5,3},{6,0},{7,1},{8,14},{9,15},{10,... | collective-permute-start | bytes 98312 | tf_op jit(solution)/shard_map/ppermute | solution.py:278
  78.9 4.7 %collective-permute-start.7 = (bf16[32,512]{1,0:T(8,128)(2,1)S(1)}, bf16[32,512]{1,0:T(8,128)(2,1)S(1)}, u32[]{:S(2)}, u32[]{:S(2)}) collective-permute-start(bf16[32,512]{1,0:T(8,128)(2,1)S(1)} %reduce_sum.12), channel_id=1, source_target_pairs={{0,2},{1,3},{2,0},{3,1},{4,6},{5,7},{6,4},{7,5},{8,10},{9,11},{10,... | collective-permute-start | bytes 98312 | tf_op jit(solution)/shard_map/ppermute | solution.py:278
  101.5 11.6 %collective-permute-start.10 = (bf16[2,512,512]{2,1,0:T(8,128)(2,1)S(1)}, bf16[2,512,512]{2,1,0:T(8,128)(2,1)S(1)}, u32[]{:S(2)}, u32[]{:S(2)}) collective-permute-start(bf16[2,512,512]{2,1,0:T(8,128)(2,1)S(1)} %bitcast.36), channel_id=1, source_target_pairs={{0,16},{1,17},{2,18},{3,19},{4,20},{5,21},{6,22},{7,23},{8,24},{9,... | collective-permute-start | bytes 3145736 | tf_op jit(solution)/shard_map/ppermute | solution.py:284

commit v3 on v2

--- a/solution.py
+++ b/solution.py
@@ -12,7 +12,7 @@
 AXES = ("y", "xh", "core", "xl", "zh", "zl")
 BLOCK = ("y", "xh", "xl", "zl")
 LAT, LON = 16, 16
-VMEM = 56 * 1024 * 1024
+MIB = 1024 * 1024
 BF16, F32 = jnp.bfloat16, jnp.float32
 
 
@@ -52,7 +52,7 @@
             jax.ShapeDtypeStruct((ROWS, PAD, CHANNELS), BF16),
         ],
         cost_estimate=pl.CostEstimate(flops=10_000_000, bytes_accessed=5_000_000, transcendentals=0),
-        compiler_params=pltpu.CompilerParams(vmem_limit_bytes=VMEM),
+        compiler_params=pltpu.CompilerParams(vmem_limit_bytes=16 * MIB),
         name="prepare",
     )(taps, act)
 
@@ -134,37 +134,42 @@
             jax.ShapeDtypeStruct((FILTERS, ROWS, PAD, CHANNELS), BF16),
             jax.ShapeDtypeStruct((2, CHANNELS, CHANNELS), BF16),
         ],
-        compiler_params=pltpu.CompilerParams(vmem_limit_bytes=VMEM),
+        compiler_params=pltpu.CompilerParams(vmem_limit_bytes=30 * MIB),
         name="stencil",
     )(place, tiles, own, lon_a, lon_b, lat_a, lat_b, cells)
 
 
-def input_kernel(f, weight, out):
-    cols = out.shape[0]
+SLAB = 32
+
+
+def input_kernel(f, weight, *rest):
+    out = rest[-1]
     total = 0.0
     for k in range(FILTERS):
-        total += jnp.dot(f[k].reshape(ROWS * cols, CHANNELS), weight[k], preferred_element_type=F32)
-    total = total.astype(BF16).reshape(ROWS, cols, CHANNELS)
-    for b in range(cols // 16):
+        total += jnp.dot(f[k].reshape(ROWS * SLAB, CHANNELS), weight[k], preferred_element_type=F32)
+    total = total.astype(BF16).reshape(ROWS, SLAB, CHANNELS)
+    for b in range(SLAB // 16):
         out[b * 16 : (b + 1) * 16] = turned(total[:, b * 16 : (b + 1) * 16])
 
 
-def input_gradient(f, weight):
-    cols = 32
-    flops = 2 * ROWS * PAD * FILTERS * CHANNELS * CHANNELS
+def input_gradient(f, weight, first, count, done=None):
+    flops = 2 * ROWS * SLAB * count * FILTERS * CHANNELS * CHANNELS
+    extra = [] if done is None else [done]
     return pl.pallas_call(
         input_kernel,
-        grid=(PAD // cols,),
+        grid=(count,),
         in_specs=[
-            pl.BlockSpec((FILTERS, ROWS, cols, CHANNELS), lambda i: (0, 0, i, 0)),
+            pl.BlockSpec((FILTERS, ROWS, SLAB, CHANNELS), lambda i: (0, 0, i + first, 0)),
             pl.BlockSpec((FILTERS, CHANNELS, CHANNELS), lambda i: (0, 0, 0)),
-        ],
-        out_specs=pl.BlockSpec((cols, ROWS, CHANNELS), lambda i: (i, 0, 0)),
+            *[pl.BlockSpec(memory_space=pl.ANY) for _ in extra],
+        ],
+        out_specs=pl.BlockSpec((SLAB, ROWS, CHANNELS), lambda i: (i + first, 0, 0)),
         out_shape=jax.ShapeDtypeStruct((COLS, ROWS, CHANNELS), BF16),
-        compiler_params=pltpu.CompilerParams(vmem_limit_bytes=VMEM),
-        cost_estimate=pl.CostEstimate(flops=flops, bytes_accessed=10_000_000, transcendentals=0),
+        input_output_aliases={2: 0} if extra else {},
+        compiler_params=pltpu.CompilerParams(vmem_limit_bytes=20 * MIB),
+        cost_estimate=pl.CostEstimate(flops=flops, bytes_accessed=4_000_000 * count, transcendentals=0),
         name="input_gradient",
-    )(f, weight)
+    )(f, weight, *extra)
 
 
 def own_half_kernel(place, f, cells, got, out):
@@ -186,7 +191,7 @@
             out_specs=pl.BlockSpec(block, lambda i, c: (i, 0, 0)),
         ),
         out_shape=jax.ShapeDtypeStruct((2, CHANNELS, CHANNELS), BF16),
-        compiler_params=pltpu.CompilerParams(vmem_limit_bytes=VMEM),
+        compiler_params=pltpu.CompilerParams(vmem_limit_bytes=20 * MIB),
         name="own_half",
     )(place, f, cells, got)
 
@@ -235,25 +240,59 @@
     return jnp.pad(taps, ((0, 0), (0, 8 - FILTERS), (0, DEPTH - TAPS * SPAN)))
 
 
-def haloes(own, core, odd):
-    start_a = jnp.where(odd == 0, COLS - REACH, 0)
-    start_b = jnp.where(odd == 0, 0, COLS - REACH)
-    lon_a, lon_b = (lax.dynamic_slice_in_dim(own, s, REACH, 0) for s in (start_a, start_b))
-    row_a = jnp.where(core == 0, ROWS - 1, 0)
-    row_b = ROWS - 1 - row_a
-    edges = lambda x: jnp.concatenate([x[:, :1], x[:, ROWS - 1 :]], axis=1)
-    edge_a = lax.ppermute(edges(lon_a), AXES, LON_A)
-    edge_b = lax.ppermute(edges(lon_b), AXES, LON_B)
-    lon_a = lax.ppermute(lon_a, AXES, LON_A)
-    lon_b = lax.ppermute(lon_b, AXES, LON_B)
-    left = jnp.where(odd == 0, edge_b, edge_a)
-    right = jnp.where(odd == 0, edge_a, edge_b)
-    middle = edges(own)
-    rest = jnp.zeros((WIDE - COLS - 2 * REACH, 2, CHANNELS), BF16)
-    wide = jnp.concatenate([left, middle, right, rest])
-    first, last = wide[:, 0], wide[:, 1]
-    lat_a = lax.ppermute(jnp.where(core == 0, last, first), AXES, LAT_A)
-    lat_b = lax.ppermute(jnp.where(core == 0, first, last), AXES, LAT_B)
+def edges_kernel(place, own, slab_a, slab_b, edge_a, edge_b, middle):
+    even = place[1] == 0
+    west, east = own[:REACH], own[COLS - REACH :]
+    slab_a[...] = jnp.where(even, east, west)
+    slab_b[...] = jnp.where(even, west, east)
+    for slab, edge in ((slab_a, edge_a), (slab_b, edge_b)):
+        block = turned(slab[...])
+        edge[0], edge[1] = block[0], block[ROWS - 1]
+    for b in range(PAD // 16):
+        block = own[16 * b : min(16 * (b + 1), COLS)]
+        if block.shape[0] < 16:
+            block = jnp.concatenate([block, jnp.zeros((16 - block.shape[0], ROWS, CHANNELS), BF16)])
+        block = turned(block)
+        middle[0, 16 * b : 16 * (b + 1)] = block[0]
+        middle[1, 16 * b : 16 * (b + 1)] = block[ROWS - 1]
+
+
+def vmem_call(kernel, name, shapes, place, *args):
+    whole = pl.BlockSpec(memory_space=pltpu.VMEM)
+    return pl.pallas_call(
+        kernel,
+        in_specs=[pl.BlockSpec(memory_space=pltpu.SMEM)] + [whole] * len(args),
+        out_specs=[whole] * len(shapes),
+        out_shape=[jax.ShapeDtypeStruct(s, BF16) for s in shapes],
+        compiler_params=pltpu.CompilerParams(vmem_limit_bytes=12 * MIB),
+        name=name,
+    )(place, *args)
+
+
+def widen_kernel(place, middle, got_a, got_b, wide_a, wide_b):
+    even, first = place[1] == 0, place[0] == 0
+    left = jnp.where(even, got_b[...], got_a[...])
+    right = jnp.where(even, got_a[...], got_b[...])
+    for wide, is_last in ((wide_a, first), (wide_b, jnp.logical_not(first))):
+        pick = lambda x: jnp.where(is_last, x[1], x[0])
+        wide[COLS + REACH :] = jnp.zeros((WIDE - COLS - REACH, CHANNELS), BF16)
+        wide[:REACH] = pick(left)
+        wide[REACH : COLS + REACH] = pick(middle)[:COLS]
+        wide[COLS + REACH : COLS + 2 * REACH] = pick(right)
+
+
+def haloes(own, place):
+    slab, edge, wide = (REACH, ROWS, CHANNELS), (2, REACH, CHANNELS), (WIDE, CHANNELS)
+    slab_a, slab_b, edge_a, edge_b, middle = vmem_call(
+        edges_kernel, "edges", [slab, slab, edge, edge, (2, PAD, CHANNELS)], place, own
+    )
+    edge_a = lax.ppermute(edge_a, AXES, LON_A)
+    edge_b = lax.ppermute(edge_b, AXES, LON_B)
+    lon_a = lax.ppermute(slab_a, AXES, LON_A)
+    lon_b = lax.ppermute(slab_b, AXES, LON_B)
+    wide_a, wide_b = vmem_call(widen_kernel, "widen", [wide, wide], place, middle, edge_a, edge_b)
+    lat_a = lax.ppermute(wide_a, AXES, LAT_A)
+    lat_b = lax.ppermute(wide_b, AXES, LAT_B)
     return lon_a, lon_b, lat_a, lat_b
 
 
@@ -268,11 +307,12 @@
     odd = lax.axis_index("zl").astype(jnp.int32)
     place = jnp.stack([core, odd])
     own, act = jnp.swapaxes(cotangent, 0, 1), jnp.swapaxes(activations, 0, 1)
-    around = haloes(own, core, odd)
+    around = haloes(own, place)
     tiles, cells = prepare(reversed_taps(basis, reach, band), act)
     f, send = stencil(place, tiles, own, *around, cells)
     got = lax.ppermute(send, AXES, SIBLING)
-    grad_input = jnp.swapaxes(input_gradient(f, weight), 0, 1)
+    grad_input = input_gradient(f, weight, 0, 2)
+    got, grad_input = lax.optimization_barrier((got, grad_input))
     half = own_half(place, f, cells, got)
     part = lax.optimization_barrier(summed(half.reshape(-1, CHANNELS), 32, BLOCK).astype(BF16))
     others = [lax.ppermute(part, AXES, along_z(m)).astype(F32) for m in (2, 6, 4)]
@@ -283,7 +323,8 @@
     mine = parts.reshape(2, CHANNELS, CHANNELS)
     theirs = lax.ppermute(mine, AXES, SIBLING)
     grad_weight = jnp.where(core == 0, jnp.concatenate([mine, theirs]), jnp.concatenate([theirs, mine]))
-    return grad_input, grad_weight
+    grad_input = input_gradient(f, weight, 2, 1, grad_input)
+    return jnp.swapaxes(grad_input, 0, 1), grad_weight
 
 
 def solution(mesh):

time: 115 us -> 103 us (0.90)
  Pallas kernels: 26.7 us -> 17 us
  waiting for transfers between devices: 9.1 us -> 6.37 us
  blocking collectives: 40.3 us -> 42 us
    pallas_call x1, Pallas kernels: 10.5 us -> 5.98 us  [stencil(): pl.pallas_call(stencil_kernel, grid_spec=pltpu.PrefetchScalarGridSpec(num...]
    pallas_call x1, Pallas kernels: 5.55 us -> 2.59 us  [own_half(): pl.pallas_call(own_half_kernel, grid_spec=pltpu.PrefetchScalarGridSpec(nu...]
    ppermute x2 -> x0, local copies, waits for them, and re-layouts: 2.72 us -> none  [the longest x1 1.84 us: haloes(): lon_b = lax.ppermute(lon_b, AXES, LON_B)]
    unnamed x13 -> x16, local copies, waits for them, and re-layouts: 4.36 us -> 6.93 us
    ppermute x1, waiting for transfers between devices: 2.5 us -> 0.01 us  [on_device(): got = lax.ppermute(send, AXES, SIBLING)]
    pallas_call x1, Pallas kernels: 3.15 us -> 1.07 us  [prepare(): pl.pallas_call(prepare_kernel, grid=(2,), in_specs=[pl.BlockSpec((ROWS //...]
    select_n x1, other arithmetic: 1.64 us -> 3.35 us  [on_device(): jnp.where(core == 0, jnp.concatenate([mine, theirs]), jnp.concatenate([th...]
    concatenate x3 -> x0, other arithmetic: 1.35 us -> none  [the longest x2 1.24 us: haloes(): edges = lambda x: jnp.concatenate([x[:, :1], x[:, ROWS - 1:]], axis=1)]
  transfers between devices with their start and end apart: 11 -> 11, of which waited for: 5 -> 4; matrix products, arithmetic and copies ran while one was open for 6% -> 3% of each run, Pallas kernels for 9% -> 7%
where the time goes in v3:
time: 103 us
  blocking collectives  42 us (41%)
  starting transfers between devices  23.8 us (23%)
  Pallas kernels  17 us (17%)
  local copies, waits for them, and re-layouts  8.05 us (8%)
  waiting for transfers between devices  6.37 us (6%)
  other arithmetic  4.65 us (5%)
    all_to_all x1, blocking collectives, summed(): lax.all_to_all(parts.reshape(groups, -1, CHANNELS), axes, 0, 0, tiled=True)  23.8 us
    all_to_all x1, blocking collectives, on_device(): lax.all_to_all(jnp.broadcast_to(part, (32, *part.shape)), BLOCK, 0, 0, ti...  18.2 us
    unnamed x16, local copies, waits for them, and re-layouts  6.93 us
    pallas_call x1, Pallas kernels, stencil(): pl.pallas_call(stencil_kernel, grid_spec=pltpu.PrefetchScalarGridSpec(num...  5.98 us
    pallas_call x2, Pallas kernels, input_gradient(): pl.pallas_call(input_kernel, grid=(count,), in_specs=[pl.BlockSpec((FILTE...  5.93 us
    ppermute x3, starting transfers between devices, on_device(): lax.ppermute(part, AXES, along_z(m)).astype(F32)  5.74 us
    ppermute x1, starting transfers between devices, haloes(): edge_b = lax.ppermute(edge_b, AXES, LON_B)  5.59 us
    ppermute x1, starting transfers between devices, on_device(): theirs = lax.ppermute(mine, AXES, SIBLING)  4.03 us
  transfers between devices with their start and end apart: 11, of which 4 were waited for; matrix products, arithmetic and copies ran while one was open for 3% of the time, Pallas kernels for 7%

profile of v3, /device:TPU:1, one launch (start us, length us, event | category | flops | bytes accessed | tf_op | source)
XLA Modules:
  0.0 102.7 jit_solution(5412852895691288645)
XLA Ops:
  0.6 0.0 copy-start.6
  0.6 0.1 pad_add_fusion.place
  0.7 0.0 copy-start.3
  0.7 1.4 %copy-done.3 = bf16[16,90,512]{2,0,1:T(8,128)(2,1)S(1)} copy-done((bf16[16,90,512]{2,0,1:T(8,128)(2,1)S(1)}, bf16[16,90,512]{2,0,1:T(8,128)(2,1)}, u32[]{:S(2)}) %copy-start.3) | copy-done | bytes 1474584
  2.1 0.8 edges.1
  2.9 2.6 %collective-permute-start.2 = (bf16[2,16,512]{2,1,0:T(8,128)(2,1)S(1)}, bf16[2,16,512]{2,1,0:T(8,128)(2,1)S(1)}, u32[]{:S(2)}, u32[]{:S(2)}) collective-permute-start(bf16[2,16,512]{2,1,0:T(8,128)(2,1)S(1)} %get-tuple-element.19), channel_id=1, source_target_pairs={{0,1},{1,0},{2,3},{3,2},{4,5},{5,4},{6,7},{7,6},{8,9},{9,8},{10,11... | collective-permute-start | bytes 98312 | tf_op jit(solution)/shard_map/ppermute | solution.py:289
  5.5 5.6 %collective-permute-start.3 = (bf16[2,16,512]{2,1,0:T(8,128)(2,1)S(1)}, bf16[2,16,512]{2,1,0:T(8,128)(2,1)S(1)}, u32[]{:S(2)}, u32[]{:S(2)}) collective-permute-start(bf16[2,16,512]{2,1,0:T(8,128)(2,1)S(1)} %get-tuple-element.20), channel_id=1, source_target_pairs={{0,15},{1,2},{2,1},{3,4},{4,3},{5,6},{6,5},{7,8},{8,7},{9,10},{10,... | collective-permute-start | bytes 98312 | tf_op jit(solution)/shard_map/ppermute | solution.py:290
  11.1 0.0 collective-permute-start
  11.1 1.5 %collective-permute-start.1 = (bf16[16,16,512]{2,1,0:T(8,128)(2,1)S(1)}, bf16[16,16,512]{2,1,0:T(8,128)(2,1)S(1)}, u32[]{:S(2)}, u32[]{:S(2)}) collective-permute-start(bf16[16,16,512]{2,1,0:T(8,128)(2,1)S(1)} %get-tuple-element.17), channel_id=1, source_target_pairs={{0,15},{1,2},{2,1},{3,4},{4,3},{5,6},{6,5},{7,8},{8,7},{9,10},{10,... | collective-permute-start | bytes 786440 | tf_op jit(solution)/shard_map/ppermute | solution.py:292
  12.6 1.3 %copy.33 = bf16[4,3,33,256]{2,3,0,1:T(8,128)(2,1)S(1)} copy(bf16[4,3,33,256]{3,0,2,1:T(4,128)(2,1)} %param.8) | data formatting | bytes 405504 | tf_op args[3]
  13.9 0.0 copy-done.6
  13.9 0.1 broadcast_compare_fusion
  14.0 0.1 broadcast_select_fusion
  14.1 0.0 copy-start.5
  14.1 0.8 slice_bitcast_fusion.2
  14.9 0.8 fusion.8
  15.7 0.0 collective-permute-done.2.got_a
  15.7 0.0 collective-permute-done.3.got_b
  15.7 0.6 widen.1
  16.3 1.9 %collective-permute-start.4 = (bf16[128,512]{1,0:T(8,128)(2,1)S(1)}, bf16[128,512]{1,0:T(8,128)(2,1)S(1)}, u32[]{:S(2)}, u32[]{:S(2)}) collective-permute-start(bf16[128,512]{1,0:T(8,128)(2,1)S(1)} %get-tuple-element.21), channel_id=1, source_target_pairs={{0,16},{1,17},{2,18},{3,19},{4,20},{5,21},{6,22},{7,23},{8,24},{9,... | collective-permute-start | bytes 393224 | tf_op jit(solution)/shard_map/ppermute | solution.py:294
  18.2 2.4 %collective-permute-start.5 = (bf16[128,512]{1,0:T(8,128)(2,1)S(1)}, bf16[128,512]{1,0:T(8,128)(2,1)S(1)}, u32[]{:S(2)}, u32[]{:S(2)}) collective-permute-start(bf16[128,512]{1,0:T(8,128)(2,1)S(1)} %get-tuple-element.22), channel_id=1, source_target_pairs={{0,8},{1,9},{2,10},{3,11},{4,12},{5,13},{6,14},{7,15},{8,0},{9,1},... | collective-permute-start | bytes 393224 | tf_op jit(solution)/shard_map/ppermute | solution.py:295
  20.7 0.1 rev.3
  20.9 0.1 reshape.19
  21.0 0.0 copy-done.5
  21.0 1.1 %prepare.1 = (bf16[16,192,256]{2,1,0:T(8,128)(2,1)S(1)}, bf16[16,96,512]{2,1,0:T(8,128)(2,1)S(1)}) custom-call(f32[16,8,256]{2,1,0:T(8,128)S(1)} %pad_convert_fusion.taps, bf16[90,16,512]{2,1,0:T(8,128)(2,1)S(1)} %bitcast.27), custom_call_target="tpu_custom_call" | custom-call | flops 10000000 | bytes 5000000 | tf_op jit(solution)/shard_map/prepare/pallas_call | solution.py:39
  22.1 0.0 collective-permute-done.4.lat_a
  22.1 3.1 %collective-permute-done.5.lat_b = bf16[128,512]{1,0:T(8,128)(2,1)S(1)} collective-permute-done((bf16[128,512]{1,0:T(8,128)(2,1)S(1)}, bf16[128,512]{1,0:T(8,128)(2,1)S(1)}, u32[]{:S(2)}, u32[]{:S(2)}) %collective-permute-start.5) | collective-permute-done | bytes 131104 | tf_op jit(solution)/shard_map/ppermute | solution.py:295
  25.2 0.0 collective-permute-done.lon_a
  25.2 0.0 collective-permute-done.1.lon_b
  25.2 0.0 copy-start.4
  25.2 1.4 %copy-done.4 = bf16[16,90,512]{2,0,1:T(8,128)(2,1)S(1)} copy-done((bf16[16,90,512]{2,0,1:T(8,128)(2,1)S(1)}, bf16[16,90,512]{2,0,1:T(8,128)(2,1)}, u32[]{:S(2)}) %copy-start.4) | copy-done | bytes 1474584
  26.6 0.0 copy-start.2
  26.6 6.0 %stencil.1 = (bf16[4,16,96,512]{3,2,1,0:T(8,128)(2,1)S(1)}, bf16[2,512,512]{2,1,0:T(8,128)(2,1)S(1)}) custom-call(s32[2]{0:T(128)S(1)} %pad_add_fusion.place, bf16[16,192,256]{2,1,0:T(8,128)(2,1)S(1)} %get-tuple-element.15.tiles, bf16[90,16,512]{2,1,0:T(8,128)(2,1)S(1)} %bitcast.25, bf16[16,16,512]{2,1,0:T(8,128)(2,1)S(1)} %collective-permute-done.lon_a, ...), custom_call_target="tpu_custom_call" | custom-call | tf_op jit(solution)/shard_map/stencil/pallas_call | solution.py:114
  32.6 0.0 copy-start
  32.6 0.1 collective-permute-start.6
  32.7 0.0 copy-done.2
  32.7 3.8 %input_gradient.2.rest_0_ = bf16[90,16,512]{2,1,0:T(8,128)(2,1)} custom-call(bf16[4,16,96,512]{3,2,1,0:T(8,128)(2,1)S(1)} %get-tuple-element.24.f, bf16[4,512,512]{2,1,0:T(8,128)(2,1)S(1)} %copy-done.2), custom_call_target="tpu_custom_call" | custom-call | flops 2147483648 | bytes 8000000 | tf_op jit(solution)/shard_map/input_gradient/pallas_call | solution.py:158
  36.6 0.0 collective-permute-done.6.got
  36.6 0.0 copy-done
  36.6 2.6 %own_half.1 = bf16[2,512,512]{2,1,0:T(8,128)(2,1)S(1)} custom-call(s32[2]{0:T(128)S(1)} %pad_add_fusion.place, bf16[4,16,96,512]{3,2,1,0:T(8,128)(2,1)S(1)} %get-tuple-element.24.f, bf16[16,96,512]{2,1,0:T(8,128)(2,1)S(1)} %get-tuple-element.23.cells, bf16[2,512,512]{2,1,0:T(8,128)(2,1)S(1)} %collective-permute-done.6.got), custom_call_target="tpu_custom_call" | custom-call | tf_op jit(solution)/shard_map/own_half/pallas_call | solution.py:181
  39.2 23.8 %all_to_all.10 = bf16[32,32,512]{2,1,0:T(8,128)(2,1)S(1)} all-to-all(bf16[32,32,512]{2,1,0:T(8,128)(2,1)S(1)} %bitcast.26), channel_id=1, replica_groups=mesh['y'=4,'xh'=2,'core'=2,'xl'=2,'zh'=4,'zl'=2] {'y','xh','xl','zl'}, dimensions={0} | all-to-all | bytes 2097152 | tf_op jit(solution)/shard_map/all_to_all | solution.py:300
  63.0 0.2 reduce_sum.12
  63.1 1.7 %collective-permute-start.9 = (bf16[32,512]{1,0:T(8,128)(2,1)S(1)}, bf16[32,512]{1,0:T(8,128)(2,1)S(1)}, u32[]{:S(2)}, u32[]{:S(2)}) collective-permute-start(bf16[32,512]{1,0:T(8,128)(2,1)S(1)} %reduce_sum.12), channel_id=1, source_target_pairs={{0,4},{1,5},{2,6},{3,7},{4,0},{5,1},{6,2},{7,3},{8,12},{9,13},{10,... | collective-permute-start | bytes 98312 | tf_op jit(solution)/shard_map/ppermute | solution.py:318
  64.9 2.8 %collective-permute-start.8 = (bf16[32,512]{1,0:T(8,128)(2,1)S(1)}, bf16[32,512]{1,0:T(8,128)(2,1)S(1)}, u32[]{:S(2)}, u32[]{:S(2)}) collective-permute-start(bf16[32,512]{1,0:T(8,128)(2,1)S(1)} %reduce_sum.12), channel_id=1, source_target_pairs={{0,6},{1,7},{2,4},{3,5},{4,2},{5,3},{6,0},{7,1},{8,14},{9,15},{10,... | collective-permute-start | bytes 98312 | tf_op jit(solution)/shard_map/ppermute | solution.py:318
  67.7 1.2 %collective-permute-start.7 = (bf16[32,512]{1,0:T(8,128)(2,1)S(1)}, bf16[32,512]{1,0:T(8,128)(2,1)S(1)}, u32[]{:S(2)}, u32[]{:S(2)}) collective-permute-start(bf16[32,512]{1,0:T(8,128)(2,1)S(1)} %reduce_sum.12), channel_id=1, source_target_pairs={{0,2},{1,3},{2,0},{3,1},{4,6},{5,7},{6,4},{7,5},{8,10},{9,11},{10,... | collective-permute-start | bytes 98312 | tf_op jit(solution)/shard_map/ppermute | solution.py:318
  68.9 1.1 %collective-permute-done.9 = bf16[32,512]{1,0:T(8,128)(2,1)S(1)} collective-permute-done((bf16[32,512]{1,0:T(8,128)(2,1)S(1)}, bf16[32,512]{1,0:T(8,128)(2,1)S(1)}, u32[]{:S(2)}, u32[]{:S(2)}) %collective-permute-start.9) | collective-permute-done | bytes 32800 | tf_op jit(solution)/shard_map/ppermute | solution.py:318
  70.0 0.1 collective-permute-done.8
  70.1 2.0 %collective-permute-done.7 = bf16[32,512]{1,0:T(8,128)(2,1)S(1)} collective-permute-done((bf16[32,512]{1,0:T(8,128)(2,1)S(1)}, bf16[32,512]{1,0:T(8,128)(2,1)S(1)}, u32[]{:S(2)}, u32[]{:S(2)}) %collective-permute-start.7) | collective-permute-done | bytes 32800 | tf_op jit(solution)/shard_map/ppermute | solution.py:318
  72.1 0.1 broadcast_in_dim.15
  72.2 18.2 %all_to_all.11 = bf16[32,32,512]{2,1,0:T(8,128)(2,1)S(1)} all-to-all(bf16[32,32,512]{2,1,0:T(8,128)(2,1)S(1)} %broadcast_in_dim.15), channel_id=1, replica_groups=mesh['y'=4,'xh'=2,'core'=2,'xl'=2,'zh'=4,'zl'=2] {'y','xh','xl','zl'}, dimensions={0} | all-to-all | bytes 2097152 | tf_op jit(solution)/shard_map/all_to_all | solution.py:322
  90.4 4.0 %collective-permute-start.10 = (bf16[2,512,512]{2,1,0:T(8,128)(2,1)S(1)}, bf16[2,512,512]{2,1,0:T(8,128)(2,1)}, u32[]{:S(2)}, u32[]{:S(2)}) collective-permute-start(bf16[2,512,512]{2,1,0:T(8,128)(2,1)S(1)} %bitcast.29), channel_id=1, source_target_pairs={{0,16},{1,17},{2,18},{3,19},{4,20},{5,21},{6,22},{7,23},{8,24},{9,... | collective-permute-start | bytes 3145736 | tf_op jit(solution)/shard_map/ppermute | solution.py:324
  94.4 0.0 copy-start.1
  94.4 2.8 %copy-done.1 = bf16[4,16,96,512]{3,2,1,0:T(8,128)(2,1)S(1)} copy-done((bf16[4,16,96,512]{3,2,1,0:T(8,128)(2,1)S(1)}, bf16[4,16,96,512]{3,2,1,0:T(8,128)(2,1)}, u32[]{:S(2)}) %copy-start.1) | copy-done | bytes 6291480
  97.2 2.1 %input_gradient.3 = bf16[90,16,512]{2,1,0:T(8,128)(2,1)} custom-call(bf16[4,16,96,512]{3,2,1,0:T(8,128)(2,1)S(1)} %copy-done.1, bf16[4,512,512]{2,1,0:T(8,128)(2,1)S(1)} %copy-done.2, bf16[90,16,512]{2,1,0:T(8,128)(2,1)} %input_gradient.2.rest_0_), custom_call_target="tpu_custom_call", output_to_operand_aliasing={{}: (2, {})} | custom-call | flops 1073741824 | bytes 4000000 | tf_op jit(solution)/shard_map/input_gradient/pallas_call | solution.py:158
  99.3 0.0 collective-permute-done.10
  99.3 3.4 %maximum_select_fusion = bf16[4,512,512]{2,1,0:T(8,128)(2,1)} fusion(bf16[2,512,512]{2,1,0:T(8,128)(2,1)} %collective-permute-done.10, bf16[2,512,512]{2,1,0:T(8,128)(2,1)S(1)} %bitcast.30, pred[]{:T(512)S(6)} %eq.3), kind=kLoop, calls=%fused_computation | loop fusion | flops 3145728 | bytes 4194305 | tf_op jit(solution)/shard_map/jit(_where)/select_n | solution.py:325
  (8 shorter events, 0.2 us)
Async XLA Ops:
  0.6 13.3 %copy-start.6 = (s32[256]{0:T(256)S(1)}, s32[256]{0:T(256)}, u32[]{:S(2)}) copy-start(s32[256]{0:T(256)} %param.9) | copy-start | bytes 3076
  0.7 1.4 %copy-start.3 = (bf16[16,90,512]{2,0,1:T(8,128)(2,1)S(1)}, bf16[16,90,512]{2,0,1:T(8,128)(2,1)}, u32[]{:S(2)}) copy-start(bf16[16,90,512]{2,0,1:T(8,128)(2,1)} %param.5) | copy-start | bytes 4423684
  2.9 12.8 %collective-permute-start.2 = (bf16[2,16,512]{2,1,0:T(8,128)(2,1)S(1)}, bf16[2,16,512]{2,1,0:T(8,128)(2,1)S(1)}, u32[]{:S(2)}, u32[]{:S(2)}) collective-permute-start(bf16[2,16,512]{2,1,0:T(8,128)(2,1)S(1)} %get-tuple-element.19), channel_id=1, source_target_pairs={{0,1},{1,0},{2,3},{3,2},{4,5},{5,4},{6,7},{7,6},{8,9},{9,8},{10,11... | collective-permute-start | bytes 98312 | tf_op jit(solution)/shard_map/ppermute | solution.py:289
  5.5 10.2 %collective-permute-start.3 = (bf16[2,16,512]{2,1,0:T(8,128)(2,1)S(1)}, bf16[2,16,512]{2,1,0:T(8,128)(2,1)S(1)}, u32[]{:S(2)}, u32[]{:S(2)}) collective-permute-start(bf16[2,16,512]{2,1,0:T(8,128)(2,1)S(1)} %get-tuple-element.20), channel_id=1, source_target_pairs={{0,15},{1,2},{2,1},{3,4},{4,3},{5,6},{6,5},{7,8},{8,7},{9,10},{10,... | collective-permute-start | bytes 98312 | tf_op jit(solution)/shard_map/ppermute | solution.py:290
  11.1 14.1 %collective-permute-start = (bf16[16,16,512]{2,1,0:T(8,128)(2,1)S(1)}, bf16[16,16,512]{2,1,0:T(8,128)(2,1)S(1)}, u32[]{:S(2)}, u32[]{:S(2)}) collective-permute-start(bf16[16,16,512]{2,1,0:T(8,128)(2,1)S(1)} %get-tuple-element.16), channel_id=1, source_target_pairs={{0,1},{1,0},{2,3},{3,2},{4,5},{5,4},{6,7},{7,6},{8,9},{9,8},{10,11... | collective-permute-start | bytes 786440 | tf_op jit(solution)/shard_map/ppermute | solution.py:291
  11.1 14.1 %collective-permute-start.1 = (bf16[16,16,512]{2,1,0:T(8,128)(2,1)S(1)}, bf16[16,16,512]{2,1,0:T(8,128)(2,1)S(1)}, u32[]{:S(2)}, u32[]{:S(2)}) collective-permute-start(bf16[16,16,512]{2,1,0:T(8,128)(2,1)S(1)} %get-tuple-element.17), channel_id=1, source_target_pairs={{0,15},{1,2},{2,1},{3,4},{4,3},{5,6},{6,5},{7,8},{8,7},{9,10},{10,... | collective-permute-start | bytes 786440 | tf_op jit(solution)/shard_map/ppermute | solution.py:292
  14.1 6.9 %copy-start.5 = (bf16[16,90,512]{2,0,1:T(8,128)(2,1)S(1)}, bf16[16,90,512]{2,0,1:T(8,128)(2,1)}, u32[]{:S(2)}) copy-start(bf16[16,90,512]{2,0,1:T(8,128)(2,1)} %param.6) | copy-start | bytes 4423684
  16.3 5.8 %collective-permute-start.4 = (bf16[128,512]{1,0:T(8,128)(2,1)S(1)}, bf16[128,512]{1,0:T(8,128)(2,1)S(1)}, u32[]{:S(2)}, u32[]{:S(2)}) collective-permute-start(bf16[128,512]{1,0:T(8,128)(2,1)S(1)} %get-tuple-element.21), channel_id=1, source_target_pairs={{0,16},{1,17},{2,18},{3,19},{4,20},{5,21},{6,22},{7,23},{8,24},{9,... | collective-permute-start | bytes 393224 | tf_op jit(solution)/shard_map/ppermute | solution.py:294
  18.2 7.0 %collective-permute-start.5 = (bf16[128,512]{1,0:T(8,128)(2,1)S(1)}, bf16[128,512]{1,0:T(8,128)(2,1)S(1)}, u32[]{:S(2)}, u32[]{:S(2)}) collective-permute-start(bf16[128,512]{1,0:T(8,128)(2,1)S(1)} %get-tuple-element.22), channel_id=1, source_target_pairs={{0,8},{1,9},{2,10},{3,11},{4,12},{5,13},{6,14},{7,15},{8,0},{9,1},... | collective-permute-start | bytes 393224 | tf_op jit(solution)/shard_map/ppermute | solution.py:295
  25.2 1.4 %copy-start.4 = (bf16[16,90,512]{2,0,1:T(8,128)(2,1)S(1)}, bf16[16,90,512]{2,0,1:T(8,128)(2,1)}, u32[]{:S(2)}) copy-start(bf16[16,90,512]{2,0,1:T(8,128)(2,1)} %param.5) | copy-start | bytes 4423684
  26.6 6.1 %copy-start.2 = (bf16[4,512,512]{2,1,0:T(8,128)(2,1)S(1)}, bf16[4,512,512]{2,1,0:T(8,128)(2,1)}, u32[]{:S(2)}) copy-start(bf16[4,512,512]{2,1,0:T(8,128)(2,1)} %weight.3) | copy-start | bytes 6291460
  32.6 3.9 %copy-start = (bf16[4,16,96,512]{3,2,1,0:T(8,128)(2,1)}, bf16[4,16,96,512]{3,2,1,0:T(8,128)(2,1)S(1)}, u32[]{:S(2)}) copy-start(bf16[4,16,96,512]{3,2,1,0:T(8,128)(2,1)S(1)} %get-tuple-element.24.f) | copy-start | bytes 18874372
  32.6 3.9 %collective-permute-start.6 = (bf16[2,512,512]{2,1,0:T(8,128)(2,1)S(1)}, bf16[2,512,512]{2,1,0:T(8,128)(2,1)S(1)}, u32[]{:S(2)}, u32[]{:S(2)}) collective-permute-start(bf16[2,512,512]{2,1,0:T(8,128)(2,1)S(1)} %get-tuple-element.25), channel_id=1, source_target_pairs={{0,16},{1,17},{2,18},{3,19},{4,20},{5,21},{6,22},{7,23},{8,24},{9,... | collective-permute-start | bytes 3145736 | tf_op jit(solution)/shard_map/ppermute | solution.py:313
  63.1 6.9 %collective-permute-start.9 = (bf16[32,512]{1,0:T(8,128)(2,1)S(1)}, bf16[32,512]{1,0:T(8,128)(2,1)S(1)}, u32[]{:S(2)}, u32[]{:S(2)}) collective-permute-start(bf16[32,512]{1,0:T(8,128)(2,1)S(1)} %reduce_sum.12), channel_id=1, source_target_pairs={{0,4},{1,5},{2,6},{3,7},{4,0},{5,1},{6,2},{7,3},{8,12},{9,13},{10,... | collective-permute-start | bytes 98312 | tf_op jit(solution)/shard_map/ppermute | solution.py:318
  64.9 5.2 %collective-permute-start.8 = (bf16[32,512]{1,0:T(8,128)(2,1)S(1)}, bf16[32,512]{1,0:T(8,128)(2,1)S(1)}, u32[]{:S(2)}, u32[]{:S(2)}) collective-permute-start(bf16[32,512]{1,0:T(8,128)(2,1)S(1)} %reduce_sum.12), channel_id=1, source_target_pairs={{0,6},{1,7},{2,4},{3,5},{4,2},{5,3},{6,0},{7,1},{8,14},{9,15},{10,... | collective-permute-start | bytes 98312 | tf_op jit(solution)/shard_map/ppermute | solution.py:318
  67.7 4.4 %collective-permute-start.7 = (bf16[32,512]{1,0:T(8,128)(2,1)S(1)}, bf16[32,512]{1,0:T(8,128)(2,1)S(1)}, u32[]{:S(2)}, u32[]{:S(2)}) collective-permute-start(bf16[32,512]{1,0:T(8,128)(2,1)S(1)} %reduce_sum.12), channel_id=1, source_target_pairs={{0,2},{1,3},{2,0},{3,1},{4,6},{5,7},{6,4},{7,5},{8,10},{9,11},{10,... | collective-permute-start | bytes 98312 | tf_op jit(solution)/shard_map/ppermute | solution.py:318
  90.4 8.9 %collective-permute-start.10 = (bf16[2,512,512]{2,1,0:T(8,128)(2,1)S(1)}, bf16[2,512,512]{2,1,0:T(8,128)(2,1)}, u32[]{:S(2)}, u32[]{:S(2)}) collective-permute-start(bf16[2,512,512]{2,1,0:T(8,128)(2,1)S(1)} %bitcast.29), channel_id=1, source_target_pairs={{0,16},{1,17},{2,18},{3,19},{4,20},{5,21},{6,22},{7,23},{8,24},{9,... | collective-permute-start | bytes 3145736 | tf_op jit(solution)/shard_map/ppermute | solution.py:324
  94.4 2.8 %copy-start.1 = (bf16[4,16,96,512]{3,2,1,0:T(8,128)(2,1)S(1)}, bf16[4,16,96,512]{3,2,1,0:T(8,128)(2,1)}, u32[]{:S(2)}) copy-start(bf16[4,16,96,512]{3,2,1,0:T(8,128)(2,1)} %copy-done) | copy-start | bytes 18874372

commit v4 on v2

v4 whole, which is shorter than its diff:
```python
import functools

import jax
import jax.numpy as jnp
from jax import lax
from jax.experimental import pallas as pl
from jax.experimental.pallas import tpu as pltpu
from jax.sharding import Mesh, PartitionSpec as P

ROWS, COLS, REACH = 16, 90, 16
PAD, HALF, SPAN, WIDE = 96, 48, 80, 128
DEPTH = 256
CHANNELS, FILTERS, TAPS = 512, 4, 3
AXES = ("y", "xh", "core", "xl", "zh", "zl")
BLOCK = ("y", "xh", "xl", "zl")
LAT, LON = 16, 16
MIB = 1024 * 1024
BF16, F32 = jnp.bfloat16, jnp.float32


def turned(block):
    return jnp.swapaxes(block, 0, 1)


def local(kernel, name, shapes, inputs, scratch=(), spaces=None, aliases=None, mib=16, cost=None):
    spaces = spaces or {}
    spec = lambda i: pl.BlockSpec(memory_space=spaces.get(i, pltpu.VMEM))
    n = len(inputs)
    return pl.pallas_call(
        kernel,
        in_specs=[pl.BlockSpec(memory_space=pltpu.SMEM)] + [spec(i) for i in range(1, n)],
        out_specs=[spec(n + i) for i in range(len(shapes))],
        out_shape=[jax.ShapeDtypeStruct(shape, BF16) for shape in shapes],
        scratch_shapes=list(scratch),
        input_output_aliases=aliases or {},
        compiler_params=pltpu.CompilerParams(vmem_limit_bytes=mib * MIB),
        cost_estimate=cost and pl.CostEstimate(flops=cost, bytes_accessed=2_000_000, transcendentals=0),
        name=name,
    )(*inputs)


def edges_kernel(place, own, slab_a, slab_b, edge_a, edge_b, sides, sems):
    copies = [
        pltpu.make_async_copy(own.at[pl.ds(start, REACH)], sides.at[i], sems.at[i]) for i, start in enumerate((0, COLS - REACH))
    ]
    for copy in copies:
        copy.start()
    for copy in copies:
        copy.wait()
    even = place[1] == 0
    slab_a[...] = jnp.where(even, sides[1], sides[0])
    slab_b[...] = jnp.where(even, sides[0], sides[1])
    for slab, edge in ((slab_a, edge_a), (slab_b, edge_b)):
        block = turned(slab[...])
        edge[0], edge[1] = block[0], block[ROWS - 1]


def chunks():
    return [(b, 16 * b, min(16, COLS - 16 * b)) for b in range(PAD // 16)]


def fetches(source, target, sems):
    copies = [
        pltpu.make_async_copy(source.at[pl.ds(left, n)], target.at[pl.ds(left, n)], sems.at[b]) for b, left, n in chunks()
    ]
    for copy in copies:
        copy.start()
    return copies


def turned_chunk(block):
    if block.shape[0] < 16:
        block = jnp.concatenate([block, jnp.zeros((16 - block.shape[0], ROWS, CHANNELS), BF16)])
    return turned(block)


def turn_kernel(place, own, rows, middle, buffer, sems):
    copies = fetches(own, buffer, sems)
    for b, left, n in chunks():
        copies[b].wait()
        block = turned_chunk(buffer[left : left + n])
        rows[:, left : left + 16, :] = block
        middle[0, left : left + 16] = block[0]
        middle[1, left : left + 16] = block[ROWS - 1]


def widen_kernel(place, middle, got_a, got_b, wide_a, wide_b):
    even, first = place[1] == 0, place[0] == 0
    left = jnp.where(even, got_b[...], got_a[...])
    right = jnp.where(even, got_a[...], got_b[...])
    for wide, is_last in ((wide_a, first), (wide_b, jnp.logical_not(first))):
        pick = lambda x: jnp.where(is_last, x[1], x[0])
        wide[COLS + REACH :] = jnp.zeros((WIDE - COLS - REACH, CHANNELS), BF16)
        wide[:REACH] = pick(left)
        wide[REACH : COLS + REACH] = pick(middle)[:COLS]
        wide[COLS + REACH : COLS + 2 * REACH] = pick(right)


LEAD = 8


def prepare_kernel(place, basis, reach, act, tiles, cells, placed, buffer, sems):
    copies = fetches(act, buffer, sems)
    length = basis.shape[1]
    lats = basis.shape[2]
    offset = lax.broadcasted_iota(jnp.int32, (length, lats), 0) // FILTERS
    inside = jnp.abs(offset - REACH) <= reach[...]
    row = lax.broadcasted_iota(jnp.int32, (length, FILTERS * DEPTH), 0)
    col = lax.broadcasted_iota(jnp.int32, (length, FILTERS * DEPTH), 1)
    gap = jnp.where(row % FILTERS == col // DEPTH, col % DEPTH + row // FILTERS - 2 * REACH, -1)

    def put(t, q, lat):
        taps = jnp.where(inside, basis[t].astype(F32), 0.0)[:, lat].astype(BF16)
        ones = jnp.where(gap == SPAN * q, 1.0, 0.0).astype(BF16)
        return lax.dot_general(taps, ones, (((0,), (0,)), ((), ())), preferred_element_type=F32)

    for q in range(TAPS):
        placed[q, LEAD : LEAD + lats, :] = put(TAPS - 1 - q, q, slice(None))
    placed[0, LEAD - 1 : LEAD, :] = put(0, 0, slice(0, 128))[:1]
    placed[2, LEAD + lats : LEAD + lats + 1, :] = put(2, 2, slice(lats - 128, lats))[127:]
    start = place[2] * ROWS + LEAD - 1
    for r in range(ROWS):
        for k in range(FILTERS):
            lanes = pl.ds(k * DEPTH, DEPTH)
            taps = [placed[q, pl.ds(start + r + q, 1), lanes] for q in range(TAPS)]
            band = jnp.broadcast_to(taps[0] + taps[1] + taps[2], (HALF, DEPTH))
            tiles[r, k * HALF : (k + 1) * HALF, :] = pltpu.roll(band, 0, 1, stride=1, stride_axis=0).astype(BF16)
    for b, left, n in chunks():
        copies[b].wait()
        cells[:, left : left + 16, :] = turned_chunk(buffer[left : left + n])


GROUP = 4
STEPS = ROWS // GROUP


def outer(f, cells):
    f = f.reshape(ROWS * PAD, CHANNELS)
    cells = cells.reshape(ROWS * PAD, CHANNELS)
    return lax.dot_general(f, cells, (((0,), (0,)), ((), ())), preferred_element_type=F32)


def stencil_kernel(place, tiles, rows, lon_a, lon_b, lat_a, lat_b, cells_ref, f_out, send, low, high, held, cells, sem, f_sems):
    step = pl.program_id(0)
    stores = [
        pltpu.make_async_copy(held.at[:, pl.ds(GROUP * i, GROUP)], f_out.at[:, pl.ds(GROUP * i, GROUP)], f_sems.at[i])
        for i in range(STEPS)
    ]
    copy = pltpu.make_async_copy(cells_ref, cells, sem)

    @pl.when(step == 0)
    def _():
        copy.start()
        even, first = place[1] == 0, place[0] == 0
        inner = slice(1, ROWS + 1)
        low[inner, :REACH, :] = turned(jnp.where(even, lon_b[...], lon_a[...]))
        low[inner, REACH:, :] = rows[:, : SPAN - REACH, :]
        high[inner, : PAD - 32, :] = rows[:, 32:PAD, :]
        high[inner, PAD - 32 :, :] = jnp.zeros((ROWS, SPAN + 32 - PAD, CHANNELS), BF16)
        right = turned(jnp.where(even, lon_a[...], lon_b[...]))
        for r in range(ROWS):
            high[r + 1, COLS - 32 : COLS - 32 + REACH, :] = right[r]
        before = jnp.where(first, lat_b[...], lat_a[...])
        after = jnp.where(first, lat_a[...], lat_b[...])
        low[0], low[ROWS + 1] = before[:SPAN], after[:SPAN]
        high[0], high[ROWS + 1] = before[HALF:], after[HALF:]

    @pl.when(step < STEPS)
    def _():
        rest = jnp.zeros((DEPTH - TAPS * SPAN, CHANNELS), BF16)
        for j in range(GROUP):
            r = step * GROUP + j
            for h, source in enumerate((low, high)):
                taken = source[pl.ds(r, TAPS)].reshape(TAPS * SPAN, CHANNELS)
                taken = jnp.concatenate([taken, rest])
                f = jnp.dot(tiles[j], taken, preferred_element_type=F32).astype(BF16)
                f = f.reshape(FILTERS, HALF, CHANNELS)
                held[:, r, h * HALF : (h + 1) * HALF, :] = f

    for i, store in enumerate(stores):
        pl.when(step == i)(store.start)

    @pl.when(step == STEPS)
    def _():
        copy.wait()

    @pl.when(step >= STEPS)
    def _():
        k = 2 * (1 - place[0]) + step - STEPS
        send[0] = outer(held[k], cells[...]).astype(BF16)

    @pl.when(step == STEPS + 1)
    def _():
        for store in stores:
            store.wait()


def stencil(place, tiles, rows, lon_a, lon_b, lat_a, lat_b, cells):
    whole = lambda a: pl.BlockSpec(a.shape, lambda i, c: (0,) * a.ndim)
    return pl.pallas_call(
        stencil_kernel,
        grid_spec=pltpu.PrefetchScalarGridSpec(
            num_scalar_prefetch=1,
            grid=(STEPS + 2,),
            in_specs=[
                pl.BlockSpec((GROUP, FILTERS * HALF, DEPTH), lambda i, c: (jnp.minimum(i, STEPS - 1), 0, 0)),
                *[whole(a) for a in (rows, lon_a, lon_b, lat_a, lat_b)],
                pl.BlockSpec(memory_space=pl.ANY),
            ],
            out_specs=[
                pl.BlockSpec(memory_space=pltpu.HBM),
                pl.BlockSpec((1, CHANNELS, CHANNELS), lambda i, c: (jnp.maximum(i - STEPS, 0), 0, 0)),
            ],
            scratch_shapes=[
                pltpu.VMEM((ROWS + 2, SPAN, CHANNELS), BF16),
                pltpu.VMEM((ROWS + 2, SPAN, CHANNELS), BF16),
                pltpu.VMEM((FILTERS, ROWS, PAD, CHANNELS), BF16),
                pltpu.VMEM((ROWS, PAD, CHANNELS), BF16),
                pltpu.SemaphoreType.DMA(()),
                pltpu.SemaphoreType.DMA((STEPS,)),
            ],
        ),
        out_shape=[
            jax.ShapeDtypeStruct((FILTERS, ROWS, PAD, CHANNELS), BF16),
            jax.ShapeDtypeStruct((2, CHANNELS, CHANNELS), BF16),
        ],
        compiler_params=pltpu.CompilerParams(vmem_limit_bytes=30 * MIB),
        name="stencil",
    )(place, tiles, rows, lon_a, lon_b, lat_a, lat_b, cells)


SLAB = 32
SLABS = PAD // SLAB


def remainder_kernel(place, f_hbm, weight_hbm, cells_ref, out, mine, weight, f, cells, stage, weight_sems, f_sems, cells_sem, out_sems):
    loads = [pltpu.make_async_copy(weight_hbm.at[k], weight.at[k], weight_sems.at[k]) for k in range(FILTERS)]
    slabs = [
        [
            pltpu.make_async_copy(f_hbm.at[k, :, pl.ds(SLAB * j, SLAB)], f.at[k, :, pl.ds(SLAB * j, SLAB)], f_sems.at[j, k])
            for k in range(FILTERS)
        ]
        for j in range(SLABS)
    ]
    cells_copy = pltpu.make_async_copy(cells_ref, cells, cells_sem)
    for k in range(FILTERS):
        slabs[0][k].start()
        loads[k].start()
    for slab in slabs[1:]:
        for copy in slab:
            copy.start()
    cells_copy.start()
    stores = []
    for j in range(SLABS):
        left = SLAB * j
        cols = min(SLAB, COLS - left)
        total = 0.0
        for k in range(FILTERS):
            slabs[j][k].wait()
            if j == 0:
                loads[k].wait()
            taken = f[k, :, left : left + SLAB, :].reshape(ROWS * SLAB, CHANNELS)
            total += jnp.dot(taken, weight[k], preferred_element_type=F32)
        total = total.astype(BF16).reshape(ROWS, SLAB, CHANNELS)
        for b in range(SLAB // 16):
            stage[j, 16 * b : 16 * (b + 1)] = turned(total[:, 16 * b : 16 * (b + 1)])
        store = pltpu.make_async_copy(stage.at[j, pl.ds(0, cols)], out.at[pl.ds(left, cols)], out_sems.at[j])
        store.start()
        stores.append(store)
    cells_copy.wait()
    for j in range(2):
        mine[j] = outer(f[2 * place[0] + j], cells[...])
    for store in stores:
        store.wait()


def remainder(place, f, weight, cells):
    filtered = (FILTERS, ROWS, PAD, CHANNELS)
    half = (2, CHANNELS, CHANNELS)
    spec = lambda space: pl.BlockSpec(memory_space=space)
    flops = 2 * ROWS * PAD * (FILTERS + 2) * CHANNELS * CHANNELS
    return pl.pallas_call(
        remainder_kernel,
        in_specs=[spec(pltpu.SMEM), spec(pltpu.HBM), spec(pltpu.HBM), spec(pl.ANY)],
        out_specs=[spec(pl.ANY), spec(pltpu.VMEM)],
        out_shape=[jax.ShapeDtypeStruct((COLS, ROWS, CHANNELS), BF16), jax.ShapeDtypeStruct(half, F32)],
        scratch_shapes=[
            pltpu.VMEM((FILTERS, CHANNELS, CHANNELS), BF16),
            pltpu.VMEM(filtered, BF16),
            pltpu.VMEM((ROWS, PAD, CHANNELS), BF16),
            pltpu.VMEM((SLABS, SLAB, ROWS, CHANNELS), BF16),
            pltpu.SemaphoreType.DMA((FILTERS,)),
            pltpu.SemaphoreType.DMA((SLABS, FILTERS)),
            pltpu.SemaphoreType.DMA(()),
            pltpu.SemaphoreType.DMA((SLABS,)),
        ],
        compiler_params=pltpu.CompilerParams(vmem_limit_bytes=24 * MIB),
        cost_estimate=pl.CostEstimate(flops=flops, bytes_accessed=12_000_000, transcendentals=0),
        name="remainder",
    )(place, f, weight, cells)


def put_half_kernel(flip, place, half, *rest):
    out, sems = rest[-2:]
    start = 2 * (1 - place[0] if flip else place[0])
    part = CHANNELS // 4
    copies = [
        pltpu.make_async_copy(half.at[:, pl.ds(i * part, part)], out.at[pl.ds(start, 2), pl.ds(i * part, part)], sems.at[i])
        for i in range(4)
    ]
    for copy in copies:
        copy.start()
    for copy in copies:
        copy.wait()


def put_half(place, half, flip, done=()):
    inputs = [place, half, *done]
    spaces = {i: pl.ANY for i in range(1, len(inputs) + 1)}
    return local(
        functools.partial(put_half_kernel, flip), "put_half", [(FILTERS, CHANNELS, CHANNELS)], inputs,
        [pltpu.SemaphoreType.DMA((4,))], spaces, {2: 0} if done else {},
    )


def device(lat, lon):
    return lat * LON + lon % LON


def route(target):
    return [(device(a, b), device(*target(a, b))) for a in range(LAT) for b in range(LON)]


def lat_b_partner(a, b):
    if a in (0, LAT - 1):
        return a, b + LON // 2
    return (a + 1 if a % 2 else a - 1), b


LON_A = route(lambda a, b: (a, b ^ 1))
LON_B = route(lambda a, b: (a, b + 1 if b % 2 else b - 1))
LAT_A = route(lambda a, b: (a ^ 1, b))
LAT_B = route(lat_b_partner)
SIBLING = LAT_A


def along_z(mask):
    return route(lambda a, b: (a, b ^ mask))


def haloes(own, place):
    slab, edge, wide = (REACH, ROWS, CHANNELS), (2, REACH, CHANNELS), (WIDE, CHANNELS)
    slab_a, slab_b, edge_a, edge_b = local(
        edges_kernel, "edges", [slab, slab, edge, edge], [place, own],
        [pltpu.VMEM((2, *slab), BF16), pltpu.SemaphoreType.DMA((2,))], {1: pltpu.HBM},
    )
    own, edge_a, edge_b = lax.optimization_barrier((own, edge_a, edge_b))
    edge_a = lax.ppermute(edge_a, AXES, LON_A)
    edge_b = lax.ppermute(edge_b, AXES, LON_B)
    lon_a = lax.ppermute(slab_a, AXES, LON_A)
    lon_b = lax.ppermute(slab_b, AXES, LON_B)
    rows, middle = local(
        turn_kernel, "turn", [(ROWS, PAD, CHANNELS), (2, PAD, CHANNELS)], [place, own],
        [pltpu.VMEM(own.shape, BF16), pltpu.SemaphoreType.DMA((PAD // 16,))], {1: pltpu.HBM},
    )
    wide_a, wide_b = local(widen_kernel, "widen", [wide, wide], [place, middle, edge_a, edge_b])
    return rows, lon_a, lon_b, wide_a, wide_b


def prepared(place, basis, reach, act):
    taps, lats = basis.shape[2] * FILTERS, basis.shape[3]
    basis = jnp.transpose(basis, (1, 2, 0, 3)).reshape(TAPS, taps, lats)
    scratch = [
        pltpu.VMEM((TAPS, lats + 2 * LEAD, FILTERS * DEPTH), F32),
        pltpu.VMEM(act.shape, BF16),
        pltpu.SemaphoreType.DMA((PAD // 16,)),
    ]
    shapes = [(ROWS, FILTERS * HALF, DEPTH), (ROWS, PAD, CHANNELS)]
    inputs = [place, basis, reach.reshape(1, lats), act]
    return local(prepare_kernel, "prepare", shapes, inputs, scratch, {3: pltpu.HBM}, cost=100_000_000)


def summed(parts, groups, axes):
    parts = lax.all_to_all(parts.reshape(groups, -1, CHANNELS), axes, 0, 0, tiled=True)
    return jnp.sum(parts.astype(F32), axis=0)


def on_device(cotangent, activations, weight, basis, reach):
    band = lax.axis_index(("y", "xh", "core")).astype(jnp.int32)
    core = lax.axis_index("core").astype(jnp.int32)
    odd = lax.axis_index("zl").astype(jnp.int32)
    place = jnp.stack([core, odd, band])
    own, act = jnp.swapaxes(cotangent, 0, 1), jnp.swapaxes(activations, 0, 1)
    rows, lon_a, lon_b, wide_a, wide_b = haloes(own, place)
    act, wide_a, wide_b = lax.optimization_barrier((act, wide_a, wide_b))
    lat_a = lax.ppermute(wide_a, AXES, LAT_A)
    lat_b = lax.ppermute(wide_b, AXES, LAT_B)
    tiles, cells = prepared(place, basis, reach, act)
    f, send = stencil(place, tiles, rows, lon_a, lon_b, lat_a, lat_b, cells)
    got = lax.ppermute(send, AXES, SIBLING)
    grad_input, mine = remainder(place, f, weight, cells)
    got, mine = lax.optimization_barrier((got, mine))
    half = (mine + got.astype(F32)).astype(BF16)
    part = lax.optimization_barrier(summed(half.reshape(-1, CHANNELS), 32, BLOCK).astype(BF16))
    others = [lax.ppermute(part, AXES, along_z(m)).astype(F32) for m in (2, 6, 4)]
    norm_factor = float(ROWS * COLS * LAT * LON) ** (-0.5)
    part = (part.astype(F32) + others[0]) + (others[1] + others[2])
    part = (part * norm_factor).astype(BF16)
    parts = lax.all_to_all(jnp.broadcast_to(part, (32, *part.shape)), BLOCK, 0, 0, tiled=True)
    mine = parts.reshape(2, CHANNELS, CHANNELS)
    theirs = lax.ppermute(mine, AXES, SIBLING)
    grad_weight = put_half(place, mine, False)
    (grad_weight,) = put_half(place, theirs, True, grad_weight)
    return jnp.swapaxes(grad_input, 0, 1), grad_weight


def solution(mesh):
    finer = Mesh(mesh.devices.reshape(4, 2, 2, 2, 4, 2), AXES)
    cells = P(("y", "xh", "core"), ("xl", "zh", "zl"), None)
    return jax.shard_map(
        on_device, mesh=finer, in_specs=(cells, cells, P(), P(), P()), out_specs=(cells, P()), check_vma=False
    )
```

time: 115 us -> 104 us (0.904)
  local copies, waits for them, and re-layouts: 7.8 us -> 2.48 us
  other arithmetic: 5.6 us -> 0.61 us
  blocking collectives: 40.3 us -> 42.5 us
  Pallas kernels: 26.7 us -> 24.6 us
    pallas_call x1, Pallas kernels: 10.5 us -> 7.13 us  [stencil(): pl.pallas_call(stencil_kernel, grid_spec=pltpu.PrefetchScalarGridSpec(num...]
    unnamed x13 -> x8, local copies, waits for them, and re-layouts: 4.36 us -> 1.39 us
    ppermute x2 -> x0, local copies, waits for them, and re-layouts: 2.72 us -> none  [the longest x1 1.84 us: haloes(): lon_b = lax.ppermute(lon_b, AXES, LON_B)]
    select_n x4 -> x0, other arithmetic: 2.51 us -> none  [the longest x1 1.64 us: on_device(): jnp.where(core == 0, jnp.concatenate([mine, theirs]), jnp.concatenate([th...]
    ppermute x1, waiting for transfers between devices: 2.5 us -> 0.01 us  [on_device(): got = lax.ppermute(send, AXES, SIBLING)]
    ppermute x6, waiting for transfers between devices: 3.85 us -> 5.35 us  [the longest x1 3.56 us: haloes(): edge_b = lax.ppermute(edge_b, AXES, LON_B)]
    concatenate x3 -> x0, other arithmetic: 1.35 us -> none  [the longest x2 1.24 us: haloes(): edges = lambda x: jnp.concatenate([x[:, :1], x[:, ROWS - 1:]], axis=1)]
    pallas_call x3 -> x7, Pallas kernels: 16.2 us -> 17.4 us  [the longest x6 9.63 us: local(): pl.pallas_call(kernel, in_specs=[pl.BlockSpec(memory_space=pltpu.SMEM)] +...]
  transfers between devices with their start and end apart: 11 -> 11, of which waited for: 5 -> 7; matrix products, arithmetic and copies ran while one was open for 6% -> 1% of each run, Pallas kernels for 9% -> 14%
where the time goes in v4:
time: 104 us; the launch traced here: 103 us
  blocking collectives  42.5 us (41%)
  Pallas kernels  24.6 us (24%)
  starting transfers between devices  23.6 us (23%)
  waiting for transfers between devices  8.75 us (8%)
  local copies, waits for them, and re-layouts  2.48 us (2%)
    all_to_all x1, blocking collectives, summed(): lax.all_to_all(parts.reshape(groups, -1, CHANNELS), axes, 0, 0, tiled=True)  23.7 us
    all_to_all x1, blocking collectives, on_device(): lax.all_to_all(jnp.broadcast_to(part, (32, *part.shape)), BLOCK, 0, 0, ti...  18.7 us
    pallas_call x6, Pallas kernels, local(): pl.pallas_call(kernel, in_specs=[pl.BlockSpec(memory_space=pltpu.SMEM)] +...  9.63 us
    pallas_call x1, Pallas kernels, remainder(): pl.pallas_call(remainder_kernel, in_specs=[spec(pltpu.SMEM), spec(pltpu.H...  7.81 us
    pallas_call x1, Pallas kernels, stencil(): pl.pallas_call(stencil_kernel, grid_spec=pltpu.PrefetchScalarGridSpec(num...  7.13 us
    ppermute x3, starting transfers between devices, on_device(): lax.ppermute(part, AXES, along_z(m)).astype(F32)  6.02 us
    ppermute x1, starting transfers between devices, haloes(): lon_b = lax.ppermute(slab_b, AXES, LON_B)  5.59 us
    ppermute x1, starting transfers between devices, on_device(): theirs = lax.ppermute(mine, AXES, SIBLING)  3.89 us
  transfers between devices with their start and end apart: 11, of which 7 were waited for; matrix products, arithmetic and copies ran while one was open for 1% of the time, Pallas kernels for 14%

profile of v4, /device:TPU:1, one launch (start us, length us, event | category | flops | bytes accessed | tf_op | source)
XLA Modules:
  0.0 103.4 jit_solution(259597489342727626)
XLA Ops:
  0.6 0.0 copy-start.2
  0.6 0.1 pad_add_fusion.place
  0.7 0.0 copy-start
  0.7 1.4 %copy-done = bf16[16,90,512]{2,0,1:T(8,128)(2,1)S(1)} copy-done((bf16[16,90,512]{2,0,1:T(8,128)(2,1)S(1)}, bf16[16,90,512]{2,0,1:T(8,128)(2,1)}, u32[]{:S(2)}) %copy-start) | copy-done | bytes 1474584
  2.1 0.0 copy-start.1
  2.1 1.4 %edges.1 = (bf16[16,16,512]{2,1,0:T(8,128)(2,1)}, bf16[16,16,512]{2,1,0:T(8,128)(2,1)}, bf16[2,16,512]{2,1,0:T(8,128)(2,1)S(1)}, bf16[2,16,512]{2,1,0:T(8,128)(2,1)S(1)}) custom-call(s32[3]{0:T(128)S(1)} %pad_add_fusion.place, bf16[90,16,512]{2,1,0:T(8,128)(2,1)S(1)} %bitcast.10), custom_call_target="tpu_custom_call" | custom-call | tf_op jit(solution)/shard_map/edges/pallas_call | solution.py:29
  3.6 2.6 %collective-permute-start.2 = (bf16[16,16,512]{2,1,0:T(8,128)(2,1)}, bf16[16,16,512]{2,1,0:T(8,128)(2,1)S(1)}, u32[]{:S(2)}, u32[]{:S(2)}) collective-permute-start(bf16[16,16,512]{2,1,0:T(8,128)(2,1)} %get-tuple-element.35), channel_id=1, source_target_pairs={{0,1},{1,0},{2,3},{3,2},{4,5},{5,4},{6,7},{7,6},{8,9},{9,8},{10,11... | collective-permute-start | bytes 786440 | tf_op jit(solution)/shard_map/ppermute | solution.py:360
  6.1 5.6 %collective-permute-start.3 = (bf16[16,16,512]{2,1,0:T(8,128)(2,1)}, bf16[16,16,512]{2,1,0:T(8,128)(2,1)}, u32[]{:S(2)}, u32[]{:S(2)}) collective-permute-start(bf16[16,16,512]{2,1,0:T(8,128)(2,1)} %get-tuple-element.36), channel_id=1, source_target_pairs={{0,15},{1,2},{2,1},{3,4},{4,3},{5,6},{6,5},{7,8},{8,7},{9,10},{10,... | collective-permute-start | bytes 786440 | tf_op jit(solution)/shard_map/ppermute | solution.py:361
  11.7 0.0 collective-permute-start
  11.7 1.5 %collective-permute-start.1 = (bf16[2,16,512]{2,1,0:T(8,128)(2,1)S(1)}, bf16[2,16,512]{2,1,0:T(8,128)(2,1)S(1)}, u32[]{:S(2)}, u32[]{:S(2)}) collective-permute-start(bf16[2,16,512]{2,1,0:T(8,128)(2,1)S(1)} %get-tuple-element.29), channel_id=1, source_target_pairs={{0,15},{1,2},{2,1},{3,4},{4,3},{5,6},{6,5},{7,8},{8,7},{9,10},{10,... | collective-permute-start | bytes 98312 | tf_op jit(solution)/shard_map/ppermute | solution.py:359
  13.2 1.3 %turn.1 = (bf16[16,96,512]{2,1,0:T(8,128)(2,1)S(1)}, bf16[2,96,512]{2,1,0:T(8,128)(2,1)S(1)}) custom-call(s32[3]{0:T(128)S(1)} %pad_add_fusion.place, bf16[90,16,512]{2,1,0:T(8,128)(2,1)S(1)} %bitcast.11), custom_call_target="tpu_custom_call" | custom-call | tf_op jit(solution)/shard_map/turn/pallas_call | solution.py:29
  14.5 0.4 collective-permute-done.got_a
  14.9 3.6 %collective-permute-done.1.got_b = bf16[2,16,512]{2,1,0:T(8,128)(2,1)S(1)} collective-permute-done((bf16[2,16,512]{2,1,0:T(8,128)(2,1)S(1)}, bf16[2,16,512]{2,1,0:T(8,128)(2,1)S(1)}, u32[]{:S(2)}, u32[]{:S(2)}) %collective-permute-start.1) | collective-permute-done | bytes 32800 | tf_op jit(solution)/shard_map/ppermute | solution.py:359
  18.4 1.3 %widen.1 = (bf16[128,512]{1,0:T(8,128)(2,1)}, bf16[128,512]{1,0:T(8,128)(2,1)}) custom-call(s32[3]{0:T(128)S(1)} %pad_add_fusion.place, bf16[2,96,512]{2,1,0:T(8,128)(2,1)S(1)} %get-tuple-element.27.middle, bf16[2,16,512]{2,1,0:T(8,128)(2,1)S(1)} %collective-permute-done.got_a, bf16[2,16,512]{2,1,0:T(8,128)(2,1)S(1)} %collective-permute-done.1.got_b), custom_call_target="tpu_custom_call" | custom-call | tf_op jit(solution)/shard_map/widen/pallas_call | solution.py:29
  19.7 1.4 %collective-permute-start.4 = (bf16[128,512]{1,0:T(8,128)(2,1)}, bf16[128,512]{1,0:T(8,128)(2,1)}, u32[]{:S(2)}, u32[]{:S(2)}) collective-permute-start(bf16[128,512]{1,0:T(8,128)(2,1)} %get-tuple-element.37), channel_id=1, source_target_pairs={{0,16},{1,17},{2,18},{3,19},{4,20},{5,21},{6,22},{7,23},{8,24},{9,... | collective-permute-start | bytes 393224 | tf_op jit(solution)/shard_map/ppermute | solution.py:396
  21.1 2.3 %collective-permute-start.5 = (bf16[128,512]{1,0:T(8,128)(2,1)}, bf16[128,512]{1,0:T(8,128)(2,1)}, u32[]{:S(2)}, u32[]{:S(2)}) collective-permute-start(bf16[128,512]{1,0:T(8,128)(2,1)} %get-tuple-element.38), channel_id=1, source_target_pairs={{0,8},{1,9},{2,10},{3,11},{4,12},{5,13},{6,14},{7,15},{8,0},{9,1},... | collective-permute-start | bytes 393224 | tf_op jit(solution)/shard_map/ppermute | solution.py:397
  23.5 1.0 reshape.13.basis
  24.5 0.0 copy-done.2
  24.5 0.0 copy-done.1
  24.5 2.6 %prepare.1 = (bf16[16,192,256]{2,1,0:T(8,128)(2,1)S(1)}, bf16[16,96,512]{2,1,0:T(8,128)(2,1)S(1)}) custom-call(s32[3]{0:T(128)S(1)} %pad_add_fusion.place, bf16[3,132,256]{2,1,0:T(8,128)(2,1)S(1)} %reshape.13.basis, s32[1,256]{1,0:T(1,128)S(1)} %bitcast.15, bf16[90,16,512]{2,1,0:T(8,128)(2,1)S(1)} %bitcast.14), custom_call_target="tpu_custom_call" | custom-call | flops 100000000 | bytes 2000000 | tf_op jit(solution)/shard_map/prepare/pallas_call | solution.py:29
  27.1 0.0 collective-permute-done.4.lat_a
  27.1 1.4 %collective-permute-done.5.lat_b = bf16[128,512]{1,0:T(8,128)(2,1)} collective-permute-done((bf16[128,512]{1,0:T(8,128)(2,1)}, bf16[128,512]{1,0:T(8,128)(2,1)}, u32[]{:S(2)}, u32[]{:S(2)}) %collective-permute-start.5) | collective-permute-done | bytes 131104 | tf_op jit(solution)/shard_map/ppermute | solution.py:397
  28.4 0.0 collective-permute-done.2.lon_a
  28.4 0.0 collective-permute-done.3.lon_b
  28.4 0.0 copy-start.3
  28.4 7.1 %stencil.1 = (bf16[4,16,96,512]{3,2,1,0:T(8,128)(2,1)S(1)}, bf16[2,512,512]{2,1,0:T(8,128)(2,1)S(1)}) custom-call(s32[3]{0:T(128)S(1)} %pad_add_fusion.place, bf16[16,192,256]{2,1,0:T(8,128)(2,1)S(1)} %get-tuple-element.33.tiles, bf16[16,96,512]{2,1,0:T(8,128)(2,1)S(1)} %get-tuple-element.34.rows, bf16[16,16,512]{2,1,0:T(8,128)(2,1)S(1)} %collective-permute-done.2.lon_a, ...), custom_call_target="tpu_custom_call" | custom-call | tf_op jit(solution)/shard_map/stencil/pallas_call | solution.py:200
  35.6 0.3 collective-permute-start.6
  35.9 0.0 copy-done.3
  35.9 7.8 %remainder.1 = (bf16[90,16,512]{2,1,0:T(8,128)(2,1)}, f32[2,512,512]{2,1,0:T(8,128)S(1)}) custom-call(s32[3]{0:T(128)S(1)} %pad_add_fusion.place, bf16[4,16,96,512]{3,2,1,0:T(8,128)(2,1)S(1)} %get-tuple-element.40.f_hbm, bf16[4,512,512]{2,1,0:T(8,128)(2,1)S(1)} %copy-done.3, bf16[16,96,512]{2,1,0:T(8,128)(2,1)S(1)} %get-tuple-element.39.cells_ref), custom_call_target="tpu_custom_call" | custom-call | flops 4831838208 | bytes 12000000 | tf_op jit(solution)/shard_map/remainder/pallas_call | solution.py:282
  43.7 0.0 collective-permute-done.6
  43.7 0.3 add_convert_fusion
  44.1 23.7 %all_to_all.10 = bf16[32,32,512]{2,1,0:T(8,128)(2,1)S(1)} all-to-all(bf16[32,32,512]{2,1,0:T(8,128)(2,1)S(1)} %bitcast.16), channel_id=1, replica_groups=mesh['y'=4,'xh'=2,'core'=2,'xl'=2,'zh'=4,'zl'=2] {'y','xh','xl','zl'}, dimensions={0} | all-to-all | bytes 2097152 | tf_op jit(solution)/shard_map/all_to_all | solution.py:384
  67.8 0.2 reduce_sum.12
  68.0 3.5 %collective-permute-start.9 = (bf16[32,512]{1,0:T(8,128)(2,1)S(1)}, bf16[32,512]{1,0:T(8,128)(2,1)S(1)}, u32[]{:S(2)}, u32[]{:S(2)}) collective-permute-start(bf16[32,512]{1,0:T(8,128)(2,1)S(1)} %reduce_sum.12), channel_id=1, source_target_pairs={{0,4},{1,5},{2,6},{3,7},{4,0},{5,1},{6,2},{7,3},{8,12},{9,13},{10,... | collective-permute-start | bytes 98312 | tf_op jit(solution)/shard_map/ppermute | solution.py:405
  71.4 0.9 collective-permute-start.8
  72.3 1.6 %collective-permute-start.7 = (bf16[32,512]{1,0:T(8,128)(2,1)S(1)}, bf16[32,512]{1,0:T(8,128)(2,1)S(1)}, u32[]{:S(2)}, u32[]{:S(2)}) collective-permute-start(bf16[32,512]{1,0:T(8,128)(2,1)S(1)} %reduce_sum.12), channel_id=1, source_target_pairs={{0,2},{1,3},{2,0},{3,1},{4,6},{5,7},{6,4},{7,5},{8,10},{9,11},{10,... | collective-permute-start | bytes 98312 | tf_op jit(solution)/shard_map/ppermute | solution.py:405
  74.0 0.7 collective-permute-done.9
  74.7 1.7 %collective-permute-done.8 = bf16[32,512]{1,0:T(8,128)(2,1)S(1)} collective-permute-done((bf16[32,512]{1,0:T(8,128)(2,1)S(1)}, bf16[32,512]{1,0:T(8,128)(2,1)S(1)}, u32[]{:S(2)}, u32[]{:S(2)}) %collective-permute-start.8) | collective-permute-done | bytes 32800 | tf_op jit(solution)/shard_map/ppermute | solution.py:405
  76.4 0.2 collective-permute-done.7
  76.7 0.1 broadcast_in_dim.3
  76.8 18.7 %all_to_all.11 = bf16[32,32,512]{2,1,0:T(8,128)(2,1)S(1)} all-to-all(bf16[32,32,512]{2,1,0:T(8,128)(2,1)S(1)} %broadcast_in_dim.3), channel_id=1, replica_groups=mesh['y'=4,'xh'=2,'core'=2,'xl'=2,'zh'=4,'zl'=2] {'y','xh','xl','zl'}, dimensions={0} | all-to-all | bytes 2097152 | tf_op jit(solution)/shard_map/all_to_all | solution.py:409
  95.5 3.9 %collective-permute-start.10 = (bf16[2,512,512]{2,1,0:T(8,128)(2,1)S(1)}, bf16[2,512,512]{2,1,0:T(8,128)(2,1)S(1)}, u32[]{:S(2)}, u32[]{:S(2)}) collective-permute-start(bf16[2,512,512]{2,1,0:T(8,128)(2,1)S(1)} %bitcast.12), channel_id=1, source_target_pairs={{0,16},{1,17},{2,18},{3,19},{4,20},{5,21},{6,22},{7,23},{8,24},{9,... | collective-permute-start | bytes 3145736 | tf_op jit(solution)/shard_map/ppermute | solution.py:411
  99.4 1.5 %put_half.2.rest_0_ = bf16[4,512,512]{2,1,0:T(8,128)(2,1)} custom-call(s32[3]{0:T(128)S(1)} %pad_add_fusion.place, bf16[2,512,512]{2,1,0:T(8,128)(2,1)S(1)} %bitcast.13), custom_call_target="tpu_custom_call" | custom-call | tf_op jit(solution)/shard_map/put_half/pallas_call | solution.py:29
  100.9 0.7 collective-permute-done.10.half
  101.7 1.5 %put_half.3 = bf16[4,512,512]{2,1,0:T(8,128)(2,1)} custom-call(s32[3]{0:T(128)S(1)} %pad_add_fusion.place, bf16[2,512,512]{2,1,0:T(8,128)(2,1)S(1)} %collective-permute-done.10.half, bf16[4,512,512]{2,1,0:T(8,128)(2,1)} %put_half.2.rest_0_), custom_call_target="tpu_custom_call", output_to_operand_aliasing={{}: (2, {})} | custom-call | tf_op jit(solution)/shard_map/put_half/pallas_call | solution.py:29
  (1 shorter events, 0.0 us)
Async XLA Ops:
  0.6 23.8 %copy-start.2 = (s32[256]{0:T(256)S(1)}, s32[256]{0:T(256)}, u32[]{:S(2)}) copy-start(s32[256]{0:T(256)} %param.9) | copy-start | bytes 3076
  0.7 1.4 %copy-start = (bf16[16,90,512]{2,0,1:T(8,128)(2,1)S(1)}, bf16[16,90,512]{2,0,1:T(8,128)(2,1)}, u32[]{:S(2)}) copy-start(bf16[16,90,512]{2,0,1:T(8,128)(2,1)} %param.5) | copy-start | bytes 4423684
  2.1 22.4 %copy-start.1 = (bf16[16,90,512]{2,0,1:T(8,128)(2,1)S(1)}, bf16[16,90,512]{2,0,1:T(8,128)(2,1)}, u32[]{:S(2)}) copy-start(bf16[16,90,512]{2,0,1:T(8,128)(2,1)} %param.6) | copy-start | bytes 4423684
  3.6 24.9 %collective-permute-start.2 = (bf16[16,16,512]{2,1,0:T(8,128)(2,1)}, bf16[16,16,512]{2,1,0:T(8,128)(2,1)S(1)}, u32[]{:S(2)}, u32[]{:S(2)}) collective-permute-start(bf16[16,16,512]{2,1,0:T(8,128)(2,1)} %get-tuple-element.35), channel_id=1, source_target_pairs={{0,1},{1,0},{2,3},{3,2},{4,5},{5,4},{6,7},{7,6},{8,9},{9,8},{10,11... | collective-permute-start | bytes 786440 | tf_op jit(solution)/shard_map/ppermute | solution.py:360
  6.1 22.3 %collective-permute-start.3 = (bf16[16,16,512]{2,1,0:T(8,128)(2,1)}, bf16[16,16,512]{2,1,0:T(8,128)(2,1)}, u32[]{:S(2)}, u32[]{:S(2)}) collective-permute-start(bf16[16,16,512]{2,1,0:T(8,128)(2,1)} %get-tuple-element.36), channel_id=1, source_target_pairs={{0,15},{1,2},{2,1},{3,4},{4,3},{5,6},{6,5},{7,8},{8,7},{9,10},{10,... | collective-permute-start | bytes 786440 | tf_op jit(solution)/shard_map/ppermute | solution.py:361
  11.7 3.2 %collective-permute-start = (bf16[2,16,512]{2,1,0:T(8,128)(2,1)S(1)}, bf16[2,16,512]{2,1,0:T(8,128)(2,1)S(1)}, u32[]{:S(2)}, u32[]{:S(2)}) collective-permute-start(bf16[2,16,512]{2,1,0:T(8,128)(2,1)S(1)} %get-tuple-element.28), channel_id=1, source_target_pairs={{0,1},{1,0},{2,3},{3,2},{4,5},{5,4},{6,7},{7,6},{8,9},{9,8},{10,11... | collective-permute-start | bytes 98312 | tf_op jit(solution)/shard_map/ppermute | solution.py:358
  11.7 6.7 %collective-permute-start.1 = (bf16[2,16,512]{2,1,0:T(8,128)(2,1)S(1)}, bf16[2,16,512]{2,1,0:T(8,128)(2,1)S(1)}, u32[]{:S(2)}, u32[]{:S(2)}) collective-permute-start(bf16[2,16,512]{2,1,0:T(8,128)(2,1)S(1)} %get-tuple-element.29), channel_id=1, source_target_pairs={{0,15},{1,2},{2,1},{3,4},{4,3},{5,6},{6,5},{7,8},{8,7},{9,10},{10,... | collective-permute-start | bytes 98312 | tf_op jit(solution)/shard_map/ppermute | solution.py:359
  19.7 7.4 %collective-permute-start.4 = (bf16[128,512]{1,0:T(8,128)(2,1)}, bf16[128,512]{1,0:T(8,128)(2,1)}, u32[]{:S(2)}, u32[]{:S(2)}) collective-permute-start(bf16[128,512]{1,0:T(8,128)(2,1)} %get-tuple-element.37), channel_id=1, source_target_pairs={{0,16},{1,17},{2,18},{3,19},{4,20},{5,21},{6,22},{7,23},{8,24},{9,... | collective-permute-start | bytes 393224 | tf_op jit(solution)/shard_map/ppermute | solution.py:396
  21.1 7.3 %collective-permute-start.5 = (bf16[128,512]{1,0:T(8,128)(2,1)}, bf16[128,512]{1,0:T(8,128)(2,1)}, u32[]{:S(2)}, u32[]{:S(2)}) collective-permute-start(bf16[128,512]{1,0:T(8,128)(2,1)} %get-tuple-element.38), channel_id=1, source_target_pairs={{0,8},{1,9},{2,10},{3,11},{4,12},{5,13},{6,14},{7,15},{8,0},{9,1},... | collective-permute-start | bytes 393224 | tf_op jit(solution)/shard_map/ppermute | solution.py:397
  28.4 7.4 %copy-start.3 = (bf16[4,512,512]{2,1,0:T(8,128)(2,1)S(1)}, bf16[4,512,512]{2,1,0:T(8,128)(2,1)}, u32[]{:S(2)}) copy-start(bf16[4,512,512]{2,1,0:T(8,128)(2,1)} %weight_hbm.1) | copy-start | bytes 6291460
  35.6 8.1 %collective-permute-start.6 = (bf16[2,512,512]{2,1,0:T(8,128)(2,1)S(1)}, bf16[2,512,512]{2,1,0:T(8,128)(2,1)S(1)}, u32[]{:S(2)}, u32[]{:S(2)}) collective-permute-start(bf16[2,512,512]{2,1,0:T(8,128)(2,1)S(1)} %get-tuple-element.42), channel_id=1, source_target_pairs={{0,16},{1,17},{2,18},{3,19},{4,20},{5,21},{6,22},{7,23},{8,24},{9,... | collective-permute-start | bytes 3145736 | tf_op jit(solution)/shard_map/ppermute | solution.py:400
  68.0 6.8 %collective-permute-start.9 = (bf16[32,512]{1,0:T(8,128)(2,1)S(1)}, bf16[32,512]{1,0:T(8,128)(2,1)S(1)}, u32[]{:S(2)}, u32[]{:S(2)}) collective-permute-start(bf16[32,512]{1,0:T(8,128)(2,1)S(1)} %reduce_sum.12), channel_id=1, source_target_pairs={{0,4},{1,5},{2,6},{3,7},{4,0},{5,1},{6,2},{7,3},{8,12},{9,13},{10,... | collective-permute-start | bytes 98312 | tf_op jit(solution)/shard_map/ppermute | solution.py:405
  71.4 5.0 %collective-permute-start.8 = (bf16[32,512]{1,0:T(8,128)(2,1)S(1)}, bf16[32,512]{1,0:T(8,128)(2,1)S(1)}, u32[]{:S(2)}, u32[]{:S(2)}) collective-permute-start(bf16[32,512]{1,0:T(8,128)(2,1)S(1)} %reduce_sum.12), channel_id=1, source_target_pairs={{0,6},{1,7},{2,4},{3,5},{4,2},{5,3},{6,0},{7,1},{8,14},{9,15},{10,... | collective-permute-start | bytes 98312 | tf_op jit(solution)/shard_map/ppermute | solution.py:405
  72.3 4.3 %collective-permute-start.7 = (bf16[32,512]{1,0:T(8,128)(2,1)S(1)}, bf16[32,512]{1,0:T(8,128)(2,1)S(1)}, u32[]{:S(2)}, u32[]{:S(2)}) collective-permute-start(bf16[32,512]{1,0:T(8,128)(2,1)S(1)} %reduce_sum.12), channel_id=1, source_target_pairs={{0,2},{1,3},{2,0},{3,1},{4,6},{5,7},{6,4},{7,5},{8,10},{9,11},{10,... | collective-permute-start | bytes 98312 | tf_op jit(solution)/shard_map/ppermute | solution.py:405
  95.5 6.2 %collective-permute-start.10 = (bf16[2,512,512]{2,1,0:T(8,128)(2,1)S(1)}, bf16[2,512,512]{2,1,0:T(8,128)(2,1)S(1)}, u32[]{:S(2)}, u32[]{:S(2)}) collective-permute-start(bf16[2,512,512]{2,1,0:T(8,128)(2,1)S(1)} %bitcast.12), channel_id=1, source_target_pairs={{0,16},{1,17},{2,18},{3,19},{4,20},{5,21},{6,22},{7,23},{8,24},{9,... | collective-permute-start | bytes 3145736 | tf_op jit(solution)/shard_map/ppermute | solution.py:411

commit v5 on v4

--- a/solution.py
+++ b/solution.py
@@ -39,17 +39,11 @@
     )(*inputs)
 
 
-def edges_kernel(place, own, slab_a, slab_b, edge_a, edge_b, sides, sems):
-    copies = [
-        pltpu.make_async_copy(own.at[pl.ds(start, REACH)], sides.at[i], sems.at[i]) for i, start in enumerate((0, COLS - REACH))
-    ]
-    for copy in copies:
-        copy.start()
-    for copy in copies:
-        copy.wait()
+def edges_kernel(place, own, slab_a, slab_b, edge_a, edge_b):
     even = place[1] == 0
-    slab_a[...] = jnp.where(even, sides[1], sides[0])
-    slab_b[...] = jnp.where(even, sides[0], sides[1])
+    west, east = own[:REACH], own[COLS - REACH :]
+    slab_a[...] = jnp.where(even, east, west)
+    slab_b[...] = jnp.where(even, west, east)
     for slab, edge in ((slab_a, edge_a), (slab_b, edge_b)):
         block = turned(slab[...])
         edge[0], edge[1] = block[0], block[ROWS - 1]
@@ -74,7 +68,7 @@
     return turned(block)
 
 
-def turn_kernel(place, own, rows, middle, buffer, sems):
+def turn_kernel(place, own, _, rows, middle, buffer, sems):
     copies = fetches(own, buffer, sems)
     for b, left, n in chunks():
         copies[b].wait()
@@ -99,7 +93,7 @@
 LEAD = 8
 
 
-def prepare_kernel(place, basis, reach, act, tiles, cells, placed, buffer, sems):
+def prepare_kernel(place, basis, reach, act, _, tiles, cells, placed, buffer, sems):
     copies = fetches(act, buffer, sems)
     length = basis.shape[1]
     lats = basis.shape[2]
@@ -350,24 +344,20 @@
 
 def haloes(own, place):
     slab, edge, wide = (REACH, ROWS, CHANNELS), (2, REACH, CHANNELS), (WIDE, CHANNELS)
-    slab_a, slab_b, edge_a, edge_b = local(
-        edges_kernel, "edges", [slab, slab, edge, edge], [place, own],
-        [pltpu.VMEM((2, *slab), BF16), pltpu.SemaphoreType.DMA((2,))], {1: pltpu.HBM},
+    slab_a, slab_b, edge_a, edge_b = local(edges_kernel, "edges", [slab, slab, edge, edge], [place, own])
+    rows, middle = local(
+        turn_kernel, "turn", [(ROWS, PAD, CHANNELS), (2, PAD, CHANNELS)], [place, own, edge_a],
+        [pltpu.VMEM(own.shape, BF16), pltpu.SemaphoreType.DMA((PAD // 16,))], {1: pltpu.HBM, 2: pl.ANY}, cost=4_000_000_000,
     )
-    own, edge_a, edge_b = lax.optimization_barrier((own, edge_a, edge_b))
     edge_a = lax.ppermute(edge_a, AXES, LON_A)
     edge_b = lax.ppermute(edge_b, AXES, LON_B)
     lon_a = lax.ppermute(slab_a, AXES, LON_A)
     lon_b = lax.ppermute(slab_b, AXES, LON_B)
-    rows, middle = local(
-        turn_kernel, "turn", [(ROWS, PAD, CHANNELS), (2, PAD, CHANNELS)], [place, own],
-        [pltpu.VMEM(own.shape, BF16), pltpu.SemaphoreType.DMA((PAD // 16,))], {1: pltpu.HBM},
-    )
     wide_a, wide_b = local(widen_kernel, "widen", [wide, wide], [place, middle, edge_a, edge_b])
     return rows, lon_a, lon_b, wide_a, wide_b
 
 
-def prepared(place, basis, reach, act):
+def prepared(place, basis, reach, act, after):
     taps, lats = basis.shape[2] * FILTERS, basis.shape[3]
     basis = jnp.transpose(basis, (1, 2, 0, 3)).reshape(TAPS, taps, lats)
     scratch = [
@@ -376,8 +366,8 @@
         pltpu.SemaphoreType.DMA((PAD // 16,)),
     ]
     shapes = [(ROWS, FILTERS * HALF, DEPTH), (ROWS, PAD, CHANNELS)]
-    inputs = [place, basis, reach.reshape(1, lats), act]
-    return local(prepare_kernel, "prepare", shapes, inputs, scratch, {3: pltpu.HBM}, cost=100_000_000)
+    inputs = [place, basis, reach.reshape(1, lats), act, after]
+    return local(prepare_kernel, "prepare", shapes, inputs, scratch, {3: pltpu.HBM, 4: pl.ANY}, cost=1_000_000_000)
 
 
 def summed(parts, groups, axes):
@@ -392,14 +382,12 @@
     place = jnp.stack([core, odd, band])
     own, act = jnp.swapaxes(cotangent, 0, 1), jnp.swapaxes(activations, 0, 1)
     rows, lon_a, lon_b, wide_a, wide_b = haloes(own, place)
-    act, wide_a, wide_b = lax.optimization_barrier((act, wide_a, wide_b))
     lat_a = lax.ppermute(wide_a, AXES, LAT_A)
     lat_b = lax.ppermute(wide_b, AXES, LAT_B)
-    tiles, cells = prepared(place, basis, reach, act)
+    tiles, cells = prepared(place, basis, reach, act, wide_a)
     f, send = stencil(place, tiles, rows, lon_a, lon_b, lat_a, lat_b, cells)
     got = lax.ppermute(send, AXES, SIBLING)
     grad_input, mine = remainder(place, f, weight, cells)
-    got, mine = lax.optimization_barrier((got, mine))
     half = (mine + got.astype(F32)).astype(BF16)
     part = lax.optimization_barrier(summed(half.reshape(-1, CHANNELS), 32, BLOCK).astype(BF16))
     others = [lax.ppermute(part, AXES, along_z(m)).astype(F32) for m in (2, 6, 4)]

time: 104 us -> 97.6 us (0.938)
  waiting for transfers between devices: 8.75 us -> 5.65 us
  Pallas kernels: 24.6 us -> 22 us
  blocking collectives: 42.5 us -> 40.5 us
  local copies, waits for them, and re-layouts: 2.48 us -> 3.84 us
    ppermute x1, starting transfers between devices: 1.45 us -> 7.42 us  [haloes(): edge_b = lax.ppermute(edge_b, AXES, LON_B)]
    ppermute x1, starting transfers between devices: 5.59 us -> 0.1 us  [haloes(): lon_b = lax.ppermute(slab_b, AXES, LON_B)]
    ppermute x1, waiting for transfers between devices: 3.56 us -> 0.01 us  [haloes(): edge_b = lax.ppermute(edge_b, AXES, LON_B)]
    ppermute x1, starting transfers between devices: 2.34 us -> 4.81 us  [on_device(): lat_b = lax.ppermute(wide_b, AXES, LAT_B)]
    pallas_call x6, Pallas kernels: 9.63 us -> 8.17 us  [local(): pl.pallas_call(kernel, in_specs=[pl.BlockSpec(memory_space=pltpu.SMEM)] +...]
    ppermute x1, starting transfers between devices: 1.44 us -> 0.01 us  [on_device(): lat_a = lax.ppermute(wide_a, AXES, LAT_A)]
    unnamed x8, local copies, waits for them, and re-layouts: 1.39 us -> 2.75 us
    ppermute x1, waiting for transfers between devices: 1.37 us -> 2.64 us  [on_device(): lat_b = lax.ppermute(wide_b, AXES, LAT_B)]
  transfers between devices with their start and end apart: 11 -> 11, of which waited for: 7 -> 4; matrix products, arithmetic and copies ran while one was open for 1% -> 1% of each run, Pallas kernels for 14% -> 14%
where the time goes in v5:
time: 97.6 us; the launch traced here: 97.4 us
  blocking collectives  40.5 us (41%)
  starting transfers between devices  23.8 us (24%)
  Pallas kernels  22 us (23%)
  waiting for transfers between devices  5.65 us (6%)
  local copies, waits for them, and re-layouts  3.84 us (4%)
    all_to_all x1, blocking collectives, summed(): lax.all_to_all(parts.reshape(groups, -1, CHANNELS), axes, 0, 0, tiled=True)  22.6 us
    all_to_all x1, blocking collectives, on_device(): lax.all_to_all(jnp.broadcast_to(part, (32, *part.shape)), BLOCK, 0, 0, ti...  17.9 us
    pallas_call x6, Pallas kernels, local(): pl.pallas_call(kernel, in_specs=[pl.BlockSpec(memory_space=pltpu.SMEM)] +...  8.17 us
    pallas_call x1, Pallas kernels, remainder(): pl.pallas_call(remainder_kernel, in_specs=[spec(pltpu.SMEM), spec(pltpu.H...  7.81 us
    ppermute x1, starting transfers between devices, haloes(): edge_b = lax.ppermute(edge_b, AXES, LON_B)  7.42 us
    pallas_call x1, Pallas kernels, stencil(): pl.pallas_call(stencil_kernel, grid_spec=pltpu.PrefetchScalarGridSpec(num...  5.99 us
    ppermute x3, starting transfers between devices, on_device(): lax.ppermute(part, AXES, along_z(m)).astype(F32)  5.74 us
    ppermute x1, starting transfers between devices, on_device(): lat_b = lax.ppermute(wide_b, AXES, LAT_B)  4.81 us
  transfers between devices with their start and end apart: 11, of which 4 were waited for; matrix products, arithmetic and copies ran while one was open for 1% of the time, Pallas kernels for 14%

profile of v5, /device:TPU:1, one launch (start us, length us, event | category | flops | bytes accessed | tf_op | source)
XLA Modules:
  0.0 97.4 jit_solution(1880932285312816204)
XLA Ops:
  0.6 0.1 pad_add_fusion.place
  0.7 0.0 copy-start
  0.7 1.4 %copy-done = bf16[16,90,512]{2,0,1:T(8,128)(2,1)S(1)} copy-done((bf16[16,90,512]{2,0,1:T(8,128)(2,1)S(1)}, bf16[16,90,512]{2,0,1:T(8,128)(2,1)}, u32[]{:S(2)}) %copy-start) | copy-done | bytes 1474584
  2.1 0.7 edges.1
  2.8 7.4 %collective-permute-start.1 = (bf16[2,16,512]{2,1,0:T(8,128)(2,1)S(1)}, bf16[2,16,512]{2,1,0:T(8,128)(2,1)S(1)}, u32[]{:S(2)}, u32[]{:S(2)}) collective-permute-start(bf16[2,16,512]{2,1,0:T(8,128)(2,1)S(1)} %get-tuple-element.18), channel_id=1, source_target_pairs={{0,15},{1,2},{2,1},{3,4},{4,3},{5,6},{6,5},{7,8},{8,7},{9,10},{10,... | collective-permute-start | bytes 98312 | tf_op jit(solution)/shard_map/ppermute | solution.py:353
  10.2 0.0 collective-permute-start
  10.2 1.5 %collective-permute-start.2 = (bf16[16,16,512]{2,1,0:T(8,128)(2,1)S(1)}, bf16[16,16,512]{2,1,0:T(8,128)(2,1)S(1)}, u32[]{:S(2)}, u32[]{:S(2)}) collective-permute-start(bf16[16,16,512]{2,1,0:T(8,128)(2,1)S(1)} %get-tuple-element.22), channel_id=1, source_target_pairs={{0,1},{1,0},{2,3},{3,2},{4,5},{5,4},{6,7},{7,6},{8,9},{9,8},{10,11... | collective-permute-start | bytes 786440 | tf_op jit(solution)/shard_map/ppermute | solution.py:354
  11.7 0.0 copy-start.3
  11.7 0.1 collective-permute-start.3
  11.8 1.3 %turn.1 = (bf16[16,96,512]{2,1,0:T(8,128)(2,1)S(1)}, bf16[2,96,512]{2,1,0:T(8,128)(2,1)S(1)}) custom-call(s32[3]{0:T(128)S(1)} %pad_add_fusion.place, bf16[90,16,512]{2,1,0:T(8,128)(2,1)S(1)} %bitcast.13, bf16[2,16,512]{2,1,0:T(8,128)(2,1)S(1)} %get-tuple-element.16._), custom_call_target="tpu_custom_call" | custom-call | flops 4000000000 | bytes 2000000 | tf_op jit(solution)/shard_map/turn/pallas_call | solution.py:29
  13.1 0.0 collective-permute-done.1.got_b
  13.1 0.0 collective-permute-done.got_a
  13.1 0.6 widen.1
  13.7 4.8 %collective-permute-start.5 = (bf16[128,512]{1,0:T(8,128)(2,1)S(1)}, bf16[128,512]{1,0:T(8,128)(2,1)S(1)}, u32[]{:S(2)}, u32[]{:S(2)}) collective-permute-start(bf16[128,512]{1,0:T(8,128)(2,1)S(1)} %get-tuple-element.24), channel_id=1, source_target_pairs={{0,8},{1,9},{2,10},{3,11},{4,12},{5,13},{6,14},{7,15},{8,0},{9,1},... | collective-permute-start | bytes 393224 | tf_op jit(solution)/shard_map/ppermute | solution.py:386
  18.5 0.0 collective-permute-start.4
  18.5 1.0 %reshape.13.basis = bf16[3,132,256]{2,1,0:T(8,128)(2,1)S(1)} reshape(bf16[3,33,4,256]{3,2,1,0:T(4,128)(2,1)} %bitcast.17) | data formatting | bytes 405504 | tf_op jit(solution)/shard_map/reshape | solution.py:362
  19.4 0.0 copy-done.3
  19.5 0.0 copy-start.2
  19.5 1.4 %copy-done.2 = bf16[16,90,512]{2,0,1:T(8,128)(2,1)S(1)} copy-done((bf16[16,90,512]{2,0,1:T(8,128)(2,1)S(1)}, bf16[16,90,512]{2,0,1:T(8,128)(2,1)}, u32[]{:S(2)}) %copy-start.2) | copy-done | bytes 1474584
  20.8 2.6 %prepare.1 = (bf16[16,192,256]{2,1,0:T(8,128)(2,1)S(1)}, bf16[16,96,512]{2,1,0:T(8,128)(2,1)S(1)}) custom-call(s32[3]{0:T(128)S(1)} %pad_add_fusion.place, bf16[3,132,256]{2,1,0:T(8,128)(2,1)S(1)} %reshape.13.basis, s32[1,256]{1,0:T(1,128)S(1)} %bitcast.15, bf16[90,16,512]{2,1,0:T(8,128)(2,1)S(1)} %bitcast.14, bf16[128,512]{1,0:T(8,128)(2,1)S(1)} %get-tuple-element.19._), custom_call_target="tpu_custom_call" | custom-call | flops 1000000000 | bytes 2000000 | tf_op jit(solution)/shard_map/prepare/pallas_call | solution.py:29
  23.4 2.6 %collective-permute-done.5.lat_b = bf16[128,512]{1,0:T(8,128)(2,1)S(1)} collective-permute-done((bf16[128,512]{1,0:T(8,128)(2,1)S(1)}, bf16[128,512]{1,0:T(8,128)(2,1)S(1)}, u32[]{:S(2)}, u32[]{:S(2)}) %collective-permute-start.5) | collective-permute-done | bytes 131104 | tf_op jit(solution)/shard_map/ppermute | solution.py:386
  26.0 0.0 collective-permute-done.4.lat_a
  26.0 0.0 collective-permute-done.2.lon_a
  26.0 0.0 collective-permute-done.3.lon_b
  26.1 0.0 copy-start.1
  26.1 6.0 %stencil.1 = (bf16[4,16,96,512]{3,2,1,0:T(8,128)(2,1)S(1)}, bf16[2,512,512]{2,1,0:T(8,128)(2,1)S(1)}) custom-call(s32[3]{0:T(128)S(1)} %pad_add_fusion.place, bf16[16,192,256]{2,1,0:T(8,128)(2,1)S(1)} %get-tuple-element.20.tiles, bf16[16,96,512]{2,1,0:T(8,128)(2,1)S(1)} %get-tuple-element.21.rows, bf16[16,16,512]{2,1,0:T(8,128)(2,1)S(1)} %collective-permute-done.2.lon_a, ...), custom_call_target="tpu_custom_call" | custom-call | tf_op jit(solution)/shard_map/stencil/pallas_call | solution.py:194
  32.1 0.3 collective-permute-start.6
  32.3 0.0 copy-done.1
  32.4 7.8 %remainder.1 = (bf16[90,16,512]{2,1,0:T(8,128)(2,1)}, f32[2,512,512]{2,1,0:T(8,128)S(1)}) custom-call(s32[3]{0:T(128)S(1)} %pad_add_fusion.place, bf16[4,16,96,512]{3,2,1,0:T(8,128)(2,1)S(1)} %get-tuple-element.26.f_hbm, bf16[4,512,512]{2,1,0:T(8,128)(2,1)S(1)} %copy-done.1, bf16[16,96,512]{2,1,0:T(8,128)(2,1)S(1)} %get-tuple-element.25.cells_ref), custom_call_target="tpu_custom_call" | custom-call | flops 4831838208 | bytes 12000000 | tf_op jit(solution)/shard_map/remainder/pallas_call | solution.py:276
  40.2 0.0 collective-permute-done.6
  40.2 0.3 add_convert_fusion
  40.5 22.6 %all_to_all.10 = bf16[32,32,512]{2,1,0:T(8,128)(2,1)S(1)} all-to-all(bf16[32,32,512]{2,1,0:T(8,128)(2,1)S(1)} %bitcast.16), channel_id=1, replica_groups=mesh['y'=4,'xh'=2,'core'=2,'xl'=2,'zh'=4,'zl'=2] {'y','xh','xl','zl'}, dimensions={0} | all-to-all | bytes 2097152 | tf_op jit(solution)/shard_map/all_to_all | solution.py:374
  63.2 0.2 reduce_sum.12
  63.3 1.1 %collective-permute-start.9 = (bf16[32,512]{1,0:T(8,128)(2,1)S(1)}, bf16[32,512]{1,0:T(8,128)(2,1)S(1)}, u32[]{:S(2)}, u32[]{:S(2)}) collective-permute-start(bf16[32,512]{1,0:T(8,128)(2,1)S(1)} %reduce_sum.12), channel_id=1, source_target_pairs={{0,4},{1,5},{2,6},{3,7},{4,0},{5,1},{6,2},{7,3},{8,12},{9,13},{10,... | collective-permute-start | bytes 98312 | tf_op jit(solution)/shard_map/ppermute | solution.py:393
  64.4 1.6 %collective-permute-start.8 = (bf16[32,512]{1,0:T(8,128)(2,1)S(1)}, bf16[32,512]{1,0:T(8,128)(2,1)S(1)}, u32[]{:S(2)}, u32[]{:S(2)}) collective-permute-start(bf16[32,512]{1,0:T(8,128)(2,1)S(1)} %reduce_sum.12), channel_id=1, source_target_pairs={{0,6},{1,7},{2,4},{3,5},{4,2},{5,3},{6,0},{7,1},{8,14},{9,15},{10,... | collective-permute-start | bytes 98312 | tf_op jit(solution)/shard_map/ppermute | solution.py:393
  66.0 3.1 %collective-permute-start.7 = (bf16[32,512]{1,0:T(8,128)(2,1)S(1)}, bf16[32,512]{1,0:T(8,128)(2,1)S(1)}, u32[]{:S(2)}, u32[]{:S(2)}) collective-permute-start(bf16[32,512]{1,0:T(8,128)(2,1)S(1)} %reduce_sum.12), channel_id=1, source_target_pairs={{0,2},{1,3},{2,0},{3,1},{4,6},{5,7},{6,4},{7,5},{8,10},{9,11},{10,... | collective-permute-start | bytes 98312 | tf_op jit(solution)/shard_map/ppermute | solution.py:393
  69.1 1.0 %collective-permute-done.9 = bf16[32,512]{1,0:T(8,128)(2,1)S(1)} collective-permute-done((bf16[32,512]{1,0:T(8,128)(2,1)S(1)}, bf16[32,512]{1,0:T(8,128)(2,1)S(1)}, u32[]{:S(2)}, u32[]{:S(2)}) %collective-permute-start.9) | collective-permute-done | bytes 32800 | tf_op jit(solution)/shard_map/ppermute | solution.py:393
  70.1 0.0 collective-permute-done.8
  70.1 1.2 %collective-permute-done.7 = bf16[32,512]{1,0:T(8,128)(2,1)S(1)} collective-permute-done((bf16[32,512]{1,0:T(8,128)(2,1)S(1)}, bf16[32,512]{1,0:T(8,128)(2,1)S(1)}, u32[]{:S(2)}, u32[]{:S(2)}) %collective-permute-start.7) | collective-permute-done | bytes 32800 | tf_op jit(solution)/shard_map/ppermute | solution.py:393
  71.3 0.1 broadcast_in_dim.3
  71.5 17.9 %all_to_all.11 = bf16[32,32,512]{2,1,0:T(8,128)(2,1)S(1)} all-to-all(bf16[32,32,512]{2,1,0:T(8,128)(2,1)S(1)} %broadcast_in_dim.3), channel_id=1, replica_groups=mesh['y'=4,'xh'=2,'core'=2,'xl'=2,'zh'=4,'zl'=2] {'y','xh','xl','zl'}, dimensions={0} | all-to-all | bytes 2097152 | tf_op jit(solution)/shard_map/all_to_all | solution.py:397
  89.4 4.0 %collective-permute-start.10 = (bf16[2,512,512]{2,1,0:T(8,128)(2,1)S(1)}, bf16[2,512,512]{2,1,0:T(8,128)(2,1)S(1)}, u32[]{:S(2)}, u32[]{:S(2)}) collective-permute-start(bf16[2,512,512]{2,1,0:T(8,128)(2,1)S(1)} %bitcast.10), channel_id=1, source_target_pairs={{0,16},{1,17},{2,18},{3,19},{4,20},{5,21},{6,22},{7,23},{8,24},{9,... | collective-permute-start | bytes 3145736 | tf_op jit(solution)/shard_map/ppermute | solution.py:399
  93.4 1.5 %put_half.2.rest_0_ = bf16[4,512,512]{2,1,0:T(8,128)(2,1)} custom-call(s32[3]{0:T(128)S(1)} %pad_add_fusion.place, bf16[2,512,512]{2,1,0:T(8,128)(2,1)S(1)} %bitcast.11), custom_call_target="tpu_custom_call" | custom-call | tf_op jit(solution)/shard_map/put_half/pallas_call | solution.py:29
  94.9 0.7 collective-permute-done.10.half
  95.7 1.5 %put_half.3 = bf16[4,512,512]{2,1,0:T(8,128)(2,1)} custom-call(s32[3]{0:T(128)S(1)} %pad_add_fusion.place, bf16[2,512,512]{2,1,0:T(8,128)(2,1)S(1)} %collective-permute-done.10.half, bf16[4,512,512]{2,1,0:T(8,128)(2,1)} %put_half.2.rest_0_), custom_call_target="tpu_custom_call", output_to_operand_aliasing={{}: (2, {})} | custom-call | tf_op jit(solution)/shard_map/put_half/pallas_call | solution.py:29
  (1 shorter events, 0.0 us)
Async XLA Ops:
  0.7 1.4 %copy-start = (bf16[16,90,512]{2,0,1:T(8,128)(2,1)S(1)}, bf16[16,90,512]{2,0,1:T(8,128)(2,1)}, u32[]{:S(2)}) copy-start(bf16[16,90,512]{2,0,1:T(8,128)(2,1)} %param.5) | copy-start | bytes 4423684
  2.8 10.3 %collective-permute-start.1 = (bf16[2,16,512]{2,1,0:T(8,128)(2,1)S(1)}, bf16[2,16,512]{2,1,0:T(8,128)(2,1)S(1)}, u32[]{:S(2)}, u32[]{:S(2)}) collective-permute-start(bf16[2,16,512]{2,1,0:T(8,128)(2,1)S(1)} %get-tuple-element.18), channel_id=1, source_target_pairs={{0,15},{1,2},{2,1},{3,4},{4,3},{5,6},{6,5},{7,8},{8,7},{9,10},{10,... | collective-permute-start | bytes 98312 | tf_op jit(solution)/shard_map/ppermute | solution.py:353
  10.2 2.9 %collective-permute-start = (bf16[2,16,512]{2,1,0:T(8,128)(2,1)S(1)}, bf16[2,16,512]{2,1,0:T(8,128)(2,1)S(1)}, u32[]{:S(2)}, u32[]{:S(2)}) collective-permute-start(bf16[2,16,512]{2,1,0:T(8,128)(2,1)S(1)} %get-tuple-element.16._), channel_id=1, source_target_pairs={{0,1},{1,0},{2,3},{3,2},{4,5},{5,4},{6,7},{7,6},{8,9},{9,8},{10,11... | collective-permute-start | bytes 98312 | tf_op jit(solution)/shard_map/ppermute | solution.py:352
  10.2 15.9 %collective-permute-start.2 = (bf16[16,16,512]{2,1,0:T(8,128)(2,1)S(1)}, bf16[16,16,512]{2,1,0:T(8,128)(2,1)S(1)}, u32[]{:S(2)}, u32[]{:S(2)}) collective-permute-start(bf16[16,16,512]{2,1,0:T(8,128)(2,1)S(1)} %get-tuple-element.22), channel_id=1, source_target_pairs={{0,1},{1,0},{2,3},{3,2},{4,5},{5,4},{6,7},{7,6},{8,9},{9,8},{10,11... | collective-permute-start | bytes 786440 | tf_op jit(solution)/shard_map/ppermute | solution.py:354
  11.7 7.8 %copy-start.3 = (s32[256]{0:T(256)S(1)}, s32[256]{0:T(256)}, u32[]{:S(2)}) copy-start(s32[256]{0:T(256)} %param.9) | copy-start | bytes 3076
  11.7 14.4 %collective-permute-start.3 = (bf16[16,16,512]{2,1,0:T(8,128)(2,1)S(1)}, bf16[16,16,512]{2,1,0:T(8,128)(2,1)S(1)}, u32[]{:S(2)}, u32[]{:S(2)}) collective-permute-start(bf16[16,16,512]{2,1,0:T(8,128)(2,1)S(1)} %get-tuple-element.23), channel_id=1, source_target_pairs={{0,15},{1,2},{2,1},{3,4},{4,3},{5,6},{6,5},{7,8},{8,7},{9,10},{10,... | collective-permute-start | bytes 786440 | tf_op jit(solution)/shard_map/ppermute | solution.py:355
  13.7 12.4 %collective-permute-start.5 = (bf16[128,512]{1,0:T(8,128)(2,1)S(1)}, bf16[128,512]{1,0:T(8,128)(2,1)S(1)}, u32[]{:S(2)}, u32[]{:S(2)}) collective-permute-start(bf16[128,512]{1,0:T(8,128)(2,1)S(1)} %get-tuple-element.24), channel_id=1, source_target_pairs={{0,8},{1,9},{2,10},{3,11},{4,12},{5,13},{6,14},{7,15},{8,0},{9,1},... | collective-permute-start | bytes 393224 | tf_op jit(solution)/shard_map/ppermute | solution.py:386
  18.5 7.6 %collective-permute-start.4 = (bf16[128,512]{1,0:T(8,128)(2,1)S(1)}, bf16[128,512]{1,0:T(8,128)(2,1)S(1)}, u32[]{:S(2)}, u32[]{:S(2)}) collective-permute-start(bf16[128,512]{1,0:T(8,128)(2,1)S(1)} %get-tuple-element.19._), channel_id=1, source_target_pairs={{0,16},{1,17},{2,18},{3,19},{4,20},{5,21},{6,22},{7,23},{8,24},{9,... | collective-permute-start | bytes 393224 | tf_op jit(solution)/shard_map/ppermute | solution.py:385
  19.5 1.4 %copy-start.2 = (bf16[16,90,512]{2,0,1:T(8,128)(2,1)S(1)}, bf16[16,90,512]{2,0,1:T(8,128)(2,1)}, u32[]{:S(2)}) copy-start(bf16[16,90,512]{2,0,1:T(8,128)(2,1)} %param.6) | copy-start | bytes 4423684
  26.1 6.3 %copy-start.1 = (bf16[4,512,512]{2,1,0:T(8,128)(2,1)S(1)}, bf16[4,512,512]{2,1,0:T(8,128)(2,1)}, u32[]{:S(2)}) copy-start(bf16[4,512,512]{2,1,0:T(8,128)(2,1)} %weight_hbm.1) | copy-start | bytes 6291460
  32.1 8.1 %collective-permute-start.6 = (bf16[2,512,512]{2,1,0:T(8,128)(2,1)S(1)}, bf16[2,512,512]{2,1,0:T(8,128)(2,1)S(1)}, u32[]{:S(2)}, u32[]{:S(2)}) collective-permute-start(bf16[2,512,512]{2,1,0:T(8,128)(2,1)S(1)} %get-tuple-element.29), channel_id=1, source_target_pairs={{0,16},{1,17},{2,18},{3,19},{4,20},{5,21},{6,22},{7,23},{8,24},{9,... | collective-permute-start | bytes 3145736 | tf_op jit(solution)/shard_map/ppermute | solution.py:389
  63.3 6.8 %collective-permute-start.9 = (bf16[32,512]{1,0:T(8,128)(2,1)S(1)}, bf16[32,512]{1,0:T(8,128)(2,1)S(1)}, u32[]{:S(2)}, u32[]{:S(2)}) collective-permute-start(bf16[32,512]{1,0:T(8,128)(2,1)S(1)} %reduce_sum.12), channel_id=1, source_target_pairs={{0,4},{1,5},{2,6},{3,7},{4,0},{5,1},{6,2},{7,3},{8,12},{9,13},{10,... | collective-permute-start | bytes 98312 | tf_op jit(solution)/shard_map/ppermute | solution.py:393
  64.4 5.7 %collective-permute-start.8 = (bf16[32,512]{1,0:T(8,128)(2,1)S(1)}, bf16[32,512]{1,0:T(8,128)(2,1)S(1)}, u32[]{:S(2)}, u32[]{:S(2)}) collective-permute-start(bf16[32,512]{1,0:T(8,128)(2,1)S(1)} %reduce_sum.12), channel_id=1, source_target_pairs={{0,6},{1,7},{2,4},{3,5},{4,2},{5,3},{6,0},{7,1},{8,14},{9,15},{10,... | collective-permute-start | bytes 98312 | tf_op jit(solution)/shard_map/ppermute | solution.py:393
  66.0 5.3 %collective-permute-start.7 = (bf16[32,512]{1,0:T(8,128)(2,1)S(1)}, bf16[32,512]{1,0:T(8,128)(2,1)S(1)}, u32[]{:S(2)}, u32[]{:S(2)}) collective-permute-start(bf16[32,512]{1,0:T(8,128)(2,1)S(1)} %reduce_sum.12), channel_id=1, source_target_pairs={{0,2},{1,3},{2,0},{3,1},{4,6},{5,7},{6,4},{7,5},{8,10},{9,11},{10,... | collective-permute-start | bytes 98312 | tf_op jit(solution)/shard_map/ppermute | solution.py:393
  89.4 6.3 %collective-permute-start.10 = (bf16[2,512,512]{2,1,0:T(8,128)(2,1)S(1)}, bf16[2,512,512]{2,1,0:T(8,128)(2,1)S(1)}, u32[]{:S(2)}, u32[]{:S(2)}) collective-permute-start(bf16[2,512,512]{2,1,0:T(8,128)(2,1)S(1)} %bitcast.10), channel_id=1, source_target_pairs={{0,16},{1,17},{2,18},{3,19},{4,20},{5,21},{6,22},{7,23},{8,24},{9,... | collective-permute-start | bytes 3145736 | tf_op jit(solution)/shard_map/ppermute | solution.py:399

commit v6 on v5

--- a/solution.py
+++ b/solution.py
@@ -95,8 +95,8 @@
 
 def prepare_kernel(place, basis, reach, act, _, tiles, cells, placed, buffer, sems):
     copies = fetches(act, buffer, sems)
-    length = basis.shape[1]
-    lats = basis.shape[2]
+    length = basis.shape[1] * FILTERS
+    lats = basis.shape[3]
     offset = lax.broadcasted_iota(jnp.int32, (length, lats), 0) // FILTERS
     inside = jnp.abs(offset - REACH) <= reach[...]
     row = lax.broadcasted_iota(jnp.int32, (length, FILTERS * DEPTH), 0)
@@ -104,7 +104,7 @@
     gap = jnp.where(row % FILTERS == col // DEPTH, col % DEPTH + row // FILTERS - 2 * REACH, -1)
 
     def put(t, q, lat):
-        taps = jnp.where(inside, basis[t].astype(F32), 0.0)[:, lat].astype(BF16)
+        taps = jnp.where(inside, basis[t].astype(F32).reshape(length, lats), 0.0)[:, lat].astype(BF16)
         ones = jnp.where(gap == SPAN * q, 1.0, 0.0).astype(BF16)
         return lax.dot_general(taps, ones, (((0,), (0,)), ((), ())), preferred_element_type=F32)
 
@@ -223,27 +223,54 @@
     )(place, tiles, rows, lon_a, lon_b, lat_a, lat_b, cells)
 
 
+def own_part_kernel(place, f_hbm, cells_ref, mine, f, cells, sems):
+    copies = [pltpu.make_async_copy(f_hbm.at[2 * place[0] + j], f.at[j], sems.at[j]) for j in range(2)]
+    copies.append(pltpu.make_async_copy(cells_ref, cells, sems.at[2]))
+    for copy in (copies[2], copies[0], copies[1]):
+        copy.start()
+    copies[2].wait()
+    for j in range(2):
+        copies[j].wait()
+        mine[j] = outer(f[j], cells[...])
+
+
+def spec(space):
+    return pl.BlockSpec(memory_space=space)
+
+
+def own_part(place, f, cells):
+    return pl.pallas_call(
+        own_part_kernel,
+        in_specs=[spec(pltpu.SMEM), spec(pl.ANY), spec(pl.ANY)],
+        out_specs=spec(pltpu.VMEM),
+        out_shape=jax.ShapeDtypeStruct((2, CHANNELS, CHANNELS), F32),
+        scratch_shapes=[
+            pltpu.VMEM((2, ROWS, PAD, CHANNELS), BF16),
+            pltpu.VMEM((ROWS, PAD, CHANNELS), BF16),
+            pltpu.SemaphoreType.DMA((3,)),
+        ],
+        compiler_params=pltpu.CompilerParams(vmem_limit_bytes=16 * MIB),
+        cost_estimate=pl.CostEstimate(flops=4 * ROWS * PAD * CHANNELS**2, bytes_accessed=6_000_000, transcendentals=0),
+        name="own_part",
+    )(place, f, cells)
+
+
 SLAB = 32
 SLABS = PAD // SLAB
 
 
-def remainder_kernel(place, f_hbm, weight_hbm, cells_ref, out, mine, weight, f, cells, stage, weight_sems, f_sems, cells_sem, out_sems):
+def input_kernel(f_hbm, weight_hbm, out, weight, f, stage, weight_sems, f_sems, out_sems):
     loads = [pltpu.make_async_copy(weight_hbm.at[k], weight.at[k], weight_sems.at[k]) for k in range(FILTERS)]
-    slabs = [
-        [
-            pltpu.make_async_copy(f_hbm.at[k, :, pl.ds(SLAB * j, SLAB)], f.at[k, :, pl.ds(SLAB * j, SLAB)], f_sems.at[j, k])
-            for k in range(FILTERS)
-        ]
-        for j in range(SLABS)
-    ]
-    cells_copy = pltpu.make_async_copy(cells_ref, cells, cells_sem)
+    slabs = []
+    for j in range(SLABS):
+        at = pl.ds(SLAB * j, SLAB)
+        slabs.append([pltpu.make_async_copy(f_hbm.at[k, :, at], f.at[k, :, at], f_sems.at[j, k]) for k in range(FILTERS)])
     for k in range(FILTERS):
         slabs[0][k].start()
         loads[k].start()
     for slab in slabs[1:]:
         for copy in slab:
             copy.start()
-    cells_copy.start()
     stores = []
     for j in range(SLABS):
         left = SLAB * j
@@ -261,37 +288,29 @@
         store = pltpu.make_async_copy(stage.at[j, pl.ds(0, cols)], out.at[pl.ds(left, cols)], out_sems.at[j])
         store.start()
         stores.append(store)
-    cells_copy.wait()
-    for j in range(2):
-        mine[j] = outer(f[2 * place[0] + j], cells[...])
     for store in stores:
         store.wait()
 
 
-def remainder(place, f, weight, cells):
-    filtered = (FILTERS, ROWS, PAD, CHANNELS)
-    half = (2, CHANNELS, CHANNELS)
-    spec = lambda space: pl.BlockSpec(memory_space=space)
-    flops = 2 * ROWS * PAD * (FILTERS + 2) * CHANNELS * CHANNELS
+def input_gradient(f, weight):
+    flops = 2 * ROWS * PAD * FILTERS * CHANNELS * CHANNELS
     return pl.pallas_call(
-        remainder_kernel,
-        in_specs=[spec(pltpu.SMEM), spec(pltpu.HBM), spec(pltpu.HBM), spec(pl.ANY)],
-        out_specs=[spec(pl.ANY), spec(pltpu.VMEM)],
-        out_shape=[jax.ShapeDtypeStruct((COLS, ROWS, CHANNELS), BF16), jax.ShapeDtypeStruct(half, F32)],
+        input_kernel,
+        in_specs=[spec(pl.ANY), spec(pltpu.HBM)],
+        out_specs=spec(pl.ANY),
+        out_shape=jax.ShapeDtypeStruct((COLS, ROWS, CHANNELS), BF16),
         scratch_shapes=[
             pltpu.VMEM((FILTERS, CHANNELS, CHANNELS), BF16),
-            pltpu.VMEM(filtered, BF16),
-            pltpu.VMEM((ROWS, PAD, CHANNELS), BF16),
+            pltpu.VMEM((FILTERS, ROWS, PAD, CHANNELS), BF16),
             pltpu.VMEM((SLABS, SLAB, ROWS, CHANNELS), BF16),
             pltpu.SemaphoreType.DMA((FILTERS,)),
             pltpu.SemaphoreType.DMA((SLABS, FILTERS)),
-            pltpu.SemaphoreType.DMA(()),
             pltpu.SemaphoreType.DMA((SLABS,)),
         ],
-        compiler_params=pltpu.CompilerParams(vmem_limit_bytes=24 * MIB),
-        cost_estimate=pl.CostEstimate(flops=flops, bytes_accessed=12_000_000, transcendentals=0),
-        name="remainder",
-    )(place, f, weight, cells)
+        compiler_params=pltpu.CompilerParams(vmem_limit_bytes=20 * MIB),
+        cost_estimate=pl.CostEstimate(flops=flops, bytes_accessed=10_000_000, transcendentals=0),
+        name="input_gradient",
+    )(f, weight)
 
 
 def put_half_kernel(flip, place, half, *rest):
@@ -358,8 +377,8 @@
 
 
 def prepared(place, basis, reach, act, after):
-    taps, lats = basis.shape[2] * FILTERS, basis.shape[3]
-    basis = jnp.transpose(basis, (1, 2, 0, 3)).reshape(TAPS, taps, lats)
+    lats = basis.shape[3]
+    basis = jnp.transpose(basis, (1, 2, 0, 3))
     scratch = [
         pltpu.VMEM((TAPS, lats + 2 * LEAD, FILTERS * DEPTH), F32),
         pltpu.VMEM(act.shape, BF16),
@@ -381,15 +400,19 @@
     odd = lax.axis_index("zl").astype(jnp.int32)
     place = jnp.stack([core, odd, band])
     own, act = jnp.swapaxes(cotangent, 0, 1), jnp.swapaxes(activations, 0, 1)
+    act = pltpu.with_memory_space_constraint(act, pltpu.HBM)
     rows, lon_a, lon_b, wide_a, wide_b = haloes(own, place)
     lat_a = lax.ppermute(wide_a, AXES, LAT_A)
     lat_b = lax.ppermute(wide_b, AXES, LAT_B)
     tiles, cells = prepared(place, basis, reach, act, wide_a)
     f, send = stencil(place, tiles, rows, lon_a, lon_b, lat_a, lat_b, cells)
     got = lax.ppermute(send, AXES, SIBLING)
-    grad_input, mine = remainder(place, f, weight, cells)
+    mine = own_part(place, f, cells)
     half = (mine + got.astype(F32)).astype(BF16)
-    part = lax.optimization_barrier(summed(half.reshape(-1, CHANNELS), 32, BLOCK).astype(BF16))
+    weight = pltpu.with_memory_space_constraint(weight, pltpu.HBM)
+    grad_input = input_gradient(f, weight)
+    part = summed(half.reshape(-1, CHANNELS), 32, BLOCK).astype(BF16)
+    part, grad_input = lax.optimization_barrier((part, grad_input))
     others = [lax.ppermute(part, AXES, along_z(m)).astype(F32) for m in (2, 6, 4)]
     norm_factor = float(ROWS * COLS * LAT * LON) ** (-0.5)
     part = (part.astype(F32) + others[0]) + (others[1] + others[2])

time: 97.6 us -> 93.9 us (0.962)
  blocking collectives: 40.5 us -> 18.2 us
  waiting for transfers between devices: 5.65 us -> 14.4 us
  starting transfers between devices: 23.8 us -> 29.7 us
  Pallas kernels: 22 us -> 24.3 us
  other arithmetic: 0.61 us -> 1.66 us
    all_to_all x1 -> x0, blocking collectives: 22.6 us -> none  [summed(): lax.all_to_all(parts.reshape(groups, -1, CHANNELS), axes, 0, 0, tiled=True)]
    all_to_all x0 -> x1, waiting for transfers between devices: none -> 7.24 us  [summed(): lax.all_to_all(parts.reshape(groups, -1, CHANNELS), axes, 0, 0, tiled=True)]
    all_to_all x0 -> x1, starting transfers between devices: none -> 6.12 us  [summed(): lax.all_to_all(parts.reshape(groups, -1, CHANNELS), axes, 0, 0, tiled=True)]
    ppermute x1, waiting for transfers between devices: 2.64 us -> 4.43 us  [on_device(): lat_b = lax.ppermute(wide_b, AXES, LAT_B)]
    pallas_call x1 -> x2, Pallas kernels: 7.81 us -> 9.57 us  [the longest x1 6.68 us: input_gradient(): pl.pallas_call(input_kernel, in_specs=[spec(pl.ANY), spec(pltpu.HBM)], ou...]
    unnamed x8 -> x10, local copies, waits for them, and re-layouts: 2.75 us -> 4.16 us
    convert_element_type x1, other arithmetic: 0.35 us -> 1.4 us  [on_device(): half = (mine + got.astype(F32)).astype(BF16)]
    reshape x1 -> x0, local copies, waits for them, and re-layouts: 0.98 us -> none  [prepared(): basis = jnp.transpose(basis, (1, 2, 0, 3)).reshape(TAPS, taps, lats)]
  transfers between devices with their start and end apart: 11 -> 12, of which waited for: 4 -> 5; matrix products, arithmetic and copies ran while one was open for 1% -> 0% of each run, Pallas kernels for 14% -> 17%
where the time goes in v6:
time: 93.9 us; the launch traced here: 93.5 us
  starting transfers between devices  29.7 us (32%)
  Pallas kernels  24.3 us (26%)
  blocking collectives  18.2 us (19%)
  waiting for transfers between devices  14.4 us (15%)
  local copies, waits for them, and re-layouts  4.27 us (5%)
  other arithmetic  1.66 us (2%)
  between operations  0.95 us (1%)
    all_to_all x1, blocking collectives, on_device(): lax.all_to_all(jnp.broadcast_to(part, (32, *part.shape)), BLOCK, 0, 0, ti...  18.2 us
    pallas_call x6, Pallas kernels, local(): pl.pallas_call(kernel, in_specs=[pl.BlockSpec(memory_space=pltpu.SMEM)] +...  8.74 us
    ppermute x1, starting transfers between devices, haloes(): edge_b = lax.ppermute(edge_b, AXES, LON_B)  7.42 us
    all_to_all x1, waiting for transfers between devices, summed(): lax.all_to_all(parts.reshape(groups, -1, CHANNELS), axes, 0, 0, tiled=True)  7.24 us
    pallas_call x1, Pallas kernels, input_gradient(): pl.pallas_call(input_kernel, in_specs=[spec(pl.ANY), spec(pltpu.HBM)], ou...  6.68 us
    all_to_all x1, starting transfers between devices, summed(): lax.all_to_all(parts.reshape(groups, -1, CHANNELS), axes, 0, 0, tiled=True)  6.12 us
    pallas_call x1, Pallas kernels, stencil(): pl.pallas_call(stencil_kernel, grid_spec=pltpu.PrefetchScalarGridSpec(num...  5.99 us
    ppermute x3, starting transfers between devices, on_device(): lax.ppermute(part, AXES, along_z(m)).astype(F32)  5.74 us
  transfers between devices with their start and end apart: 12, of which 5 were waited for; matrix products, arithmetic and copies ran while one was open for 0% of the time, Pallas kernels for 17%

profile of v6, /device:TPU:1, one launch (start us, length us, event | category | flops | bytes accessed | tf_op | source)
XLA Modules:
  0.0 93.5 jit_solution(2559004036472284448)
XLA Ops:
  0.6 0.1 pad_add_fusion.place
  0.7 0.0 copy-start.2
  0.7 1.4 %copy-done.2 = bf16[16,90,512]{2,0,1:T(8,128)(2,1)S(1)} copy-done((bf16[16,90,512]{2,0,1:T(8,128)(2,1)S(1)}, bf16[16,90,512]{2,0,1:T(8,128)(2,1)}, u32[]{:S(2)}) %copy-start.2) | copy-done | bytes 1474584
  2.1 0.7 edges.1
  2.8 7.4 %collective-permute-start.1 = (bf16[2,16,512]{2,1,0:T(8,128)(2,1)S(1)}, bf16[2,16,512]{2,1,0:T(8,128)(2,1)S(1)}, u32[]{:S(2)}, u32[]{:S(2)}) collective-permute-start(bf16[2,16,512]{2,1,0:T(8,128)(2,1)S(1)} %get-tuple-element.18), channel_id=1, source_target_pairs={{0,15},{1,2},{2,1},{3,4},{4,3},{5,6},{6,5},{7,8},{8,7},{9,10},{10,... | collective-permute-start | bytes 98312 | tf_op jit(solution)/shard_map/ppermute | solution.py:372
  10.2 0.0 collective-permute-start
  10.2 1.5 %collective-permute-start.2 = (bf16[16,16,512]{2,1,0:T(8,128)(2,1)S(1)}, bf16[16,16,512]{2,1,0:T(8,128)(2,1)S(1)}, u32[]{:S(2)}, u32[]{:S(2)}) collective-permute-start(bf16[16,16,512]{2,1,0:T(8,128)(2,1)S(1)} %get-tuple-element.22), channel_id=1, source_target_pairs={{0,1},{1,0},{2,3},{3,2},{4,5},{5,4},{6,7},{7,6},{8,9},{9,8},{10,11... | collective-permute-start | bytes 786440 | tf_op jit(solution)/shard_map/ppermute | solution.py:373
  11.7 0.0 copy-start.3
  11.7 0.0 copy-start.4
  11.7 0.1 collective-permute-start.3
  11.8 1.3 %turn.1 = (bf16[16,96,512]{2,1,0:T(8,128)(2,1)S(1)}, bf16[2,96,512]{2,1,0:T(8,128)(2,1)S(1)}) custom-call(s32[3]{0:T(128)S(1)} %pad_add_fusion.place, bf16[90,16,512]{2,1,0:T(8,128)(2,1)S(1)} %bitcast.13, bf16[2,16,512]{2,1,0:T(8,128)(2,1)S(1)} %get-tuple-element.16._), custom_call_target="tpu_custom_call" | custom-call | flops 4000000000 | bytes 2000000 | tf_op jit(solution)/shard_map/turn/pallas_call | solution.py:29
  13.1 0.0 collective-permute-done.1.got_b
  13.1 0.0 collective-permute-done.got_a
  13.1 0.6 widen.1
  13.7 4.8 %collective-permute-start.5 = (bf16[128,512]{1,0:T(8,128)(2,1)S(1)}, bf16[128,512]{1,0:T(8,128)(2,1)S(1)}, u32[]{:S(2)}, u32[]{:S(2)}) collective-permute-start(bf16[128,512]{1,0:T(8,128)(2,1)S(1)} %get-tuple-element.24), channel_id=1, source_target_pairs={{0,8},{1,9},{2,10},{3,11},{4,12},{5,13},{6,14},{7,15},{8,0},{9,1},... | collective-permute-start | bytes 393224 | tf_op jit(solution)/shard_map/ppermute | solution.py:406
  18.5 0.0 collective-permute-start.4
  18.5 0.0 copy-done.3
  18.5 0.0 copy-done.4
  18.5 3.1 %prepare.1 = (bf16[16,192,256]{2,1,0:T(8,128)(2,1)S(1)}, bf16[16,96,512]{2,1,0:T(8,128)(2,1)S(1)}) custom-call(s32[3]{0:T(128)S(1)} %pad_add_fusion.place, bf16[3,33,4,256]{3,2,1,0:T(4,128)(2,1)S(1)} %bitcast.14, s32[1,256]{1,0:T(1,128)S(1)} %bitcast.15, bf16[90,16,512]{2,1,0:T(8,128)(2,1)} %bitcast.16, bf16[128,512]{1,0:T(8,128)(2,1)S(1)} %get-tuple-element.19._), custom_call_target="tpu_custom_call" | custom-call | flops 1000000000 | bytes 2000000 | tf_op jit(solution)/shard_map/prepare/pallas_call | solution.py:29
  21.6 4.4 %collective-permute-done.5.lat_b = bf16[128,512]{1,0:T(8,128)(2,1)S(1)} collective-permute-done((bf16[128,512]{1,0:T(8,128)(2,1)S(1)}, bf16[128,512]{1,0:T(8,128)(2,1)S(1)}, u32[]{:S(2)}, u32[]{:S(2)}) %collective-permute-start.5) | collective-permute-done | bytes 131104 | tf_op jit(solution)/shard_map/ppermute | solution.py:406
  26.0 0.0 collective-permute-done.4.lat_a
  26.0 0.0 collective-permute-done.2.lon_a
  26.0 0.0 collective-permute-done.3.lon_b
  26.1 6.0 %stencil.1 = (bf16[4,16,96,512]{3,2,1,0:T(8,128)(2,1)S(1)}, bf16[2,512,512]{2,1,0:T(8,128)(2,1)S(1)}) custom-call(s32[3]{0:T(128)S(1)} %pad_add_fusion.place, bf16[16,192,256]{2,1,0:T(8,128)(2,1)S(1)} %get-tuple-element.20.tiles, bf16[16,96,512]{2,1,0:T(8,128)(2,1)S(1)} %get-tuple-element.21.rows, bf16[16,16,512]{2,1,0:T(8,128)(2,1)S(1)} %collective-permute-done.2.lon_a, ...), custom_call_target="tpu_custom_call" | custom-call | tf_op jit(solution)/shard_map/stencil/pallas_call | solution.py:194
  32.0 0.0 copy-start
  32.1 0.1 collective-permute-start.6
  32.2 2.9 %own_part.1 = f32[2,512,512]{2,1,0:T(8,128)S(1)} custom-call(s32[3]{0:T(128)S(1)} %pad_add_fusion.place, bf16[4,16,96,512]{3,2,1,0:T(8,128)(2,1)S(1)} %get-tuple-element.26.f_hbm, bf16[16,96,512]{2,1,0:T(8,128)(2,1)S(1)} %get-tuple-element.25.cells_ref), custom_call_target="tpu_custom_call" | custom-call | flops 1610612736 | bytes 6000000 | tf_op jit(solution)/shard_map/own_part/pallas_call | solution.py:242
  35.1 0.0 copy-done
  35.1 0.0 collective-permute-done.6
  35.1 1.4 %add_convert_fusion = bf16[2,512,512]{2,1,0:T(8,128)(2,1)} fusion(f32[2,512,512]{2,1,0:T(8,128)S(1)} %own_part.1, bf16[2,512,512]{2,1,0:T(8,128)(2,1)S(1)} %collective-permute-done.6), kind=kLoop, calls=%fused_computation | loop fusion | flops 1572864 | bytes 4194304 | tf_op jit(solution)/shard_map/convert_element_type | solution.py:411
  36.5 6.1 %all-to-all-start = ((bf16[32,32,512]{2,1,0:T(8,128)(2,1)}), bf16[32,32,512]{2,1,0:T(8,128)(2,1)S(1)}, u32[]{:S(2)}, u32[]{:S(2)}) async-start(bf16[32,32,512]{2,1,0:T(8,128)(2,1)} %bitcast.7), calls=%async_computation | async-start | bytes 2097152 | tf_op jit(solution)/shard_map/all_to_all | solution.py:393
  42.6 0.0 copy-start.1
  42.6 2.8 %copy-done.1 = bf16[4,16,96,512]{3,2,1,0:T(8,128)(2,1)S(1)} copy-done((bf16[4,16,96,512]{3,2,1,0:T(8,128)(2,1)S(1)}, bf16[4,16,96,512]{3,2,1,0:T(8,128)(2,1)}, u32[]{:S(2)}) %copy-start.1) | copy-done | bytes 6291480
  45.4 6.7 %input_gradient.1 = bf16[90,16,512]{2,1,0:T(8,128)(2,1)} custom-call(bf16[4,16,96,512]{3,2,1,0:T(8,128)(2,1)S(1)} %copy-done.1, bf16[4,512,512]{2,1,0:T(8,128)(2,1)} %weight_hbm.1), custom_call_target="tpu_custom_call" | custom-call | flops 3221225472 | bytes 10000000 | tf_op jit(solution)/shard_map/input_gradient/pallas_call | solution.py:297
  52.1 7.2 %all-to-all-done = bf16[32,32,512]{2,1,0:T(8,128)(2,1)S(1)} async-done(((bf16[32,32,512]{2,1,0:T(8,128)(2,1)}), bf16[32,32,512]{2,1,0:T(8,128)(2,1)S(1)}, u32[]{:S(2)}, u32[]{:S(2)}) %all-to-all-start) | async-done | bytes 1048608 | tf_op jit(solution)/shard_map/all_to_all | solution.py:393
  59.3 0.2 reduce_sum.12
  59.5 0.3 collective-permute-start.9
  59.8 1.3 %collective-permute-start.8 = (bf16[32,512]{1,0:T(8,128)(2,1)S(1)}, bf16[32,512]{1,0:T(8,128)(2,1)S(1)}, u32[]{:S(2)}, u32[]{:S(2)}) collective-permute-start(bf16[32,512]{1,0:T(8,128)(2,1)S(1)} %reduce_sum.12), channel_id=1, source_target_pairs={{0,6},{1,7},{2,4},{3,5},{4,2},{5,3},{6,0},{7,1},{8,14},{9,15},{10,... | collective-permute-start | bytes 98312 | tf_op jit(solution)/shard_map/ppermute | solution.py:416
  61.1 4.1 %collective-permute-start.7 = (bf16[32,512]{1,0:T(8,128)(2,1)S(1)}, bf16[32,512]{1,0:T(8,128)(2,1)S(1)}, u32[]{:S(2)}, u32[]{:S(2)}) collective-permute-start(bf16[32,512]{1,0:T(8,128)(2,1)S(1)} %reduce_sum.12), channel_id=1, source_target_pairs={{0,2},{1,3},{2,0},{3,1},{4,6},{5,7},{6,4},{7,5},{8,10},{9,11},{10,... | collective-permute-start | bytes 98312 | tf_op jit(solution)/shard_map/ppermute | solution.py:416
  65.2 1.1 %collective-permute-done.9 = bf16[32,512]{1,0:T(8,128)(2,1)S(1)} collective-permute-done((bf16[32,512]{1,0:T(8,128)(2,1)S(1)}, bf16[32,512]{1,0:T(8,128)(2,1)S(1)}, u32[]{:S(2)}, u32[]{:S(2)}) %collective-permute-start.9) | collective-permute-done | bytes 32800 | tf_op jit(solution)/shard_map/ppermute | solution.py:416
  66.3 0.0 collective-permute-done.8
  66.3 0.9 collective-permute-done.7
  67.2 0.1 broadcast_in_dim.3
  67.3 18.2 %all_to_all.10 = bf16[32,32,512]{2,1,0:T(8,128)(2,1)S(1)} all-to-all(bf16[32,32,512]{2,1,0:T(8,128)(2,1)S(1)} %broadcast_in_dim.3), channel_id=1, replica_groups=mesh['y'=4,'xh'=2,'core'=2,'xl'=2,'zh'=4,'zl'=2] {'y','xh','xl','zl'}, dimensions={0} | all-to-all | bytes 2097152 | tf_op jit(solution)/shard_map/all_to_all | solution.py:420
  85.6 4.0 %collective-permute-start.10 = (bf16[2,512,512]{2,1,0:T(8,128)(2,1)S(1)}, bf16[2,512,512]{2,1,0:T(8,128)(2,1)S(1)}, u32[]{:S(2)}, u32[]{:S(2)}) collective-permute-start(bf16[2,512,512]{2,1,0:T(8,128)(2,1)S(1)} %bitcast.10), channel_id=1, source_target_pairs={{0,16},{1,17},{2,18},{3,19},{4,20},{5,21},{6,22},{7,23},{8,24},{9,... | collective-permute-start | bytes 3145736 | tf_op jit(solution)/shard_map/ppermute | solution.py:422
  89.5 1.5 %put_half.2.rest_0_ = bf16[4,512,512]{2,1,0:T(8,128)(2,1)} custom-call(s32[3]{0:T(128)S(1)} %pad_add_fusion.place, bf16[2,512,512]{2,1,0:T(8,128)(2,1)S(1)} %bitcast.11), custom_call_target="tpu_custom_call" | custom-call | tf_op jit(solution)/shard_map/put_half/pallas_call | solution.py:29
  91.1 0.7 collective-permute-done.10.half
  91.8 1.5 %put_half.3 = bf16[4,512,512]{2,1,0:T(8,128)(2,1)} custom-call(s32[3]{0:T(128)S(1)} %pad_add_fusion.place, bf16[2,512,512]{2,1,0:T(8,128)(2,1)S(1)} %collective-permute-done.10.half, bf16[4,512,512]{2,1,0:T(8,128)(2,1)} %put_half.2.rest_0_), custom_call_target="tpu_custom_call", output_to_operand_aliasing={{}: (2, {})} | custom-call | tf_op jit(solution)/shard_map/put_half/pallas_call | solution.py:29
  (1 shorter events, 0.0 us)
Async XLA Ops:
  0.7 1.4 %copy-start.2 = (bf16[16,90,512]{2,0,1:T(8,128)(2,1)S(1)}, bf16[16,90,512]{2,0,1:T(8,128)(2,1)}, u32[]{:S(2)}) copy-start(bf16[16,90,512]{2,0,1:T(8,128)(2,1)} %param.5) | copy-start | bytes 4423684
  2.8 10.3 %collective-permute-start.1 = (bf16[2,16,512]{2,1,0:T(8,128)(2,1)S(1)}, bf16[2,16,512]{2,1,0:T(8,128)(2,1)S(1)}, u32[]{:S(2)}, u32[]{:S(2)}) collective-permute-start(bf16[2,16,512]{2,1,0:T(8,128)(2,1)S(1)} %get-tuple-element.18), channel_id=1, source_target_pairs={{0,15},{1,2},{2,1},{3,4},{4,3},{5,6},{6,5},{7,8},{8,7},{9,10},{10,... | collective-permute-start | bytes 98312 | tf_op jit(solution)/shard_map/ppermute | solution.py:372
  10.2 2.9 %collective-permute-start = (bf16[2,16,512]{2,1,0:T(8,128)(2,1)S(1)}, bf16[2,16,512]{2,1,0:T(8,128)(2,1)S(1)}, u32[]{:S(2)}, u32[]{:S(2)}) collective-permute-start(bf16[2,16,512]{2,1,0:T(8,128)(2,1)S(1)} %get-tuple-element.16._), channel_id=1, source_target_pairs={{0,1},{1,0},{2,3},{3,2},{4,5},{5,4},{6,7},{7,6},{8,9},{9,8},{10,11... | collective-permute-start | bytes 98312 | tf_op jit(solution)/shard_map/ppermute | solution.py:371
  10.2 15.9 %collective-permute-start.2 = (bf16[16,16,512]{2,1,0:T(8,128)(2,1)S(1)}, bf16[16,16,512]{2,1,0:T(8,128)(2,1)S(1)}, u32[]{:S(2)}, u32[]{:S(2)}) collective-permute-start(bf16[16,16,512]{2,1,0:T(8,128)(2,1)S(1)} %get-tuple-element.22), channel_id=1, source_target_pairs={{0,1},{1,0},{2,3},{3,2},{4,5},{5,4},{6,7},{7,6},{8,9},{9,8},{10,11... | collective-permute-start | bytes 786440 | tf_op jit(solution)/shard_map/ppermute | solution.py:373
  11.7 6.8 %copy-start.3 = (bf16[4,3,33,256]{3,0,2,1:T(4,128)(2,1)S(1)}, bf16[4,3,33,256]{3,0,2,1:T(4,128)(2,1)}, u32[]{:S(2)}) copy-start(bf16[4,3,33,256]{3,0,2,1:T(4,128)(2,1)} %param.8) | copy-start | bytes 608260
  11.7 6.8 %copy-start.4 = (s32[256]{0:T(256)S(1)}, s32[256]{0:T(256)}, u32[]{:S(2)}) copy-start(s32[256]{0:T(256)} %param.9) | copy-start | bytes 3076
  11.7 14.4 %collective-permute-start.3 = (bf16[16,16,512]{2,1,0:T(8,128)(2,1)S(1)}, bf16[16,16,512]{2,1,0:T(8,128)(2,1)S(1)}, u32[]{:S(2)}, u32[]{:S(2)}) collective-permute-start(bf16[16,16,512]{2,1,0:T(8,128)(2,1)S(1)} %get-tuple-element.23), channel_id=1, source_target_pairs={{0,15},{1,2},{2,1},{3,4},{4,3},{5,6},{6,5},{7,8},{8,7},{9,10},{10,... | collective-permute-start | bytes 786440 | tf_op jit(solution)/shard_map/ppermute | solution.py:374
  13.7 12.4 %collective-permute-start.5 = (bf16[128,512]{1,0:T(8,128)(2,1)S(1)}, bf16[128,512]{1,0:T(8,128)(2,1)S(1)}, u32[]{:S(2)}, u32[]{:S(2)}) collective-permute-start(bf16[128,512]{1,0:T(8,128)(2,1)S(1)} %get-tuple-element.24), channel_id=1, source_target_pairs={{0,8},{1,9},{2,10},{3,11},{4,12},{5,13},{6,14},{7,15},{8,0},{9,1},... | collective-permute-start | bytes 393224 | tf_op jit(solution)/shard_map/ppermute | solution.py:406
  18.5 7.6 %collective-permute-start.4 = (bf16[128,512]{1,0:T(8,128)(2,1)S(1)}, bf16[128,512]{1,0:T(8,128)(2,1)S(1)}, u32[]{:S(2)}, u32[]{:S(2)}) collective-permute-start(bf16[128,512]{1,0:T(8,128)(2,1)S(1)} %get-tuple-element.19._), channel_id=1, source_target_pairs={{0,16},{1,17},{2,18},{3,19},{4,20},{5,21},{6,22},{7,23},{8,24},{9,... | collective-permute-start | bytes 393224 | tf_op jit(solution)/shard_map/ppermute | solution.py:405
  32.0 3.0 %copy-start = (bf16[4,16,96,512]{3,2,1,0:T(8,128)(2,1)}, bf16[4,16,96,512]{3,2,1,0:T(8,128)(2,1)S(1)}, u32[]{:S(2)}) copy-start(bf16[4,16,96,512]{3,2,1,0:T(8,128)(2,1)S(1)} %get-tuple-element.26.f_hbm) | copy-start | bytes 18874372
  32.1 3.0 %collective-permute-start.6 = (bf16[2,512,512]{2,1,0:T(8,128)(2,1)S(1)}, bf16[2,512,512]{2,1,0:T(8,128)(2,1)S(1)}, u32[]{:S(2)}, u32[]{:S(2)}) collective-permute-start(bf16[2,512,512]{2,1,0:T(8,128)(2,1)S(1)} %get-tuple-element.27), channel_id=1, source_target_pairs={{0,16},{1,17},{2,18},{3,19},{4,20},{5,21},{6,22},{7,23},{8,24},{9,... | collective-permute-start | bytes 3145736 | tf_op jit(solution)/shard_map/ppermute | solution.py:409
  36.5 22.8 %all-to-all-start = ((bf16[32,32,512]{2,1,0:T(8,128)(2,1)}), bf16[32,32,512]{2,1,0:T(8,128)(2,1)S(1)}, u32[]{:S(2)}, u32[]{:S(2)}) async-start(bf16[32,32,512]{2,1,0:T(8,128)(2,1)} %bitcast.7), calls=%async_computation | async-start | bytes 2097152 | tf_op jit(solution)/shard_map/all_to_all | solution.py:393
  42.6 2.8 %copy-start.1 = (bf16[4,16,96,512]{3,2,1,0:T(8,128)(2,1)S(1)}, bf16[4,16,96,512]{3,2,1,0:T(8,128)(2,1)}, u32[]{:S(2)}) copy-start(bf16[4,16,96,512]{3,2,1,0:T(8,128)(2,1)} %copy-done) | copy-start | bytes 18874372
  59.5 6.9 %collective-permute-start.9 = (bf16[32,512]{1,0:T(8,128)(2,1)S(1)}, bf16[32,512]{1,0:T(8,128)(2,1)S(1)}, u32[]{:S(2)}, u32[]{:S(2)}) collective-permute-start(bf16[32,512]{1,0:T(8,128)(2,1)S(1)} %reduce_sum.12), channel_id=1, source_target_pairs={{0,4},{1,5},{2,6},{3,7},{4,0},{5,1},{6,2},{7,3},{8,12},{9,13},{10,... | collective-permute-start | bytes 98312 | tf_op jit(solution)/shard_map/ppermute | solution.py:416
  59.8 6.5 %collective-permute-start.8 = (bf16[32,512]{1,0:T(8,128)(2,1)S(1)}, bf16[32,512]{1,0:T(8,128)(2,1)S(1)}, u32[]{:S(2)}, u32[]{:S(2)}) collective-permute-start(bf16[32,512]{1,0:T(8,128)(2,1)S(1)} %reduce_sum.12), channel_id=1, source_target_pairs={{0,6},{1,7},{2,4},{3,5},{4,2},{5,3},{6,0},{7,1},{8,14},{9,15},{10,... | collective-permute-start | bytes 98312 | tf_op jit(solution)/shard_map/ppermute | solution.py:416
  61.1 6.1 %collective-permute-start.7 = (bf16[32,512]{1,0:T(8,128)(2,1)S(1)}, bf16[32,512]{1,0:T(8,128)(2,1)S(1)}, u32[]{:S(2)}, u32[]{:S(2)}) collective-permute-start(bf16[32,512]{1,0:T(8,128)(2,1)S(1)} %reduce_sum.12), channel_id=1, source_target_pairs={{0,2},{1,3},{2,0},{3,1},{4,6},{5,7},{6,4},{7,5},{8,10},{9,11},{10,... | collective-permute-start | bytes 98312 | tf_op jit(solution)/shard_map/ppermute | solution.py:416
  85.6 6.3 %collective-permute-start.10 = (bf16[2,512,512]{2,1,0:T(8,128)(2,1)S(1)}, bf16[2,512,512]{2,1,0:T(8,128)(2,1)S(1)}, u32[]{:S(2)}, u32[]{:S(2)}) collective-permute-start(bf16[2,512,512]{2,1,0:T(8,128)(2,1)S(1)} %bitcast.10), channel_id=1, source_target_pairs={{0,16},{1,17},{2,18},{3,19},{4,20},{5,21},{6,22},{7,23},{8,24},{9,... | collective-permute-start | bytes 3145736 | tf_op jit(solution)/shard_map/ppermute | solution.py:422

commit v7 on v6

--- a/solution.py
+++ b/solution.py
@@ -134,7 +134,7 @@
     return lax.dot_general(f, cells, (((0,), (0,)), ((), ())), preferred_element_type=F32)
 
 
-def stencil_kernel(place, tiles, rows, lon_a, lon_b, lat_a, lat_b, cells_ref, f_out, send, low, high, held, cells, sem, f_sems):
+def stencil_kernel(place, tiles, rows, lon_b, lon_a, lat_a, lat_b, cells_ref, f_out, send, low, high, held, cells, sem, f_sems):
     step = pl.program_id(0)
     stores = [
         pltpu.make_async_copy(held.at[:, pl.ds(GROUP * i, GROUP)], f_out.at[:, pl.ds(GROUP * i, GROUP)], f_sems.at[i])
@@ -198,7 +198,7 @@
             grid=(STEPS + 2,),
             in_specs=[
                 pl.BlockSpec((GROUP, FILTERS * HALF, DEPTH), lambda i, c: (jnp.minimum(i, STEPS - 1), 0, 0)),
-                *[whole(a) for a in (rows, lon_a, lon_b, lat_a, lat_b)],
+                *[whole(a) for a in (rows, lon_b, lon_a, lat_a, lat_b)],
                 pl.BlockSpec(memory_space=pl.ANY),
             ],
             out_specs=[
@@ -220,7 +220,7 @@
         ],
         compiler_params=pltpu.CompilerParams(vmem_limit_bytes=30 * MIB),
         name="stencil",
-    )(place, tiles, rows, lon_a, lon_b, lat_a, lat_b, cells)
+    )(place, tiles, rows, lon_b, lon_a, lat_a, lat_b, cells)
 
 
 def own_part_kernel(place, f_hbm, cells_ref, mine, f, cells, sems):
@@ -365,7 +365,7 @@
     slab, edge, wide = (REACH, ROWS, CHANNELS), (2, REACH, CHANNELS), (WIDE, CHANNELS)
     slab_a, slab_b, edge_a, edge_b = local(edges_kernel, "edges", [slab, slab, edge, edge], [place, own])
     rows, middle = local(
-        turn_kernel, "turn", [(ROWS, PAD, CHANNELS), (2, PAD, CHANNELS)], [place, own, edge_a],
+        turn_kernel, "turn", [(ROWS, PAD, CHANNELS), (2, PAD, CHANNELS)], [place, own, edge_b],
         [pltpu.VMEM(own.shape, BF16), pltpu.SemaphoreType.DMA((PAD // 16,))], {1: pltpu.HBM, 2: pl.ANY}, cost=4_000_000_000,
     )
     edge_a = lax.ppermute(edge_a, AXES, LON_A)

time: 93.9 us -> 93.3 us (level)
  starting transfers between devices: 29.7 us -> 28.3 us
  waiting for transfers between devices: 14.4 us -> 15.6 us
    ppermute x1, starting transfers between devices: 0.01 us -> 2.55 us  [haloes(): edge_a = lax.ppermute(edge_a, AXES, LON_A)]
    ppermute x1, starting transfers between devices: 7.42 us -> 5.59 us  [haloes(): edge_b = lax.ppermute(edge_b, AXES, LON_B)]
    ppermute x1, starting transfers between devices: 1.46 us -> 0.01 us  [haloes(): lon_a = lax.ppermute(slab_a, AXES, LON_A)]
where the time goes in v7:
time: 93.3 us; the launch traced here: 93 us
  starting transfers between devices  28.3 us (30%)
  Pallas kernels  24.3 us (26%)
  blocking collectives  17.9 us (19%)
  waiting for transfers between devices  15.6 us (17%)
  local copies, waits for them, and re-layouts  4.27 us (5%)
  other arithmetic  1.66 us (2%)
  between operations  0.95 us (1%)
    all_to_all x1, blocking collectives, on_device(): lax.all_to_all(jnp.broadcast_to(part, (32, *part.shape)), BLOCK, 0, 0, ti...  17.9 us
    pallas_call x6, Pallas kernels, local(): pl.pallas_call(kernel, in_specs=[pl.BlockSpec(memory_space=pltpu.SMEM)] +...  8.74 us
    all_to_all x1, waiting for transfers between devices, summed(): lax.all_to_all(parts.reshape(groups, -1, CHANNELS), axes, 0, 0, tiled=True)  7.24 us
    pallas_call x1, Pallas kernels, input_gradient(): pl.pallas_call(input_kernel, in_specs=[spec(pl.ANY), spec(pltpu.HBM)], ou...  6.68 us
    all_to_all x1, starting transfers between devices, summed(): lax.all_to_all(parts.reshape(groups, -1, CHANNELS), axes, 0, 0, tiled=True)  6.12 us
    pallas_call x1, Pallas kernels, stencil(): pl.pallas_call(stencil_kernel, grid_spec=pltpu.PrefetchScalarGridSpec(num...  5.99 us
    ppermute x3, starting transfers between devices, on_device(): lax.ppermute(part, AXES, along_z(m)).astype(F32)  5.74 us
    ppermute x1, starting transfers between devices, haloes(): edge_b = lax.ppermute(edge_b, AXES, LON_B)  5.59 us
  transfers between devices with their start and end apart: 12, of which 5 were waited for; matrix products, arithmetic and copies ran while one was open for 0% of the time, Pallas kernels for 17%

profile of v7, /device:TPU:1, one launch (start us, length us, event | category | flops | bytes accessed | tf_op | source)
XLA Modules:
  0.0 93.0 jit_solution(13229464931472006440)
XLA Ops:
  0.6 0.1 pad_add_fusion.place
  0.7 0.0 copy-start.2
  0.7 1.4 %copy-done.2 = bf16[16,90,512]{2,0,1:T(8,128)(2,1)S(1)} copy-done((bf16[16,90,512]{2,0,1:T(8,128)(2,1)S(1)}, bf16[16,90,512]{2,0,1:T(8,128)(2,1)}, u32[]{:S(2)}) %copy-start.2) | copy-done | bytes 1474584
  2.1 0.7 edges.1
  2.8 2.6 %collective-permute-start = (bf16[2,16,512]{2,1,0:T(8,128)(2,1)S(1)}, bf16[2,16,512]{2,1,0:T(8,128)(2,1)S(1)}, u32[]{:S(2)}, u32[]{:S(2)}) collective-permute-start(bf16[2,16,512]{2,1,0:T(8,128)(2,1)S(1)} %get-tuple-element.18), channel_id=1, source_target_pairs={{0,1},{1,0},{2,3},{3,2},{4,5},{5,4},{6,7},{7,6},{8,9},{9,8},{10,11... | collective-permute-start | bytes 98312 | tf_op jit(solution)/shard_map/ppermute | solution.py:371
  5.3 5.6 %collective-permute-start.1 = (bf16[2,16,512]{2,1,0:T(8,128)(2,1)S(1)}, bf16[2,16,512]{2,1,0:T(8,128)(2,1)S(1)}, u32[]{:S(2)}, u32[]{:S(2)}) collective-permute-start(bf16[2,16,512]{2,1,0:T(8,128)(2,1)S(1)} %get-tuple-element.16._), channel_id=1, source_target_pairs={{0,15},{1,2},{2,1},{3,4},{4,3},{5,6},{6,5},{7,8},{8,7},{9,10},{10,... | collective-permute-start | bytes 98312 | tf_op jit(solution)/shard_map/ppermute | solution.py:372
  10.9 0.0 collective-permute-start.2
  10.9 0.0 copy-start.3
  11.0 0.0 copy-start.4
  11.0 0.0 collective-permute-start.3
  11.0 1.3 %turn.1 = (bf16[16,96,512]{2,1,0:T(8,128)(2,1)S(1)}, bf16[2,96,512]{2,1,0:T(8,128)(2,1)S(1)}) custom-call(s32[3]{0:T(128)S(1)} %pad_add_fusion.place, bf16[90,16,512]{2,1,0:T(8,128)(2,1)S(1)} %bitcast.13, bf16[2,16,512]{2,1,0:T(8,128)(2,1)S(1)} %get-tuple-element.16._), custom_call_target="tpu_custom_call" | custom-call | flops 4000000000 | bytes 2000000 | tf_op jit(solution)/shard_map/turn/pallas_call | solution.py:29
  12.3 0.0 collective-permute-done.got_a
  12.3 0.0 collective-permute-done.1.got_b
  12.3 0.6 widen.1
  12.9 4.2 %collective-permute-start.5 = (bf16[128,512]{1,0:T(8,128)(2,1)S(1)}, bf16[128,512]{1,0:T(8,128)(2,1)S(1)}, u32[]{:S(2)}, u32[]{:S(2)}) collective-permute-start(bf16[128,512]{1,0:T(8,128)(2,1)S(1)} %get-tuple-element.24), channel_id=1, source_target_pairs={{0,8},{1,9},{2,10},{3,11},{4,12},{5,13},{6,14},{7,15},{8,0},{9,1},... | collective-permute-start | bytes 393224 | tf_op jit(solution)/shard_map/ppermute | solution.py:406
  17.0 0.0 collective-permute-start.4
  17.0 0.0 copy-done.3
  17.0 0.0 copy-done.4
  17.1 3.1 %prepare.1 = (bf16[16,192,256]{2,1,0:T(8,128)(2,1)S(1)}, bf16[16,96,512]{2,1,0:T(8,128)(2,1)S(1)}) custom-call(s32[3]{0:T(128)S(1)} %pad_add_fusion.place, bf16[3,33,4,256]{3,2,1,0:T(4,128)(2,1)S(1)} %bitcast.14, s32[1,256]{1,0:T(1,128)S(1)} %bitcast.15, bf16[90,16,512]{2,1,0:T(8,128)(2,1)} %bitcast.16, bf16[128,512]{1,0:T(8,128)(2,1)S(1)} %get-tuple-element.19._), custom_call_target="tpu_custom_call" | custom-call | flops 1000000000 | bytes 2000000 | tf_op jit(solution)/shard_map/prepare/pallas_call | solution.py:29
  20.2 5.1 %collective-permute-done.5.lat_b = bf16[128,512]{1,0:T(8,128)(2,1)S(1)} collective-permute-done((bf16[128,512]{1,0:T(8,128)(2,1)S(1)}, bf16[128,512]{1,0:T(8,128)(2,1)S(1)}, u32[]{:S(2)}, u32[]{:S(2)}) %collective-permute-start.5) | collective-permute-done | bytes 131104 | tf_op jit(solution)/shard_map/ppermute | solution.py:406
  25.3 0.0 collective-permute-done.4.lat_a
  25.3 0.0 collective-permute-done.2.lon_b
  25.3 0.0 collective-permute-done.3.lon_a
  25.3 6.0 %stencil.1 = (bf16[4,16,96,512]{3,2,1,0:T(8,128)(2,1)S(1)}, bf16[2,512,512]{2,1,0:T(8,128)(2,1)S(1)}) custom-call(s32[3]{0:T(128)S(1)} %pad_add_fusion.place, bf16[16,192,256]{2,1,0:T(8,128)(2,1)S(1)} %get-tuple-element.20.tiles, bf16[16,96,512]{2,1,0:T(8,128)(2,1)S(1)} %get-tuple-element.21.rows, bf16[16,16,512]{2,1,0:T(8,128)(2,1)S(1)} %collective-permute-done.2.lon_b, ...), custom_call_target="tpu_custom_call" | custom-call | tf_op jit(solution)/shard_map/stencil/pallas_call | solution.py:194
  31.3 0.0 copy-start
  31.3 0.1 collective-permute-start.6
  31.4 2.9 %own_part.1 = f32[2,512,512]{2,1,0:T(8,128)S(1)} custom-call(s32[3]{0:T(128)S(1)} %pad_add_fusion.place, bf16[4,16,96,512]{3,2,1,0:T(8,128)(2,1)S(1)} %get-tuple-element.26.f_hbm, bf16[16,96,512]{2,1,0:T(8,128)(2,1)S(1)} %get-tuple-element.25.cells_ref), custom_call_target="tpu_custom_call" | custom-call | flops 1610612736 | bytes 6000000 | tf_op jit(solution)/shard_map/own_part/pallas_call | solution.py:242
  34.3 0.0 copy-done
  34.3 0.0 collective-permute-done.6
  34.3 1.4 %add_convert_fusion = bf16[2,512,512]{2,1,0:T(8,128)(2,1)} fusion(f32[2,512,512]{2,1,0:T(8,128)S(1)} %own_part.1, bf16[2,512,512]{2,1,0:T(8,128)(2,1)S(1)} %collective-permute-done.6), kind=kLoop, calls=%fused_computation | loop fusion | flops 1572864 | bytes 4194304 | tf_op jit(solution)/shard_map/convert_element_type | solution.py:411
  35.7 6.1 %all-to-all-start = ((bf16[32,32,512]{2,1,0:T(8,128)(2,1)}), bf16[32,32,512]{2,1,0:T(8,128)(2,1)S(1)}, u32[]{:S(2)}, u32[]{:S(2)}) async-start(bf16[32,32,512]{2,1,0:T(8,128)(2,1)} %bitcast.7), calls=%async_computation | async-start | bytes 2097152 | tf_op jit(solution)/shard_map/all_to_all | solution.py:393
  41.9 0.0 copy-start.1
  41.9 2.8 %copy-done.1 = bf16[4,16,96,512]{3,2,1,0:T(8,128)(2,1)S(1)} copy-done((bf16[4,16,96,512]{3,2,1,0:T(8,128)(2,1)S(1)}, bf16[4,16,96,512]{3,2,1,0:T(8,128)(2,1)}, u32[]{:S(2)}) %copy-start.1) | copy-done | bytes 6291480
  44.7 6.7 %input_gradient.1 = bf16[90,16,512]{2,1,0:T(8,128)(2,1)} custom-call(bf16[4,16,96,512]{3,2,1,0:T(8,128)(2,1)S(1)} %copy-done.1, bf16[4,512,512]{2,1,0:T(8,128)(2,1)} %weight_hbm.1), custom_call_target="tpu_custom_call" | custom-call | flops 3221225472 | bytes 10000000 | tf_op jit(solution)/shard_map/input_gradient/pallas_call | solution.py:297
  51.3 7.2 %all-to-all-done = bf16[32,32,512]{2,1,0:T(8,128)(2,1)S(1)} async-done(((bf16[32,32,512]{2,1,0:T(8,128)(2,1)}), bf16[32,32,512]{2,1,0:T(8,128)(2,1)S(1)}, u32[]{:S(2)}, u32[]{:S(2)}) %all-to-all-start) | async-done | bytes 1048608 | tf_op jit(solution)/shard_map/all_to_all | solution.py:393
  58.6 0.2 reduce_sum.12
  58.7 1.5 %collective-permute-start.9 = (bf16[32,512]{1,0:T(8,128)(2,1)S(1)}, bf16[32,512]{1,0:T(8,128)(2,1)S(1)}, u32[]{:S(2)}, u32[]{:S(2)}) collective-permute-start(bf16[32,512]{1,0:T(8,128)(2,1)S(1)} %reduce_sum.12), channel_id=1, source_target_pairs={{0,4},{1,5},{2,6},{3,7},{4,0},{5,1},{6,2},{7,3},{8,12},{9,13},{10,... | collective-permute-start | bytes 98312 | tf_op jit(solution)/shard_map/ppermute | solution.py:416
  60.3 0.1 collective-permute-start.8
  60.4 4.1 %collective-permute-start.7 = (bf16[32,512]{1,0:T(8,128)(2,1)S(1)}, bf16[32,512]{1,0:T(8,128)(2,1)S(1)}, u32[]{:S(2)}, u32[]{:S(2)}) collective-permute-start(bf16[32,512]{1,0:T(8,128)(2,1)S(1)} %reduce_sum.12), channel_id=1, source_target_pairs={{0,2},{1,3},{2,0},{3,1},{4,6},{5,7},{6,4},{7,5},{8,10},{9,11},{10,... | collective-permute-start | bytes 98312 | tf_op jit(solution)/shard_map/ppermute | solution.py:416
  64.5 1.0 %collective-permute-done.9 = bf16[32,512]{1,0:T(8,128)(2,1)S(1)} collective-permute-done((bf16[32,512]{1,0:T(8,128)(2,1)S(1)}, bf16[32,512]{1,0:T(8,128)(2,1)S(1)}, u32[]{:S(2)}, u32[]{:S(2)}) %collective-permute-start.9) | collective-permute-done | bytes 32800 | tf_op jit(solution)/shard_map/ppermute | solution.py:416
  65.5 0.0 collective-permute-done.8
  65.5 1.4 %collective-permute-done.7 = bf16[32,512]{1,0:T(8,128)(2,1)S(1)} collective-permute-done((bf16[32,512]{1,0:T(8,128)(2,1)S(1)}, bf16[32,512]{1,0:T(8,128)(2,1)S(1)}, u32[]{:S(2)}, u32[]{:S(2)}) %collective-permute-start.7) | collective-permute-done | bytes 32800 | tf_op jit(solution)/shard_map/ppermute | solution.py:416
  67.0 0.1 broadcast_in_dim.3
  67.1 17.9 %all_to_all.10 = bf16[32,32,512]{2,1,0:T(8,128)(2,1)S(1)} all-to-all(bf16[32,32,512]{2,1,0:T(8,128)(2,1)S(1)} %broadcast_in_dim.3), channel_id=1, replica_groups=mesh['y'=4,'xh'=2,'core'=2,'xl'=2,'zh'=4,'zl'=2] {'y','xh','xl','zl'}, dimensions={0} | all-to-all | bytes 2097152 | tf_op jit(solution)/shard_map/all_to_all | solution.py:420
  85.0 4.0 %collective-permute-start.10 = (bf16[2,512,512]{2,1,0:T(8,128)(2,1)S(1)}, bf16[2,512,512]{2,1,0:T(8,128)(2,1)S(1)}, u32[]{:S(2)}, u32[]{:S(2)}) collective-permute-start(bf16[2,512,512]{2,1,0:T(8,128)(2,1)S(1)} %bitcast.10), channel_id=1, source_target_pairs={{0,16},{1,17},{2,18},{3,19},{4,20},{5,21},{6,22},{7,23},{8,24},{9,... | collective-permute-start | bytes 3145736 | tf_op jit(solution)/shard_map/ppermute | solution.py:422
  89.0 1.5 %put_half.2.rest_0_ = bf16[4,512,512]{2,1,0:T(8,128)(2,1)} custom-call(s32[3]{0:T(128)S(1)} %pad_add_fusion.place, bf16[2,512,512]{2,1,0:T(8,128)(2,1)S(1)} %bitcast.11), custom_call_target="tpu_custom_call" | custom-call | tf_op jit(solution)/shard_map/put_half/pallas_call | solution.py:29
  90.5 0.7 collective-permute-done.10.half
  91.3 1.5 %put_half.3 = bf16[4,512,512]{2,1,0:T(8,128)(2,1)} custom-call(s32[3]{0:T(128)S(1)} %pad_add_fusion.place, bf16[2,512,512]{2,1,0:T(8,128)(2,1)S(1)} %collective-permute-done.10.half, bf16[4,512,512]{2,1,0:T(8,128)(2,1)} %put_half.2.rest_0_), custom_call_target="tpu_custom_call", output_to_operand_aliasing={{}: (2, {})} | custom-call | tf_op jit(solution)/shard_map/put_half/pallas_call | solution.py:29
  (1 shorter events, 0.0 us)
Async XLA Ops:
  0.7 1.4 %copy-start.2 = (bf16[16,90,512]{2,0,1:T(8,128)(2,1)S(1)}, bf16[16,90,512]{2,0,1:T(8,128)(2,1)}, u32[]{:S(2)}) copy-start(bf16[16,90,512]{2,0,1:T(8,128)(2,1)} %param.5) | copy-start | bytes 4423684
  2.8 9.5 %collective-permute-start = (bf16[2,16,512]{2,1,0:T(8,128)(2,1)S(1)}, bf16[2,16,512]{2,1,0:T(8,128)(2,1)S(1)}, u32[]{:S(2)}, u32[]{:S(2)}) collective-permute-start(bf16[2,16,512]{2,1,0:T(8,128)(2,1)S(1)} %get-tuple-element.18), channel_id=1, source_target_pairs={{0,1},{1,0},{2,3},{3,2},{4,5},{5,4},{6,7},{7,6},{8,9},{9,8},{10,11... | collective-permute-start | bytes 98312 | tf_op jit(solution)/shard_map/ppermute | solution.py:371
  5.3 6.9 %collective-permute-start.1 = (bf16[2,16,512]{2,1,0:T(8,128)(2,1)S(1)}, bf16[2,16,512]{2,1,0:T(8,128)(2,1)S(1)}, u32[]{:S(2)}, u32[]{:S(2)}) collective-permute-start(bf16[2,16,512]{2,1,0:T(8,128)(2,1)S(1)} %get-tuple-element.16._), channel_id=1, source_target_pairs={{0,15},{1,2},{2,1},{3,4},{4,3},{5,6},{6,5},{7,8},{8,7},{9,10},{10,... | collective-permute-start | bytes 98312 | tf_op jit(solution)/shard_map/ppermute | solution.py:372
  10.9 14.4 %collective-permute-start.2 = (bf16[16,16,512]{2,1,0:T(8,128)(2,1)S(1)}, bf16[16,16,512]{2,1,0:T(8,128)(2,1)S(1)}, u32[]{:S(2)}, u32[]{:S(2)}) collective-permute-start(bf16[16,16,512]{2,1,0:T(8,128)(2,1)S(1)} %get-tuple-element.22), channel_id=1, source_target_pairs={{0,15},{1,2},{2,1},{3,4},{4,3},{5,6},{6,5},{7,8},{8,7},{9,10},{10,... | collective-permute-start | bytes 786440 | tf_op jit(solution)/shard_map/ppermute | solution.py:374
  10.9 6.1 %copy-start.3 = (bf16[4,3,33,256]{3,0,2,1:T(4,128)(2,1)S(1)}, bf16[4,3,33,256]{3,0,2,1:T(4,128)(2,1)}, u32[]{:S(2)}) copy-start(bf16[4,3,33,256]{3,0,2,1:T(4,128)(2,1)} %param.8) | copy-start | bytes 608260
  11.0 6.1 %copy-start.4 = (s32[256]{0:T(256)S(1)}, s32[256]{0:T(256)}, u32[]{:S(2)}) copy-start(s32[256]{0:T(256)} %param.9) | copy-start | bytes 3076
  11.0 14.4 %collective-permute-start.3 = (bf16[16,16,512]{2,1,0:T(8,128)(2,1)S(1)}, bf16[16,16,512]{2,1,0:T(8,128)(2,1)S(1)}, u32[]{:S(2)}, u32[]{:S(2)}) collective-permute-start(bf16[16,16,512]{2,1,0:T(8,128)(2,1)S(1)} %get-tuple-element.23), channel_id=1, source_target_pairs={{0,1},{1,0},{2,3},{3,2},{4,5},{5,4},{6,7},{7,6},{8,9},{9,8},{10,11... | collective-permute-start | bytes 786440 | tf_op jit(solution)/shard_map/ppermute | solution.py:373
  12.9 12.4 %collective-permute-start.5 = (bf16[128,512]{1,0:T(8,128)(2,1)S(1)}, bf16[128,512]{1,0:T(8,128)(2,1)S(1)}, u32[]{:S(2)}, u32[]{:S(2)}) collective-permute-start(bf16[128,512]{1,0:T(8,128)(2,1)S(1)} %get-tuple-element.24), channel_id=1, source_target_pairs={{0,8},{1,9},{2,10},{3,11},{4,12},{5,13},{6,14},{7,15},{8,0},{9,1},... | collective-permute-start | bytes 393224 | tf_op jit(solution)/shard_map/ppermute | solution.py:406
  17.0 8.3 %collective-permute-start.4 = (bf16[128,512]{1,0:T(8,128)(2,1)S(1)}, bf16[128,512]{1,0:T(8,128)(2,1)S(1)}, u32[]{:S(2)}, u32[]{:S(2)}) collective-permute-start(bf16[128,512]{1,0:T(8,128)(2,1)S(1)} %get-tuple-element.19._), channel_id=1, source_target_pairs={{0,16},{1,17},{2,18},{3,19},{4,20},{5,21},{6,22},{7,23},{8,24},{9,... | collective-permute-start | bytes 393224 | tf_op jit(solution)/shard_map/ppermute | solution.py:405
  31.3 3.0 %copy-start = (bf16[4,16,96,512]{3,2,1,0:T(8,128)(2,1)}, bf16[4,16,96,512]{3,2,1,0:T(8,128)(2,1)S(1)}, u32[]{:S(2)}) copy-start(bf16[4,16,96,512]{3,2,1,0:T(8,128)(2,1)S(1)} %get-tuple-element.26.f_hbm) | copy-start | bytes 18874372
  31.3 3.0 %collective-permute-start.6 = (bf16[2,512,512]{2,1,0:T(8,128)(2,1)S(1)}, bf16[2,512,512]{2,1,0:T(8,128)(2,1)S(1)}, u32[]{:S(2)}, u32[]{:S(2)}) collective-permute-start(bf16[2,512,512]{2,1,0:T(8,128)(2,1)S(1)} %get-tuple-element.27), channel_id=1, source_target_pairs={{0,16},{1,17},{2,18},{3,19},{4,20},{5,21},{6,22},{7,23},{8,24},{9,... | collective-permute-start | bytes 3145736 | tf_op jit(solution)/shard_map/ppermute | solution.py:409
  35.7 22.8 %all-to-all-start = ((bf16[32,32,512]{2,1,0:T(8,128)(2,1)}), bf16[32,32,512]{2,1,0:T(8,128)(2,1)S(1)}, u32[]{:S(2)}, u32[]{:S(2)}) async-start(bf16[32,32,512]{2,1,0:T(8,128)(2,1)} %bitcast.7), calls=%async_computation | async-start | bytes 2097152 | tf_op jit(solution)/shard_map/all_to_all | solution.py:393
  41.9 2.8 %copy-start.1 = (bf16[4,16,96,512]{3,2,1,0:T(8,128)(2,1)S(1)}, bf16[4,16,96,512]{3,2,1,0:T(8,128)(2,1)}, u32[]{:S(2)}) copy-start(bf16[4,16,96,512]{3,2,1,0:T(8,128)(2,1)} %copy-done) | copy-start | bytes 18874372
  58.7 6.8 %collective-permute-start.9 = (bf16[32,512]{1,0:T(8,128)(2,1)S(1)}, bf16[32,512]{1,0:T(8,128)(2,1)S(1)}, u32[]{:S(2)}, u32[]{:S(2)}) collective-permute-start(bf16[32,512]{1,0:T(8,128)(2,1)S(1)} %reduce_sum.12), channel_id=1, source_target_pairs={{0,4},{1,5},{2,6},{3,7},{4,0},{5,1},{6,2},{7,3},{8,12},{9,13},{10,... | collective-permute-start | bytes 98312 | tf_op jit(solution)/shard_map/ppermute | solution.py:416
  60.3 5.2 %collective-permute-start.8 = (bf16[32,512]{1,0:T(8,128)(2,1)S(1)}, bf16[32,512]{1,0:T(8,128)(2,1)S(1)}, u32[]{:S(2)}, u32[]{:S(2)}) collective-permute-start(bf16[32,512]{1,0:T(8,128)(2,1)S(1)} %reduce_sum.12), channel_id=1, source_target_pairs={{0,6},{1,7},{2,4},{3,5},{4,2},{5,3},{6,0},{7,1},{8,14},{9,15},{10,... | collective-permute-start | bytes 98312 | tf_op jit(solution)/shard_map/ppermute | solution.py:416
  60.4 6.6 %collective-permute-start.7 = (bf16[32,512]{1,0:T(8,128)(2,1)S(1)}, bf16[32,512]{1,0:T(8,128)(2,1)S(1)}, u32[]{:S(2)}, u32[]{:S(2)}) collective-permute-start(bf16[32,512]{1,0:T(8,128)(2,1)S(1)} %reduce_sum.12), channel_id=1, source_target_pairs={{0,2},{1,3},{2,0},{3,1},{4,6},{5,7},{6,4},{7,5},{8,10},{9,11},{10,... | collective-permute-start | bytes 98312 | tf_op jit(solution)/shard_map/ppermute | solution.py:416
  85.0 6.3 %collective-permute-start.10 = (bf16[2,512,512]{2,1,0:T(8,128)(2,1)S(1)}, bf16[2,512,512]{2,1,0:T(8,128)(2,1)S(1)}, u32[]{:S(2)}, u32[]{:S(2)}) collective-permute-start(bf16[2,512,512]{2,1,0:T(8,128)(2,1)S(1)} %bitcast.10), channel_id=1, source_target_pairs={{0,16},{1,17},{2,18},{3,19},{4,20},{5,21},{6,22},{7,23},{8,24},{9,... | collective-permute-start | bytes 3145736 | tf_op jit(solution)/shard_map/ppermute | solution.py:422

commit v8 on v7

--- a/solution.py
+++ b/solution.py
@@ -8,8 +8,9 @@
 from jax.sharding import Mesh, PartitionSpec as P
 
 ROWS, COLS, REACH = 16, 90, 16
-PAD, HALF, SPAN, WIDE = 96, 48, 80, 128
-DEPTH = 256
+PAD, PART, SPAN, WIDE = 96, 32, 64, 128
+DEPTH = 4 * SPAN
+PARTS = PAD // PART
 CHANNELS, FILTERS, TAPS = 512, 4, 3
 AXES = ("y", "xh", "core", "xl", "zh", "zl")
 BLOCK = ("y", "xh", "xl", "zl")
@@ -39,7 +40,7 @@
     )(*inputs)
 
 
-def edges_kernel(place, own, slab_a, slab_b, edge_a, edge_b):
+def edges_kernel(place, own, slab_a, slab_b, edge_a, edge_b, middle):
     even = place[1] == 0
     west, east = own[:REACH], own[COLS - REACH :]
     slab_a[...] = jnp.where(even, east, west)
@@ -47,6 +48,10 @@
     for slab, edge in ((slab_a, edge_a), (slab_b, edge_b)):
         block = turned(slab[...])
         edge[0], edge[1] = block[0], block[ROWS - 1]
+    for b, left, n in chunks():
+        block = turned_chunk(own[left : left + n])
+        middle[0, left : left + 16] = block[0]
+        middle[1, left : left + 16] = block[ROWS - 1]
 
 
 def chunks():
@@ -68,32 +73,28 @@
     return turned(block)
 
 
-def turn_kernel(place, own, _, rows, middle, buffer, sems):
-    copies = fetches(own, buffer, sems)
-    for b, left, n in chunks():
-        copies[b].wait()
-        block = turned_chunk(buffer[left : left + n])
-        rows[:, left : left + 16, :] = block
-        middle[0, left : left + 16] = block[0]
-        middle[1, left : left + 16] = block[ROWS - 1]
+def ordered_kernel(place, middle, _, out):
+    first = place[0] == 0
+    out[0] = jnp.where(first, middle[1], middle[0])
+    out[1] = jnp.where(first, middle[0], middle[1])
 
 
 def widen_kernel(place, middle, got_a, got_b, wide_a, wide_b):
     even, first = place[1] == 0, place[0] == 0
     left = jnp.where(even, got_b[...], got_a[...])
     right = jnp.where(even, got_a[...], got_b[...])
-    for wide, is_last in ((wide_a, first), (wide_b, jnp.logical_not(first))):
+    for i, (wide, is_last) in enumerate(((wide_a, first), (wide_b, jnp.logical_not(first)))):
         pick = lambda x: jnp.where(is_last, x[1], x[0])
         wide[COLS + REACH :] = jnp.zeros((WIDE - COLS - REACH, CHANNELS), BF16)
         wide[:REACH] = pick(left)
-        wide[REACH : COLS + REACH] = pick(middle)[:COLS]
+        wide[REACH : COLS + REACH] = middle[i, :COLS]
         wide[COLS + REACH : COLS + 2 * REACH] = pick(right)
 
 
 LEAD = 8
 
 
-def prepare_kernel(place, basis, reach, act, _, tiles, cells, placed, buffer, sems):
+def prepare_kernel(place, basis, reach, act, own, _, tiles, cells, rows, placed, buffer, sems):
     copies = fetches(act, buffer, sems)
     length = basis.shape[1] * FILTERS
     lats = basis.shape[3]
@@ -117,14 +118,17 @@
         for k in range(FILTERS):
             lanes = pl.ds(k * DEPTH, DEPTH)
             taps = [placed[q, pl.ds(start + r + q, 1), lanes] for q in range(TAPS)]
-            band = jnp.broadcast_to(taps[0] + taps[1] + taps[2], (HALF, DEPTH))
-            tiles[r, k * HALF : (k + 1) * HALF, :] = pltpu.roll(band, 0, 1, stride=1, stride_axis=0).astype(BF16)
+            band = jnp.broadcast_to(taps[0] + taps[1] + taps[2], (PART, DEPTH))
+            band = pltpu.roll(band, SPAN * (r % 2), 1, stride=1, stride_axis=0)
+            first = (r % 2) * FILTERS * PART + k * PART
+            tiles[r // 2, first : first + PART, :] = band.astype(BF16)
     for b, left, n in chunks():
         copies[b].wait()
         cells[:, left : left + 16, :] = turned_chunk(buffer[left : left + n])
-
-
-GROUP = 4
+        rows[:, left : left + 16, :] = turned_chunk(own[left : left + n])
+
+
+GROUP = 8
 STEPS = ROWS // GROUP
 
 
@@ -134,7 +138,7 @@
     return lax.dot_general(f, cells, (((0,), (0,)), ((), ())), preferred_element_type=F32)
 
 
-def stencil_kernel(place, tiles, rows, lon_b, lon_a, lat_a, lat_b, cells_ref, f_out, send, low, high, held, cells, sem, f_sems):
+def stencil_kernel(place, tiles, rows, lon_b, lon_a, lat_a, lat_b, cells_ref, f_out, send, spans, held, cells, sem, f_sems):
     step = pl.program_id(0)
     stores = [
         pltpu.make_async_copy(held.at[:, pl.ds(GROUP * i, GROUP)], f_out.at[:, pl.ds(GROUP * i, GROUP)], f_sems.at[i])
@@ -147,29 +151,30 @@
         copy.start()
         even, first = place[1] == 0, place[0] == 0
         inner = slice(1, ROWS + 1)
-        low[inner, :REACH, :] = turned(jnp.where(even, lon_b[...], lon_a[...]))
-        low[inner, REACH:, :] = rows[:, : SPAN - REACH, :]
-        high[inner, : PAD - 32, :] = rows[:, 32:PAD, :]
-        high[inner, PAD - 32 :, :] = jnp.zeros((ROWS, SPAN + 32 - PAD, CHANNELS), BF16)
+        spans[0, inner, :REACH, :] = turned(jnp.where(even, lon_b[...], lon_a[...]))
+        spans[0, inner, REACH:, :] = rows[:, :48, :]
+        spans[1, inner, :, :] = rows[:, 16:80, :]
+        spans[2, inner, :48, :] = rows[:, 48:PAD, :]
+        spans[2, inner, 48:, :] = jnp.zeros((ROWS, SPAN - 48, CHANNELS), BF16)
         right = turned(jnp.where(even, lon_a[...], lon_b[...]))
         for r in range(ROWS):
-            high[r + 1, COLS - 32 : COLS - 32 + REACH, :] = right[r]
+            spans[2, r + 1, COLS - 48 : COLS - 48 + REACH, :] = right[r]
         before = jnp.where(first, lat_b[...], lat_a[...])
         after = jnp.where(first, lat_a[...], lat_b[...])
-        low[0], low[ROWS + 1] = before[:SPAN], after[:SPAN]
-        high[0], high[ROWS + 1] = before[HALF:], after[HALF:]
+        for h in range(PARTS):
+            spans[h, 0] = before[PART * h : PART * h + SPAN]
+            spans[h, ROWS + 1] = after[PART * h : PART * h + SPAN]
 
     @pl.when(step < STEPS)
     def _():
-        rest = jnp.zeros((DEPTH - TAPS * SPAN, CHANNELS), BF16)
-        for j in range(GROUP):
-            r = step * GROUP + j
-            for h, source in enumerate((low, high)):
-                taken = source[pl.ds(r, TAPS)].reshape(TAPS * SPAN, CHANNELS)
-                taken = jnp.concatenate([taken, rest])
-                f = jnp.dot(tiles[j], taken, preferred_element_type=F32).astype(BF16)
-                f = f.reshape(FILTERS, HALF, CHANNELS)
-                held[:, r, h * HALF : (h + 1) * HALF, :] = f
+        for pair in range(GROUP // 2):
+            r = step * GROUP + 2 * pair
+            for h in range(PARTS):
+                taken = spans[h, pl.ds(r, 4)].reshape(DEPTH, CHANNELS)
+                f = jnp.dot(tiles[pair], taken, preferred_element_type=F32).astype(BF16)
+                f = f.reshape(2, FILTERS, PART, CHANNELS)
+                for j in range(2):
+                    held[:, r + j, h * PART : (h + 1) * PART, :] = f[j]
 
     for i, store in enumerate(stores):
         pl.when(step == i)(store.start)
@@ -177,14 +182,8 @@
     @pl.when(step == STEPS)
     def _():
         copy.wait()
-
-    @pl.when(step >= STEPS)
-    def _():
-        k = 2 * (1 - place[0]) + step - STEPS
-        send[0] = outer(held[k], cells[...]).astype(BF16)
-
-    @pl.when(step == STEPS + 1)
-    def _():
+        for j in range(2):
+            send[j] = outer(held[2 * (1 - place[0]) + j], cells[...]).astype(BF16)
         for store in stores:
             store.wait()
 
@@ -195,19 +194,18 @@
         stencil_kernel,
         grid_spec=pltpu.PrefetchScalarGridSpec(
             num_scalar_prefetch=1,
-            grid=(STEPS + 2,),
+            grid=(STEPS + 1,),
             in_specs=[
-                pl.BlockSpec((GROUP, FILTERS * HALF, DEPTH), lambda i, c: (jnp.minimum(i, STEPS - 1), 0, 0)),
+                pl.BlockSpec((GROUP // 2, 2 * FILTERS * PART, DEPTH), lambda i, c: (jnp.minimum(i, STEPS - 1), 0, 0)),
                 *[whole(a) for a in (rows, lon_b, lon_a, lat_a, lat_b)],
                 pl.BlockSpec(memory_space=pl.ANY),
             ],
             out_specs=[
                 pl.BlockSpec(memory_space=pltpu.HBM),
-                pl.BlockSpec((1, CHANNELS, CHANNELS), lambda i, c: (jnp.maximum(i - STEPS, 0), 0, 0)),
+                pl.BlockSpec((2, CHANNELS, CHANNELS), lambda i, c: (0, 0, 0)),
             ],
             scratch_shapes=[
-                pltpu.VMEM((ROWS + 2, SPAN, CHANNELS), BF16),
-                pltpu.VMEM((ROWS + 2, SPAN, CHANNELS), BF16),
+                pltpu.VMEM((PARTS, ROWS + 2, SPAN, CHANNELS), BF16),
                 pltpu.VMEM((FILTERS, ROWS, PAD, CHANNELS), BF16),
                 pltpu.VMEM((ROWS, PAD, CHANNELS), BF16),
                 pltpu.SemaphoreType.DMA(()),
@@ -363,20 +361,18 @@
 
 def haloes(own, place):
     slab, edge, wide = (REACH, ROWS, CHANNELS), (2, REACH, CHANNELS), (WIDE, CHANNELS)
-    slab_a, slab_b, edge_a, edge_b = local(edges_kernel, "edges", [slab, slab, edge, edge], [place, own])
-    rows, middle = local(
-        turn_kernel, "turn", [(ROWS, PAD, CHANNELS), (2, PAD, CHANNELS)], [place, own, edge_b],
-        [pltpu.VMEM(own.shape, BF16), pltpu.SemaphoreType.DMA((PAD // 16,))], {1: pltpu.HBM, 2: pl.ANY}, cost=4_000_000_000,
-    )
+    rows = (2, PAD, CHANNELS)
+    slab_a, slab_b, edge_a, edge_b, middle = local(edges_kernel, "edges", [slab, slab, edge, edge, rows], [place, own])
+    (middle,) = local(ordered_kernel, "ordered", [rows], [place, middle, edge_b], spaces={2: pl.ANY}, cost=4_000_000_000)
     edge_a = lax.ppermute(edge_a, AXES, LON_A)
     edge_b = lax.ppermute(edge_b, AXES, LON_B)
     lon_a = lax.ppermute(slab_a, AXES, LON_A)
     lon_b = lax.ppermute(slab_b, AXES, LON_B)
     wide_a, wide_b = local(widen_kernel, "widen", [wide, wide], [place, middle, edge_a, edge_b])
-    return rows, lon_a, lon_b, wide_a, wide_b
-
-
-def prepared(place, basis, reach, act, after):
+    return lon_a, lon_b, wide_a, wide_b
+
+
+def prepared(place, basis, reach, act, own, after):
     lats = basis.shape[3]
     basis = jnp.transpose(basis, (1, 2, 0, 3))
     scratch = [
@@ -384,9 +380,10 @@
         pltpu.VMEM(act.shape, BF16),
         pltpu.SemaphoreType.DMA((PAD // 16,)),
     ]
-    shapes = [(ROWS, FILTERS * HALF, DEPTH), (ROWS, PAD, CHANNELS)]
-    inputs = [place, basis, reach.reshape(1, lats), act, after]
-    return local(prepare_kernel, "prepare", shapes, inputs, scratch, {3: pltpu.HBM, 4: pl.ANY}, cost=1_000_000_000)
+    rows = (ROWS, PAD, CHANNELS)
+    shapes = [(ROWS // 2, 2 * FILTERS * PART, DEPTH), rows, rows]
+    inputs = [place, basis, reach.reshape(1, lats), act, own, after]
+    return local(prepare_kernel, "prepare", shapes, inputs, scratch, {3: pltpu.HBM, 5: pl.ANY}, cost=1_000_000_000)
 
 
 def summed(parts, groups, axes):
@@ -401,10 +398,10 @@
     place = jnp.stack([core, odd, band])
     own, act = jnp.swapaxes(cotangent, 0, 1), jnp.swapaxes(activations, 0, 1)
     act = pltpu.with_memory_space_constraint(act, pltpu.HBM)
-    rows, lon_a, lon_b, wide_a, wide_b = haloes(own, place)
+    lon_a, lon_b, wide_a, wide_b = haloes(own, place)
     lat_a = lax.ppermute(wide_a, AXES, LAT_A)
     lat_b = lax.ppermute(wide_b, AXES, LAT_B)
-    tiles, cells = prepared(place, basis, reach, act, wide_a)
+    tiles, cells, rows = prepared(place, basis, reach, act, own, wide_a)
     f, send = stencil(place, tiles, rows, lon_a, lon_b, lat_a, lat_b, cells)
     got = lax.ppermute(send, AXES, SIBLING)
     mine = own_part(place, f, cells)

time: 93.3 us -> 92.7 us (level)
  Pallas kernels: 24.3 us -> 23.3 us
    unnamed x10 -> x12, local copies, waits for them, and re-layouts: 4.16 us -> 4.17 us
  transfers between devices with their start and end apart: 12 -> 12, of which waited for: 5 -> 6; matrix products, arithmetic and copies ran while one was open for 0% -> 0% of each run, Pallas kernels for 17% -> 17%
where the time goes in v8:
time: 92.7 us; the launch traced here: 92.4 us
  starting transfers between devices  28.4 us (31%)
  Pallas kernels  23.3 us (25%)
  blocking collectives  18 us (19%)
  waiting for transfers between devices  15.9 us (17%)
  local copies, waits for them, and re-layouts  4.28 us (5%)
  other arithmetic  1.6 us (2%)
  between operations  0.96 us (1%)
    all_to_all x1, blocking collectives, on_device(): lax.all_to_all(jnp.broadcast_to(part, (32, *part.shape)), BLOCK, 0, 0, ti...  18 us
    pallas_call x6, Pallas kernels, local(): pl.pallas_call(kernel, in_specs=[pl.BlockSpec(memory_space=pltpu.SMEM)] +...  8.39 us
    all_to_all x1, waiting for transfers between devices, summed(): lax.all_to_all(parts.reshape(groups, -1, CHANNELS), axes, 0, 0, tiled=True)  7.24 us
    pallas_call x1, Pallas kernels, input_gradient(): pl.pallas_call(input_kernel, in_specs=[spec(pl.ANY), spec(pltpu.HBM)], ou...  6.68 us
    all_to_all x1, starting transfers between devices, summed(): lax.all_to_all(parts.reshape(groups, -1, CHANNELS), axes, 0, 0, tiled=True)  6.12 us
    ppermute x3, starting transfers between devices, on_device(): lax.ppermute(part, AXES, along_z(m)).astype(F32)  5.74 us
    ppermute x1, starting transfers between devices, haloes(): edge_b = lax.ppermute(edge_b, AXES, LON_B)  5.59 us
    pallas_call x1, Pallas kernels, stencil(): pl.pallas_call(stencil_kernel, grid_spec=pltpu.PrefetchScalarGridSpec(num...  5.32 us
  transfers between devices with their start and end apart: 12, of which 6 were waited for; matrix products, arithmetic and copies ran while one was open for 0% of the time, Pallas kernels for 17%

profile of v8, /device:TPU:1, one launch (start us, length us, event | category | flops | bytes accessed | tf_op | source)
XLA Modules:
  0.0 92.4 jit_solution(2305079164129112439)
XLA Ops:
  0.6 0.1 pad_add_fusion.place
  0.7 0.0 copy-start.2
  0.7 1.4 %copy-done.2 = bf16[16,90,512]{2,0,1:T(8,128)(2,1)S(1)} copy-done((bf16[16,90,512]{2,0,1:T(8,128)(2,1)S(1)}, bf16[16,90,512]{2,0,1:T(8,128)(2,1)}, u32[]{:S(2)}) %copy-start.2) | copy-done | bytes 1474584
  2.1 0.8 edges.1
  2.9 2.6 %collective-permute-start = (bf16[2,16,512]{2,1,0:T(8,128)(2,1)S(1)}, bf16[2,16,512]{2,1,0:T(8,128)(2,1)S(1)}, u32[]{:S(2)}, u32[]{:S(2)}) collective-permute-start(bf16[2,16,512]{2,1,0:T(8,128)(2,1)S(1)} %get-tuple-element.18), channel_id=1, source_target_pairs={{0,1},{1,0},{2,3},{3,2},{4,5},{5,4},{6,7},{7,6},{8,9},{9,8},{10,11... | collective-permute-start | bytes 98312 | tf_op jit(solution)/shard_map/ppermute | solution.py:367
  5.5 5.6 %collective-permute-start.1 = (bf16[2,16,512]{2,1,0:T(8,128)(2,1)S(1)}, bf16[2,16,512]{2,1,0:T(8,128)(2,1)S(1)}, u32[]{:S(2)}, u32[]{:S(2)}) collective-permute-start(bf16[2,16,512]{2,1,0:T(8,128)(2,1)S(1)} %get-tuple-element.17._), channel_id=1, source_target_pairs={{0,15},{1,2},{2,1},{3,4},{4,3},{5,6},{6,5},{7,8},{8,7},{9,10},{10,... | collective-permute-start | bytes 98312 | tf_op jit(solution)/shard_map/ppermute | solution.py:368
  11.1 0.0 collective-permute-start.2
  11.1 0.0 collective-permute-start.3
  11.1 0.0 copy-start.3
  11.1 0.0 copy-start.4
  11.1 0.0 copy-start.5
  11.1 0.6 ordered.1.middle
  11.7 0.0 collective-permute-done.got_a
  11.7 0.7 collective-permute-done.1.got_b
  12.4 0.6 widen.1
  13.0 4.2 %collective-permute-start.5 = (bf16[128,512]{1,0:T(8,128)(2,1)S(1)}, bf16[128,512]{1,0:T(8,128)(2,1)S(1)}, u32[]{:S(2)}, u32[]{:S(2)}) collective-permute-start(bf16[128,512]{1,0:T(8,128)(2,1)S(1)} %get-tuple-element.24), channel_id=1, source_target_pairs={{0,8},{1,9},{2,10},{3,11},{4,12},{5,13},{6,14},{7,15},{8,0},{9,1},... | collective-permute-start | bytes 393224 | tf_op jit(solution)/shard_map/ppermute | solution.py:403
  17.2 0.0 collective-permute-start.4
  17.2 0.0 copy-done.3
  17.2 0.0 copy-done.4
  17.2 0.0 copy-done.5
  17.2 3.3 %prepare.1 = (bf16[8,256,256]{2,1,0:T(8,128)(2,1)S(1)}, bf16[16,96,512]{2,1,0:T(8,128)(2,1)S(1)}, bf16[16,96,512]{2,1,0:T(8,128)(2,1)S(1)}) custom-call(s32[3]{0:T(128)S(1)} %pad_add_fusion.place, bf16[3,33,4,256]{3,2,1,0:T(4,128)(2,1)S(1)} %bitcast.14, s32[1,256]{1,0:T(1,128)S(1)} %bitcast.15, bf16[90,16,512]{2,1,0:T(8,128)(2,1)} %bitcast.16, ...), custom_call_target="tpu_custom_call" | custom-call | flops 1000000000 | bytes 2000000 | tf_op jit(solution)/shard_map/prepare/pallas_call | solution.py:30
  20.6 4.9 %collective-permute-done.5.lat_b = bf16[128,512]{1,0:T(8,128)(2,1)S(1)} collective-permute-done((bf16[128,512]{1,0:T(8,128)(2,1)S(1)}, bf16[128,512]{1,0:T(8,128)(2,1)S(1)}, u32[]{:S(2)}, u32[]{:S(2)}) %collective-permute-start.5) | collective-permute-done | bytes 131104 | tf_op jit(solution)/shard_map/ppermute | solution.py:403
  25.5 0.0 collective-permute-done.4.lat_a
  25.5 0.0 collective-permute-done.2.lon_b
  25.5 0.0 collective-permute-done.3.lon_a
  25.5 5.3 %stencil.1 = (bf16[4,16,96,512]{3,2,1,0:T(8,128)(2,1)S(1)}, bf16[2,512,512]{2,1,0:T(8,128)(2,1)S(1)}) custom-call(s32[3]{0:T(128)S(1)} %pad_add_fusion.place, bf16[8,256,256]{2,1,0:T(8,128)(2,1)S(1)} %get-tuple-element.20.tiles, bf16[16,96,512]{2,1,0:T(8,128)(2,1)S(1)} %get-tuple-element.21.rows, bf16[16,16,512]{2,1,0:T(8,128)(2,1)S(1)} %collective-permute-done.2.lon_b, ...), custom_call_target="tpu_custom_call" | custom-call | tf_op jit(solution)/shard_map/stencil/pallas_call | solution.py:193
  30.8 0.0 copy-start
  30.8 0.1 collective-permute-start.6
  30.9 2.9 %own_part.1 = f32[2,512,512]{2,1,0:T(8,128)S(1)} custom-call(s32[3]{0:T(128)S(1)} %pad_add_fusion.place, bf16[4,16,96,512]{3,2,1,0:T(8,128)(2,1)S(1)} %get-tuple-element.26.f_hbm, bf16[16,96,512]{2,1,0:T(8,128)(2,1)S(1)} %get-tuple-element.25.cells_ref), custom_call_target="tpu_custom_call" | custom-call | flops 1610612736 | bytes 6000000 | tf_op jit(solution)/shard_map/own_part/pallas_call | solution.py:240
  33.8 0.0 copy-done
  33.8 0.0 collective-permute-done.6
  33.8 1.3 %add_convert_fusion = bf16[2,512,512]{2,1,0:T(8,128)(2,1)} fusion(f32[2,512,512]{2,1,0:T(8,128)S(1)} %own_part.1, bf16[2,512,512]{2,1,0:T(8,128)(2,1)S(1)} %collective-permute-done.6), kind=kLoop, calls=%fused_computation | loop fusion | flops 1572864 | bytes 4194304 | tf_op jit(solution)/shard_map/convert_element_type | solution.py:408
  35.2 6.1 %all-to-all-start = ((bf16[32,32,512]{2,1,0:T(8,128)(2,1)}), bf16[32,32,512]{2,1,0:T(8,128)(2,1)S(1)}, u32[]{:S(2)}, u32[]{:S(2)}) async-start(bf16[32,32,512]{2,1,0:T(8,128)(2,1)} %bitcast.7), calls=%async_computation | async-start | bytes 2097152 | tf_op jit(solution)/shard_map/all_to_all | solution.py:390
  41.3 0.0 copy-start.1
  41.3 2.8 %copy-done.1 = bf16[4,16,96,512]{3,2,1,0:T(8,128)(2,1)S(1)} copy-done((bf16[4,16,96,512]{3,2,1,0:T(8,128)(2,1)S(1)}, bf16[4,16,96,512]{3,2,1,0:T(8,128)(2,1)}, u32[]{:S(2)}) %copy-start.1) | copy-done | bytes 6291480
  44.1 6.7 %input_gradient.1 = bf16[90,16,512]{2,1,0:T(8,128)(2,1)} custom-call(bf16[4,16,96,512]{3,2,1,0:T(8,128)(2,1)S(1)} %copy-done.1, bf16[4,512,512]{2,1,0:T(8,128)(2,1)} %weight_hbm.1), custom_call_target="tpu_custom_call" | custom-call | flops 3221225472 | bytes 10000000 | tf_op jit(solution)/shard_map/input_gradient/pallas_call | solution.py:295
  50.8 7.2 %all-to-all-done = bf16[32,32,512]{2,1,0:T(8,128)(2,1)S(1)} async-done(((bf16[32,32,512]{2,1,0:T(8,128)(2,1)}), bf16[32,32,512]{2,1,0:T(8,128)(2,1)S(1)}, u32[]{:S(2)}, u32[]{:S(2)}) %all-to-all-start) | async-done | bytes 1048608 | tf_op jit(solution)/shard_map/all_to_all | solution.py:390
  58.0 0.2 reduce_sum.12
  58.2 0.8 collective-permute-start.9
  59.0 0.8 collective-permute-start.8
  59.8 4.1 %collective-permute-start.7 = (bf16[32,512]{1,0:T(8,128)(2,1)S(1)}, bf16[32,512]{1,0:T(8,128)(2,1)S(1)}, u32[]{:S(2)}, u32[]{:S(2)}) collective-permute-start(bf16[32,512]{1,0:T(8,128)(2,1)S(1)} %reduce_sum.12), channel_id=1, source_target_pairs={{0,2},{1,3},{2,0},{3,1},{4,6},{5,7},{6,4},{7,5},{8,10},{9,11},{10,... | collective-permute-start | bytes 98312 | tf_op jit(solution)/shard_map/ppermute | solution.py:413
  63.9 1.0 %collective-permute-done.9 = bf16[32,512]{1,0:T(8,128)(2,1)S(1)} collective-permute-done((bf16[32,512]{1,0:T(8,128)(2,1)S(1)}, bf16[32,512]{1,0:T(8,128)(2,1)S(1)}, u32[]{:S(2)}, u32[]{:S(2)}) %collective-permute-start.9) | collective-permute-done | bytes 32800 | tf_op jit(solution)/shard_map/ppermute | solution.py:413
  65.0 0.0 collective-permute-done.8
  65.0 1.3 %collective-permute-done.7 = bf16[32,512]{1,0:T(8,128)(2,1)S(1)} collective-permute-done((bf16[32,512]{1,0:T(8,128)(2,1)S(1)}, bf16[32,512]{1,0:T(8,128)(2,1)S(1)}, u32[]{:S(2)}, u32[]{:S(2)}) %collective-permute-start.7) | collective-permute-done | bytes 32800 | tf_op jit(solution)/shard_map/ppermute | solution.py:413
  66.3 0.1 broadcast_in_dim.3
  66.4 18.0 %all_to_all.10 = bf16[32,32,512]{2,1,0:T(8,128)(2,1)S(1)} all-to-all(bf16[32,32,512]{2,1,0:T(8,128)(2,1)S(1)} %broadcast_in_dim.3), channel_id=1, replica_groups=mesh['y'=4,'xh'=2,'core'=2,'xl'=2,'zh'=4,'zl'=2] {'y','xh','xl','zl'}, dimensions={0} | all-to-all | bytes 2097152 | tf_op jit(solution)/shard_map/all_to_all | solution.py:417
  84.4 4.0 %collective-permute-start.10 = (bf16[2,512,512]{2,1,0:T(8,128)(2,1)S(1)}, bf16[2,512,512]{2,1,0:T(8,128)(2,1)S(1)}, u32[]{:S(2)}, u32[]{:S(2)}) collective-permute-start(bf16[2,512,512]{2,1,0:T(8,128)(2,1)S(1)} %bitcast.10), channel_id=1, source_target_pairs={{0,16},{1,17},{2,18},{3,19},{4,20},{5,21},{6,22},{7,23},{8,24},{9,... | collective-permute-start | bytes 3145736 | tf_op jit(solution)/shard_map/ppermute | solution.py:419
  88.4 1.5 %put_half.2.rest_0_ = bf16[4,512,512]{2,1,0:T(8,128)(2,1)} custom-call(s32[3]{0:T(128)S(1)} %pad_add_fusion.place, bf16[2,512,512]{2,1,0:T(8,128)(2,1)S(1)} %bitcast.11), custom_call_target="tpu_custom_call" | custom-call | tf_op jit(solution)/shard_map/put_half/pallas_call | solution.py:30
  89.9 0.7 collective-permute-done.10.half
  90.7 1.5 %put_half.3 = bf16[4,512,512]{2,1,0:T(8,128)(2,1)} custom-call(s32[3]{0:T(128)S(1)} %pad_add_fusion.place, bf16[2,512,512]{2,1,0:T(8,128)(2,1)S(1)} %collective-permute-done.10.half, bf16[4,512,512]{2,1,0:T(8,128)(2,1)} %put_half.2.rest_0_), custom_call_target="tpu_custom_call", output_to_operand_aliasing={{}: (2, {})} | custom-call | tf_op jit(solution)/shard_map/put_half/pallas_call | solution.py:30
  (1 shorter events, 0.0 us)
Async XLA Ops:
  0.7 1.4 %copy-start.2 = (bf16[16,90,512]{2,0,1:T(8,128)(2,1)S(1)}, bf16[16,90,512]{2,0,1:T(8,128)(2,1)}, u32[]{:S(2)}) copy-start(bf16[16,90,512]{2,0,1:T(8,128)(2,1)} %param.5) | copy-start | bytes 4423684
  2.9 8.8 %collective-permute-start = (bf16[2,16,512]{2,1,0:T(8,128)(2,1)S(1)}, bf16[2,16,512]{2,1,0:T(8,128)(2,1)S(1)}, u32[]{:S(2)}, u32[]{:S(2)}) collective-permute-start(bf16[2,16,512]{2,1,0:T(8,128)(2,1)S(1)} %get-tuple-element.18), channel_id=1, source_target_pairs={{0,1},{1,0},{2,3},{3,2},{4,5},{5,4},{6,7},{7,6},{8,9},{9,8},{10,11... | collective-permute-start | bytes 98312 | tf_op jit(solution)/shard_map/ppermute | solution.py:367
  5.5 6.9 %collective-permute-start.1 = (bf16[2,16,512]{2,1,0:T(8,128)(2,1)S(1)}, bf16[2,16,512]{2,1,0:T(8,128)(2,1)S(1)}, u32[]{:S(2)}, u32[]{:S(2)}) collective-permute-start(bf16[2,16,512]{2,1,0:T(8,128)(2,1)S(1)} %get-tuple-element.17._), channel_id=1, source_target_pairs={{0,15},{1,2},{2,1},{3,4},{4,3},{5,6},{6,5},{7,8},{8,7},{9,10},{10,... | collective-permute-start | bytes 98312 | tf_op jit(solution)/shard_map/ppermute | solution.py:368
  11.1 14.4 %collective-permute-start.2 = (bf16[16,16,512]{2,1,0:T(8,128)(2,1)S(1)}, bf16[16,16,512]{2,1,0:T(8,128)(2,1)S(1)}, u32[]{:S(2)}, u32[]{:S(2)}) collective-permute-start(bf16[16,16,512]{2,1,0:T(8,128)(2,1)S(1)} %get-tuple-element.22), channel_id=1, source_target_pairs={{0,15},{1,2},{2,1},{3,4},{4,3},{5,6},{6,5},{7,8},{8,7},{9,10},{10,... | collective-permute-start | bytes 786440 | tf_op jit(solution)/shard_map/ppermute | solution.py:370
  11.1 14.4 %collective-permute-start.3 = (bf16[16,16,512]{2,1,0:T(8,128)(2,1)S(1)}, bf16[16,16,512]{2,1,0:T(8,128)(2,1)S(1)}, u32[]{:S(2)}, u32[]{:S(2)}) collective-permute-start(bf16[16,16,512]{2,1,0:T(8,128)(2,1)S(1)} %get-tuple-element.23), channel_id=1, source_target_pairs={{0,1},{1,0},{2,3},{3,2},{4,5},{5,4},{6,7},{7,6},{8,9},{9,8},{10,11... | collective-permute-start | bytes 786440 | tf_op jit(solution)/shard_map/ppermute | solution.py:369
  11.1 6.1 %copy-start.3 = (bf16[16,90,512]{2,0,1:T(8,128)(2,1)S(1)}, bf16[16,90,512]{2,0,1:T(8,128)(2,1)}, u32[]{:S(2)}) copy-start(bf16[16,90,512]{2,0,1:T(8,128)(2,1)} %param.5) | copy-start | bytes 4423684
  11.1 6.1 %copy-start.4 = (bf16[4,3,33,256]{3,0,2,1:T(4,128)(2,1)S(1)}, bf16[4,3,33,256]{3,0,2,1:T(4,128)(2,1)}, u32[]{:S(2)}) copy-start(bf16[4,3,33,256]{3,0,2,1:T(4,128)(2,1)} %param.8) | copy-start | bytes 608260
  11.1 6.1 %copy-start.5 = (s32[256]{0:T(256)S(1)}, s32[256]{0:T(256)}, u32[]{:S(2)}) copy-start(s32[256]{0:T(256)} %param.9) | copy-start | bytes 3076
  13.0 12.5 %collective-permute-start.5 = (bf16[128,512]{1,0:T(8,128)(2,1)S(1)}, bf16[128,512]{1,0:T(8,128)(2,1)S(1)}, u32[]{:S(2)}, u32[]{:S(2)}) collective-permute-start(bf16[128,512]{1,0:T(8,128)(2,1)S(1)} %get-tuple-element.24), channel_id=1, source_target_pairs={{0,8},{1,9},{2,10},{3,11},{4,12},{5,13},{6,14},{7,15},{8,0},{9,1},... | collective-permute-start | bytes 393224 | tf_op jit(solution)/shard_map/ppermute | solution.py:403
  17.2 8.3 %collective-permute-start.4 = (bf16[128,512]{1,0:T(8,128)(2,1)S(1)}, bf16[128,512]{1,0:T(8,128)(2,1)S(1)}, u32[]{:S(2)}, u32[]{:S(2)}) collective-permute-start(bf16[128,512]{1,0:T(8,128)(2,1)S(1)} %get-tuple-element.19._), channel_id=1, source_target_pairs={{0,16},{1,17},{2,18},{3,19},{4,20},{5,21},{6,22},{7,23},{8,24},{9,... | collective-permute-start | bytes 393224 | tf_op jit(solution)/shard_map/ppermute | solution.py:402
  30.8 3.0 %copy-start = (bf16[4,16,96,512]{3,2,1,0:T(8,128)(2,1)}, bf16[4,16,96,512]{3,2,1,0:T(8,128)(2,1)S(1)}, u32[]{:S(2)}) copy-start(bf16[4,16,96,512]{3,2,1,0:T(8,128)(2,1)S(1)} %get-tuple-element.26.f_hbm) | copy-start | bytes 18874372
  30.8 3.0 %collective-permute-start.6 = (bf16[2,512,512]{2,1,0:T(8,128)(2,1)S(1)}, bf16[2,512,512]{2,1,0:T(8,128)(2,1)S(1)}, u32[]{:S(2)}, u32[]{:S(2)}) collective-permute-start(bf16[2,512,512]{2,1,0:T(8,128)(2,1)S(1)} %get-tuple-element.27), channel_id=1, source_target_pairs={{0,16},{1,17},{2,18},{3,19},{4,20},{5,21},{6,22},{7,23},{8,24},{9,... | collective-permute-start | bytes 3145736 | tf_op jit(solution)/shard_map/ppermute | solution.py:406
  35.2 22.8 %all-to-all-start = ((bf16[32,32,512]{2,1,0:T(8,128)(2,1)}), bf16[32,32,512]{2,1,0:T(8,128)(2,1)S(1)}, u32[]{:S(2)}, u32[]{:S(2)}) async-start(bf16[32,32,512]{2,1,0:T(8,128)(2,1)} %bitcast.7), calls=%async_computation | async-start | bytes 2097152 | tf_op jit(solution)/shard_map/all_to_all | solution.py:390
  41.3 2.8 %copy-start.1 = (bf16[4,16,96,512]{3,2,1,0:T(8,128)(2,1)S(1)}, bf16[4,16,96,512]{3,2,1,0:T(8,128)(2,1)}, u32[]{:S(2)}) copy-start(bf16[4,16,96,512]{3,2,1,0:T(8,128)(2,1)} %copy-done) | copy-start | bytes 18874372
  58.2 6.8 %collective-permute-start.9 = (bf16[32,512]{1,0:T(8,128)(2,1)S(1)}, bf16[32,512]{1,0:T(8,128)(2,1)S(1)}, u32[]{:S(2)}, u32[]{:S(2)}) collective-permute-start(bf16[32,512]{1,0:T(8,128)(2,1)S(1)} %reduce_sum.12), channel_id=1, source_target_pairs={{0,4},{1,5},{2,6},{3,7},{4,0},{5,1},{6,2},{7,3},{8,12},{9,13},{10,... | collective-permute-start | bytes 98312 | tf_op jit(solution)/shard_map/ppermute | solution.py:413
  59.0 6.0 %collective-permute-start.8 = (bf16[32,512]{1,0:T(8,128)(2,1)S(1)}, bf16[32,512]{1,0:T(8,128)(2,1)S(1)}, u32[]{:S(2)}, u32[]{:S(2)}) collective-permute-start(bf16[32,512]{1,0:T(8,128)(2,1)S(1)} %reduce_sum.12), channel_id=1, source_target_pairs={{0,6},{1,7},{2,4},{3,5},{4,2},{5,3},{6,0},{7,1},{8,14},{9,15},{10,... | collective-permute-start | bytes 98312 | tf_op jit(solution)/shard_map/ppermute | solution.py:413
  59.8 6.4 %collective-permute-start.7 = (bf16[32,512]{1,0:T(8,128)(2,1)S(1)}, bf16[32,512]{1,0:T(8,128)(2,1)S(1)}, u32[]{:S(2)}, u32[]{:S(2)}) collective-permute-start(bf16[32,512]{1,0:T(8,128)(2,1)S(1)} %reduce_sum.12), channel_id=1, source_target_pairs={{0,2},{1,3},{2,0},{3,1},{4,6},{5,7},{6,4},{7,5},{8,10},{9,11},{10,... | collective-permute-start | bytes 98312 | tf_op jit(solution)/shard_map/ppermute | solution.py:413
  84.4 6.3 %collective-permute-start.10 = (bf16[2,512,512]{2,1,0:T(8,128)(2,1)S(1)}, bf16[2,512,512]{2,1,0:T(8,128)(2,1)S(1)}, u32[]{:S(2)}, u32[]{:S(2)}) collective-permute-start(bf16[2,512,512]{2,1,0:T(8,128)(2,1)S(1)} %bitcast.10), channel_id=1, source_target_pairs={{0,16},{1,17},{2,18},{3,19},{4,20},{5,21},{6,22},{7,23},{8,24},{9,... | collective-permute-start | bytes 3145736 | tf_op jit(solution)/shard_map/ppermute | solution.py:419

commit v9 on v8

--- a/solution.py
+++ b/solution.py
@@ -79,16 +79,17 @@
     out[1] = jnp.where(first, middle[0], middle[1])
 
 
-def widen_kernel(place, middle, got_a, got_b, wide_a, wide_b):
+def widen_kernel(place, middle, got_a, got_b, wide_a, wide_b, joined):
     even, first = place[1] == 0, place[0] == 0
     left = jnp.where(even, got_b[...], got_a[...])
     right = jnp.where(even, got_a[...], got_b[...])
     for i, (wide, is_last) in enumerate(((wide_a, first), (wide_b, jnp.logical_not(first)))):
-        pick = lambda x: jnp.where(is_last, x[1], x[0])
-        wide[COLS + REACH :] = jnp.zeros((WIDE - COLS - REACH, CHANNELS), BF16)
-        wide[:REACH] = pick(left)
-        wide[REACH : COLS + REACH] = middle[i, :COLS]
-        wide[COLS + REACH : COLS + 2 * REACH] = pick(right)
+        pick = lambda x: jnp.where(is_last, x[1], x[0]).astype(F32)
+        joined[i, :REACH] = pick(left)
+        joined[i, REACH : REACH + PAD] = middle[i].astype(F32)
+        joined[i, REACH + PAD :] = jnp.zeros((WIDE - REACH - PAD, CHANNELS), F32)
+        joined[i, COLS + REACH : COLS + 2 * REACH] = pick(right)
+        wide[...] = joined[i].astype(BF16)
 
 
 LEAD = 8
@@ -138,7 +139,7 @@
     return lax.dot_general(f, cells, (((0,), (0,)), ((), ())), preferred_element_type=F32)
 
 
-def stencil_kernel(place, tiles, rows, lon_b, lon_a, lat_a, lat_b, cells_ref, f_out, send, spans, held, cells, sem, f_sems):
+def stencil_kernel(place, tiles, rows, lon_b, lon_a, lat_a, lat_b, cells_ref, f_out, send, spans, joined, held, cells, sem, f_sems):
     step = pl.program_id(0)
     stores = [
         pltpu.make_async_copy(held.at[:, pl.ds(GROUP * i, GROUP)], f_out.at[:, pl.ds(GROUP * i, GROUP)], f_sems.at[i])
@@ -154,11 +155,11 @@
         spans[0, inner, :REACH, :] = turned(jnp.where(even, lon_b[...], lon_a[...]))
         spans[0, inner, REACH:, :] = rows[:, :48, :]
         spans[1, inner, :, :] = rows[:, 16:80, :]
-        spans[2, inner, :48, :] = rows[:, 48:PAD, :]
-        spans[2, inner, 48:, :] = jnp.zeros((ROWS, SPAN - 48, CHANNELS), BF16)
-        right = turned(jnp.where(even, lon_a[...], lon_b[...]))
-        for r in range(ROWS):
-            spans[2, r + 1, COLS - 48 : COLS - 48 + REACH, :] = right[r]
+        spans[2, inner, :32, :] = rows[:, 48:80, :]
+        joined[:, :16, :] = rows[:, 80:PAD, :].astype(F32)
+        joined[:, 16:, :] = jnp.zeros((ROWS, 16, CHANNELS), F32)
+        joined[:, COLS - 80 : COLS - 80 + REACH, :] = turned(jnp.where(even, lon_a[...], lon_b[...])).astype(F32)
+        spans[2, inner, 32:, :] = joined[...].astype(BF16)
         before = jnp.where(first, lat_b[...], lat_a[...])
         after = jnp.where(first, lat_a[...], lat_b[...])
         for h in range(PARTS):
@@ -206,6 +207,7 @@
             ],
             scratch_shapes=[
                 pltpu.VMEM((PARTS, ROWS + 2, SPAN, CHANNELS), BF16),
+                pltpu.VMEM((ROWS, 32, CHANNELS), F32),
                 pltpu.VMEM((FILTERS, ROWS, PAD, CHANNELS), BF16),
                 pltpu.VMEM((ROWS, PAD, CHANNELS), BF16),
                 pltpu.SemaphoreType.DMA(()),
@@ -368,7 +370,9 @@
     edge_b = lax.ppermute(edge_b, AXES, LON_B)
     lon_a = lax.ppermute(slab_a, AXES, LON_A)
     lon_b = lax.ppermute(slab_b, AXES, LON_B)
-    wide_a, wide_b = local(widen_kernel, "widen", [wide, wide], [place, middle, edge_a, edge_b])
+    wide_a, wide_b = local(
+        widen_kernel, "widen", [wide, wide], [place, middle, edge_a, edge_b], [pltpu.VMEM((2, *wide), F32)]
+    )
     return lon_a, lon_b, wide_a, wide_b
 
 

time: 92.7 us -> 92.8 us (level)
  no operation moved by 1% of the time
where the time goes in v9:
time: 92.8 us; the launch traced here: 92.5 us
  starting transfers between devices  28.4 us (31%)
  Pallas kernels  23.4 us (25%)
  blocking collectives  18 us (19%)
  waiting for transfers between devices  15.8 us (17%)
  local copies, waits for them, and re-layouts  4.28 us (5%)
  other arithmetic  1.6 us (2%)
  between operations  0.96 us (1%)
    all_to_all x1, blocking collectives, on_device(): lax.all_to_all(jnp.broadcast_to(part, (32, *part.shape)), BLOCK, 0, 0, ti...  18 us
    pallas_call x6, Pallas kernels, local(): pl.pallas_call(kernel, in_specs=[pl.BlockSpec(memory_space=pltpu.SMEM)] +...  8.41 us
    all_to_all x1, waiting for transfers between devices, summed(): lax.all_to_all(parts.reshape(groups, -1, CHANNELS), axes, 0, 0, tiled=True)  7.25 us
    pallas_call x1, Pallas kernels, input_gradient(): pl.pallas_call(input_kernel, in_specs=[spec(pl.ANY), spec(pltpu.HBM)], ou...  6.68 us
    all_to_all x1, starting transfers between devices, summed(): lax.all_to_all(parts.reshape(groups, -1, CHANNELS), axes, 0, 0, tiled=True)  6.12 us
    ppermute x3, starting transfers between devices, on_device(): lax.ppermute(part, AXES, along_z(m)).astype(F32)  5.74 us
    ppermute x1, starting transfers between devices, haloes(): edge_b = lax.ppermute(edge_b, AXES, LON_B)  5.59 us
    pallas_call x1, Pallas kernels, stencil(): pl.pallas_call(stencil_kernel, grid_spec=pltpu.PrefetchScalarGridSpec(num...  5.43 us
  transfers between devices with their start and end apart: 12, of which 6 were waited for; matrix products, arithmetic and copies ran while one was open for 0% of the time, Pallas kernels for 17%

profile of v9, /device:TPU:1, one launch (start us, length us, event | category | flops | bytes accessed | tf_op | source)
XLA Modules:
  0.0 92.5 jit_solution(16976751817382717731)
XLA Ops:
  0.6 0.1 pad_add_fusion.place
  0.7 0.0 copy-start.2
  0.7 1.4 %copy-done.2 = bf16[16,90,512]{2,0,1:T(8,128)(2,1)S(1)} copy-done((bf16[16,90,512]{2,0,1:T(8,128)(2,1)S(1)}, bf16[16,90,512]{2,0,1:T(8,128)(2,1)}, u32[]{:S(2)}) %copy-start.2) | copy-done | bytes 1474584
  2.1 0.8 edges.1
  2.9 2.6 %collective-permute-start = (bf16[2,16,512]{2,1,0:T(8,128)(2,1)S(1)}, bf16[2,16,512]{2,1,0:T(8,128)(2,1)S(1)}, u32[]{:S(2)}, u32[]{:S(2)}) collective-permute-start(bf16[2,16,512]{2,1,0:T(8,128)(2,1)S(1)} %get-tuple-element.18), channel_id=1, source_target_pairs={{0,1},{1,0},{2,3},{3,2},{4,5},{5,4},{6,7},{7,6},{8,9},{9,8},{10,11... | collective-permute-start | bytes 98312 | tf_op jit(solution)/shard_map/ppermute | solution.py:369
  5.5 5.6 %collective-permute-start.1 = (bf16[2,16,512]{2,1,0:T(8,128)(2,1)S(1)}, bf16[2,16,512]{2,1,0:T(8,128)(2,1)S(1)}, u32[]{:S(2)}, u32[]{:S(2)}) collective-permute-start(bf16[2,16,512]{2,1,0:T(8,128)(2,1)S(1)} %get-tuple-element.17._), channel_id=1, source_target_pairs={{0,15},{1,2},{2,1},{3,4},{4,3},{5,6},{6,5},{7,8},{8,7},{9,10},{10,... | collective-permute-start | bytes 98312 | tf_op jit(solution)/shard_map/ppermute | solution.py:370
  11.1 0.0 collective-permute-start.2
  11.1 0.0 collective-permute-start.3
  11.1 0.0 copy-start.3
  11.1 0.0 copy-start.4
  11.1 0.0 copy-start.5
  11.1 0.6 ordered.1.middle
  11.7 0.0 collective-permute-done.got_a
  11.7 0.7 collective-permute-done.1.got_b
  12.4 0.6 widen.1
  13.0 4.2 %collective-permute-start.5 = (bf16[128,512]{1,0:T(8,128)(2,1)S(1)}, bf16[128,512]{1,0:T(8,128)(2,1)S(1)}, u32[]{:S(2)}, u32[]{:S(2)}) collective-permute-start(bf16[128,512]{1,0:T(8,128)(2,1)S(1)} %get-tuple-element.24), channel_id=1, source_target_pairs={{0,8},{1,9},{2,10},{3,11},{4,12},{5,13},{6,14},{7,15},{8,0},{9,1},... | collective-permute-start | bytes 393224 | tf_op jit(solution)/shard_map/ppermute | solution.py:407
  17.2 0.0 collective-permute-start.4
  17.2 0.0 copy-done.3
  17.2 0.0 copy-done.4
  17.2 0.0 copy-done.5
  17.2 3.3 %prepare.1 = (bf16[8,256,256]{2,1,0:T(8,128)(2,1)S(1)}, bf16[16,96,512]{2,1,0:T(8,128)(2,1)S(1)}, bf16[16,96,512]{2,1,0:T(8,128)(2,1)S(1)}) custom-call(s32[3]{0:T(128)S(1)} %pad_add_fusion.place, bf16[3,33,4,256]{3,2,1,0:T(4,128)(2,1)S(1)} %bitcast.14, s32[1,256]{1,0:T(1,128)S(1)} %bitcast.15, bf16[90,16,512]{2,1,0:T(8,128)(2,1)} %bitcast.16, ...), custom_call_target="tpu_custom_call" | custom-call | flops 1000000000 | bytes 2000000 | tf_op jit(solution)/shard_map/prepare/pallas_call | solution.py:30
  20.6 4.9 %collective-permute-done.5.lat_b = bf16[128,512]{1,0:T(8,128)(2,1)S(1)} collective-permute-done((bf16[128,512]{1,0:T(8,128)(2,1)S(1)}, bf16[128,512]{1,0:T(8,128)(2,1)S(1)}, u32[]{:S(2)}, u32[]{:S(2)}) %collective-permute-start.5) | collective-permute-done | bytes 131104 | tf_op jit(solution)/shard_map/ppermute | solution.py:407
  25.5 0.0 collective-permute-done.4.lat_a
  25.5 0.0 collective-permute-done.2.lon_b
  25.5 0.0 collective-permute-done.3.lon_a
  25.5 5.4 %stencil.1 = (bf16[4,16,96,512]{3,2,1,0:T(8,128)(2,1)S(1)}, bf16[2,512,512]{2,1,0:T(8,128)(2,1)S(1)}) custom-call(s32[3]{0:T(128)S(1)} %pad_add_fusion.place, bf16[8,256,256]{2,1,0:T(8,128)(2,1)S(1)} %get-tuple-element.20.tiles, bf16[16,96,512]{2,1,0:T(8,128)(2,1)S(1)} %get-tuple-element.21.rows, bf16[16,16,512]{2,1,0:T(8,128)(2,1)S(1)} %collective-permute-done.2.lon_b, ...), custom_call_target="tpu_custom_call" | custom-call | tf_op jit(solution)/shard_map/stencil/pallas_call | solution.py:194
  30.9 0.0 copy-start
  30.9 0.1 collective-permute-start.6
  31.0 2.9 %own_part.1 = f32[2,512,512]{2,1,0:T(8,128)S(1)} custom-call(s32[3]{0:T(128)S(1)} %pad_add_fusion.place, bf16[4,16,96,512]{3,2,1,0:T(8,128)(2,1)S(1)} %get-tuple-element.26.f_hbm, bf16[16,96,512]{2,1,0:T(8,128)(2,1)S(1)} %get-tuple-element.25.cells_ref), custom_call_target="tpu_custom_call" | custom-call | flops 1610612736 | bytes 6000000 | tf_op jit(solution)/shard_map/own_part/pallas_call | solution.py:242
  33.9 0.0 copy-done
  33.9 0.0 collective-permute-done.6
  34.0 1.3 %add_convert_fusion = bf16[2,512,512]{2,1,0:T(8,128)(2,1)} fusion(f32[2,512,512]{2,1,0:T(8,128)S(1)} %own_part.1, bf16[2,512,512]{2,1,0:T(8,128)(2,1)S(1)} %collective-permute-done.6), kind=kLoop, calls=%fused_computation | loop fusion | flops 1572864 | bytes 4194304 | tf_op jit(solution)/shard_map/convert_element_type | solution.py:412
  35.3 6.1 %all-to-all-start = ((bf16[32,32,512]{2,1,0:T(8,128)(2,1)}), bf16[32,32,512]{2,1,0:T(8,128)(2,1)S(1)}, u32[]{:S(2)}, u32[]{:S(2)}) async-start(bf16[32,32,512]{2,1,0:T(8,128)(2,1)} %bitcast.7), calls=%async_computation | async-start | bytes 2097152 | tf_op jit(solution)/shard_map/all_to_all | solution.py:394
  41.4 0.0 copy-start.1
  41.4 2.8 %copy-done.1 = bf16[4,16,96,512]{3,2,1,0:T(8,128)(2,1)S(1)} copy-done((bf16[4,16,96,512]{3,2,1,0:T(8,128)(2,1)S(1)}, bf16[4,16,96,512]{3,2,1,0:T(8,128)(2,1)}, u32[]{:S(2)}) %copy-start.1) | copy-done | bytes 6291480
  44.2 6.7 %input_gradient.1 = bf16[90,16,512]{2,1,0:T(8,128)(2,1)} custom-call(bf16[4,16,96,512]{3,2,1,0:T(8,128)(2,1)S(1)} %copy-done.1, bf16[4,512,512]{2,1,0:T(8,128)(2,1)} %weight_hbm.1), custom_call_target="tpu_custom_call" | custom-call | flops 3221225472 | bytes 10000000 | tf_op jit(solution)/shard_map/input_gradient/pallas_call | solution.py:297
  50.9 7.2 %all-to-all-done = bf16[32,32,512]{2,1,0:T(8,128)(2,1)S(1)} async-done(((bf16[32,32,512]{2,1,0:T(8,128)(2,1)}), bf16[32,32,512]{2,1,0:T(8,128)(2,1)S(1)}, u32[]{:S(2)}, u32[]{:S(2)}) %all-to-all-start) | async-done | bytes 1048608 | tf_op jit(solution)/shard_map/all_to_all | solution.py:394
  58.1 0.2 reduce_sum.12
  58.3 0.8 collective-permute-start.9
  59.1 0.9 collective-permute-start.8
  60.0 4.1 %collective-permute-start.7 = (bf16[32,512]{1,0:T(8,128)(2,1)S(1)}, bf16[32,512]{1,0:T(8,128)(2,1)S(1)}, u32[]{:S(2)}, u32[]{:S(2)}) collective-permute-start(bf16[32,512]{1,0:T(8,128)(2,1)S(1)} %reduce_sum.12), channel_id=1, source_target_pairs={{0,2},{1,3},{2,0},{3,1},{4,6},{5,7},{6,4},{7,5},{8,10},{9,11},{10,... | collective-permute-start | bytes 98312 | tf_op jit(solution)/shard_map/ppermute | solution.py:417
  64.0 1.0 %collective-permute-done.9 = bf16[32,512]{1,0:T(8,128)(2,1)S(1)} collective-permute-done((bf16[32,512]{1,0:T(8,128)(2,1)S(1)}, bf16[32,512]{1,0:T(8,128)(2,1)S(1)}, u32[]{:S(2)}, u32[]{:S(2)}) %collective-permute-start.9) | collective-permute-done | bytes 32800 | tf_op jit(solution)/shard_map/ppermute | solution.py:417
  65.1 0.0 collective-permute-done.8
  65.1 1.3 %collective-permute-done.7 = bf16[32,512]{1,0:T(8,128)(2,1)S(1)} collective-permute-done((bf16[32,512]{1,0:T(8,128)(2,1)S(1)}, bf16[32,512]{1,0:T(8,128)(2,1)S(1)}, u32[]{:S(2)}, u32[]{:S(2)}) %collective-permute-start.7) | collective-permute-done | bytes 32800 | tf_op jit(solution)/shard_map/ppermute | solution.py:417
  66.4 0.1 broadcast_in_dim.3
  66.5 18.0 %all_to_all.10 = bf16[32,32,512]{2,1,0:T(8,128)(2,1)S(1)} all-to-all(bf16[32,32,512]{2,1,0:T(8,128)(2,1)S(1)} %broadcast_in_dim.3), channel_id=1, replica_groups=mesh['y'=4,'xh'=2,'core'=2,'xl'=2,'zh'=4,'zl'=2] {'y','xh','xl','zl'}, dimensions={0} | all-to-all | bytes 2097152 | tf_op jit(solution)/shard_map/all_to_all | solution.py:421
  84.5 4.0 %collective-permute-start.10 = (bf16[2,512,512]{2,1,0:T(8,128)(2,1)S(1)}, bf16[2,512,512]{2,1,0:T(8,128)(2,1)S(1)}, u32[]{:S(2)}, u32[]{:S(2)}) collective-permute-start(bf16[2,512,512]{2,1,0:T(8,128)(2,1)S(1)} %bitcast.10), channel_id=1, source_target_pairs={{0,16},{1,17},{2,18},{3,19},{4,20},{5,21},{6,22},{7,23},{8,24},{9,... | collective-permute-start | bytes 3145736 | tf_op jit(solution)/shard_map/ppermute | solution.py:423
  88.5 1.5 %put_half.2.rest_0_ = bf16[4,512,512]{2,1,0:T(8,128)(2,1)} custom-call(s32[3]{0:T(128)S(1)} %pad_add_fusion.place, bf16[2,512,512]{2,1,0:T(8,128)(2,1)S(1)} %bitcast.11), custom_call_target="tpu_custom_call" | custom-call | tf_op jit(solution)/shard_map/put_half/pallas_call | solution.py:30
  90.1 0.7 collective-permute-done.10.half
  90.8 1.5 %put_half.3 = bf16[4,512,512]{2,1,0:T(8,128)(2,1)} custom-call(s32[3]{0:T(128)S(1)} %pad_add_fusion.place, bf16[2,512,512]{2,1,0:T(8,128)(2,1)S(1)} %collective-permute-done.10.half, bf16[4,512,512]{2,1,0:T(8,128)(2,1)} %put_half.2.rest_0_), custom_call_target="tpu_custom_call", output_to_operand_aliasing={{}: (2, {})} | custom-call | tf_op jit(solution)/shard_map/put_half/pallas_call | solution.py:30
  (1 shorter events, 0.0 us)
Async XLA Ops:
  0.7 1.4 %copy-start.2 = (bf16[16,90,512]{2,0,1:T(8,128)(2,1)S(1)}, bf16[16,90,512]{2,0,1:T(8,128)(2,1)}, u32[]{:S(2)}) copy-start(bf16[16,90,512]{2,0,1:T(8,128)(2,1)} %param.5) | copy-start | bytes 4423684
  2.9 8.8 %collective-permute-start = (bf16[2,16,512]{2,1,0:T(8,128)(2,1)S(1)}, bf16[2,16,512]{2,1,0:T(8,128)(2,1)S(1)}, u32[]{:S(2)}, u32[]{:S(2)}) collective-permute-start(bf16[2,16,512]{2,1,0:T(8,128)(2,1)S(1)} %get-tuple-element.18), channel_id=1, source_target_pairs={{0,1},{1,0},{2,3},{3,2},{4,5},{5,4},{6,7},{7,6},{8,9},{9,8},{10,11... | collective-permute-start | bytes 98312 | tf_op jit(solution)/shard_map/ppermute | solution.py:369
  5.5 6.9 %collective-permute-start.1 = (bf16[2,16,512]{2,1,0:T(8,128)(2,1)S(1)}, bf16[2,16,512]{2,1,0:T(8,128)(2,1)S(1)}, u32[]{:S(2)}, u32[]{:S(2)}) collective-permute-start(bf16[2,16,512]{2,1,0:T(8,128)(2,1)S(1)} %get-tuple-element.17._), channel_id=1, source_target_pairs={{0,15},{1,2},{2,1},{3,4},{4,3},{5,6},{6,5},{7,8},{8,7},{9,10},{10,... | collective-permute-start | bytes 98312 | tf_op jit(solution)/shard_map/ppermute | solution.py:370
  11.1 14.4 %collective-permute-start.2 = (bf16[16,16,512]{2,1,0:T(8,128)(2,1)S(1)}, bf16[16,16,512]{2,1,0:T(8,128)(2,1)S(1)}, u32[]{:S(2)}, u32[]{:S(2)}) collective-permute-start(bf16[16,16,512]{2,1,0:T(8,128)(2,1)S(1)} %get-tuple-element.22), channel_id=1, source_target_pairs={{0,15},{1,2},{2,1},{3,4},{4,3},{5,6},{6,5},{7,8},{8,7},{9,10},{10,... | collective-permute-start | bytes 786440 | tf_op jit(solution)/shard_map/ppermute | solution.py:372
  11.1 14.4 %collective-permute-start.3 = (bf16[16,16,512]{2,1,0:T(8,128)(2,1)S(1)}, bf16[16,16,512]{2,1,0:T(8,128)(2,1)S(1)}, u32[]{:S(2)}, u32[]{:S(2)}) collective-permute-start(bf16[16,16,512]{2,1,0:T(8,128)(2,1)S(1)} %get-tuple-element.23), channel_id=1, source_target_pairs={{0,1},{1,0},{2,3},{3,2},{4,5},{5,4},{6,7},{7,6},{8,9},{9,8},{10,11... | collective-permute-start | bytes 786440 | tf_op jit(solution)/shard_map/ppermute | solution.py:371
  11.1 6.1 %copy-start.3 = (bf16[16,90,512]{2,0,1:T(8,128)(2,1)S(1)}, bf16[16,90,512]{2,0,1:T(8,128)(2,1)}, u32[]{:S(2)}) copy-start(bf16[16,90,512]{2,0,1:T(8,128)(2,1)} %param.5) | copy-start | bytes 4423684
  11.1 6.1 %copy-start.4 = (bf16[4,3,33,256]{3,0,2,1:T(4,128)(2,1)S(1)}, bf16[4,3,33,256]{3,0,2,1:T(4,128)(2,1)}, u32[]{:S(2)}) copy-start(bf16[4,3,33,256]{3,0,2,1:T(4,128)(2,1)} %param.8) | copy-start | bytes 608260
  11.1 6.1 %copy-start.5 = (s32[256]{0:T(256)S(1)}, s32[256]{0:T(256)}, u32[]{:S(2)}) copy-start(s32[256]{0:T(256)} %param.9) | copy-start | bytes 3076
  13.0 12.5 %collective-permute-start.5 = (bf16[128,512]{1,0:T(8,128)(2,1)S(1)}, bf16[128,512]{1,0:T(8,128)(2,1)S(1)}, u32[]{:S(2)}, u32[]{:S(2)}) collective-permute-start(bf16[128,512]{1,0:T(8,128)(2,1)S(1)} %get-tuple-element.24), channel_id=1, source_target_pairs={{0,8},{1,9},{2,10},{3,11},{4,12},{5,13},{6,14},{7,15},{8,0},{9,1},... | collective-permute-start | bytes 393224 | tf_op jit(solution)/shard_map/ppermute | solution.py:407
  17.2 8.3 %collective-permute-start.4 = (bf16[128,512]{1,0:T(8,128)(2,1)S(1)}, bf16[128,512]{1,0:T(8,128)(2,1)S(1)}, u32[]{:S(2)}, u32[]{:S(2)}) collective-permute-start(bf16[128,512]{1,0:T(8,128)(2,1)S(1)} %get-tuple-element.19._), channel_id=1, source_target_pairs={{0,16},{1,17},{2,18},{3,19},{4,20},{5,21},{6,22},{7,23},{8,24},{9,... | collective-permute-start | bytes 393224 | tf_op jit(solution)/shard_map/ppermute | solution.py:406
  30.9 3.0 %copy-start = (bf16[4,16,96,512]{3,2,1,0:T(8,128)(2,1)}, bf16[4,16,96,512]{3,2,1,0:T(8,128)(2,1)S(1)}, u32[]{:S(2)}) copy-start(bf16[4,16,96,512]{3,2,1,0:T(8,128)(2,1)S(1)} %get-tuple-element.26.f_hbm) | copy-start | bytes 18874372
  30.9 3.0 %collective-permute-start.6 = (bf16[2,512,512]{2,1,0:T(8,128)(2,1)S(1)}, bf16[2,512,512]{2,1,0:T(8,128)(2,1)S(1)}, u32[]{:S(2)}, u32[]{:S(2)}) collective-permute-start(bf16[2,512,512]{2,1,0:T(8,128)(2,1)S(1)} %get-tuple-element.27), channel_id=1, source_target_pairs={{0,16},{1,17},{2,18},{3,19},{4,20},{5,21},{6,22},{7,23},{8,24},{9,... | collective-permute-start | bytes 3145736 | tf_op jit(solution)/shard_map/ppermute | solution.py:410
  35.3 22.8 %all-to-all-start = ((bf16[32,32,512]{2,1,0:T(8,128)(2,1)}), bf16[32,32,512]{2,1,0:T(8,128)(2,1)S(1)}, u32[]{:S(2)}, u32[]{:S(2)}) async-start(bf16[32,32,512]{2,1,0:T(8,128)(2,1)} %bitcast.7), calls=%async_computation | async-start | bytes 2097152 | tf_op jit(solution)/shard_map/all_to_all | solution.py:394
  41.4 2.8 %copy-start.1 = (bf16[4,16,96,512]{3,2,1,0:T(8,128)(2,1)S(1)}, bf16[4,16,96,512]{3,2,1,0:T(8,128)(2,1)}, u32[]{:S(2)}) copy-start(bf16[4,16,96,512]{3,2,1,0:T(8,128)(2,1)} %copy-done) | copy-start | bytes 18874372
  58.3 6.8 %collective-permute-start.9 = (bf16[32,512]{1,0:T(8,128)(2,1)S(1)}, bf16[32,512]{1,0:T(8,128)(2,1)S(1)}, u32[]{:S(2)}, u32[]{:S(2)}) collective-permute-start(bf16[32,512]{1,0:T(8,128)(2,1)S(1)} %reduce_sum.12), channel_id=1, source_target_pairs={{0,4},{1,5},{2,6},{3,7},{4,0},{5,1},{6,2},{7,3},{8,12},{9,13},{10,... | collective-permute-start | bytes 98312 | tf_op jit(solution)/shard_map/ppermute | solution.py:417
  59.1 6.0 %collective-permute-start.8 = (bf16[32,512]{1,0:T(8,128)(2,1)S(1)}, bf16[32,512]{1,0:T(8,128)(2,1)S(1)}, u32[]{:S(2)}, u32[]{:S(2)}) collective-permute-start(bf16[32,512]{1,0:T(8,128)(2,1)S(1)} %reduce_sum.12), channel_id=1, source_target_pairs={{0,6},{1,7},{2,4},{3,5},{4,2},{5,3},{6,0},{7,1},{8,14},{9,15},{10,... | collective-permute-start | bytes 98312 | tf_op jit(solution)/shard_map/ppermute | solution.py:417
  60.0 6.4 %collective-permute-start.7 = (bf16[32,512]{1,0:T(8,128)(2,1)S(1)}, bf16[32,512]{1,0:T(8,128)(2,1)S(1)}, u32[]{:S(2)}, u32[]{:S(2)}) collective-permute-start(bf16[32,512]{1,0:T(8,128)(2,1)S(1)} %reduce_sum.12), channel_id=1, source_target_pairs={{0,2},{1,3},{2,0},{3,1},{4,6},{5,7},{6,4},{7,5},{8,10},{9,11},{10,... | collective-permute-start | bytes 98312 | tf_op jit(solution)/shard_map/ppermute | solution.py:417
  84.5 6.3 %collective-permute-start.10 = (bf16[2,512,512]{2,1,0:T(8,128)(2,1)S(1)}, bf16[2,512,512]{2,1,0:T(8,128)(2,1)S(1)}, u32[]{:S(2)}, u32[]{:S(2)}) collective-permute-start(bf16[2,512,512]{2,1,0:T(8,128)(2,1)S(1)} %bitcast.10), channel_id=1, source_target_pairs={{0,16},{1,17},{2,18},{3,19},{4,20},{5,21},{6,22},{7,23},{8,24},{9,... | collective-permute-start | bytes 3145736 | tf_op jit(solution)/shard_map/ppermute | solution.py:423
